TPU v7x, 32 devices: a whole 2x2x4 slice. The times are simulated.
32 devices in a mesh: dp: 2 (over core), context: 4 (over y, x), tensor: 4 (over z).
Axes of the slice: x: 2, y: 2, z: 4, core: 2. Of those that a mesh axis runs over, the one named last changes fastest.
Arguments:
- hidden_input: bfloat16 [2, 2, 1024, 2048], P(None, 'dp', ('context', 'tensor')), may hold values from -27 to 27
- cotangent: bfloat16 [2, 2, 1024, 2048], P(None, 'dp', ('context', 'tensor')), may hold values from -6 to 6
- window_before: bfloat16 [2048], P(('dp', 'context', 'tensor')), may hold values from 0.5 to 1.5
- window_query: bfloat16 [2048, 2048], P(('dp', 'context'), 'tensor'), may hold values from -0.125 to 0.125
- window_keys: bfloat16 [2048, 256], P(('dp', 'context', 'tensor')), may hold values from -0.125 to 0.125
- window_values: bfloat16 [2048, 256], P(('dp', 'context', 'tensor')), may hold values from -0.125 to 0.125
- window_output: bfloat16 [2048, 2048], P(('dp', 'context'), 'tensor'), may hold values from -1.5 to 1.5
- window_middle: bfloat16 [2048], P(('dp', 'context', 'tensor')), may hold values from 0.5 to 1.5
- window_gate: bfloat16 [2048, 5632], P(('dp', 'context'), 'tensor'), may hold values from -0.125 to 0.125
- window_up: bfloat16 [2048, 5632], P(('dp', 'context'), 'tensor'), may hold values from -0.125 to 0.125
- window_down: bfloat16 [2048, 5632], P(('dp', 'context'), 'tensor'), may hold values from -0.078125 to 0.078125
- causal_before: bfloat16 [2048], P(('dp', 'context', 'tensor')), may hold values from 0.5 to 1.5
- causal_query: bfloat16 [2048, 2048], P(('dp', 'context'), 'tensor'), may hold values from -0.125 to 0.125
- causal_keys: bfloat16 [2048, 256], P(('dp', 'context', 'tensor')), may hold values from -0.125 to 0.125
- causal_values: bfloat16 [2048, 256], P(('dp', 'context', 'tensor')), may hold values from -0.125 to 0.125
- causal_output: bfloat16 [2048, 2048], P(('dp', 'context'), 'tensor'), may hold values from -1.5 to 1.5
- causal_middle: bfloat16 [2048], P(('dp', 'context', 'tensor')), may hold values from 0.5 to 1.5
- causal_gate: bfloat16 [2048, 5632], P(('dp', 'context'), 'tensor'), may hold values from -0.125 to 0.125
- causal_up: bfloat16 [2048, 5632], P(('dp', 'context'), 'tensor'), may hold values from -0.125 to 0.125
- causal_down: bfloat16 [2048, 5632], P(('dp', 'context'), 'tensor'), may hold values from -0.078125 to 0.078125
Outputs:
- hidden_output: bfloat16 [2, 2, 1024, 2048], P(None, 'dp', ('context', 'tensor'))
- input_grad: float32 [2, 2, 1024, 2048], P(None, 'dp', ('context', 'tensor'))
- grad_window_before: float32 [2048], P(('dp', 'context', 'tensor'))
- grad_window_query: float32 [2048, 2048], P(('dp', 'context'), 'tensor')
- grad_window_keys: float32 [2048, 256], P(('dp', 'context', 'tensor'))
- grad_window_values: float32 [2048, 256], P(('dp', 'context', 'tensor'))
- grad_window_output: float32 [2048, 2048], P(('dp', 'context'), 'tensor')
- grad_window_middle: float32 [2048], P(('dp', 'context', 'tensor'))
- grad_window_gate: float32 [2048, 5632], P(('dp', 'context'), 'tensor')
- grad_window_up: float32 [2048, 5632], P(('dp', 'context'), 'tensor')
- grad_window_down: float32 [2048, 5632], P(('dp', 'context'), 'tensor')
- grad_causal_before: float32 [2048], P(('dp', 'context', 'tensor'))
- grad_causal_query: float32 [2048, 2048], P(('dp', 'context'), 'tensor')
- grad_causal_keys: float32 [2048, 256], P(('dp', 'context', 'tensor'))
- grad_causal_values: float32 [2048, 256], P(('dp', 'context', 'tensor'))
- grad_causal_output: float32 [2048, 2048], P(('dp', 'context'), 'tensor')
- grad_causal_middle: float32 [2048], P(('dp', 'context', 'tensor'))
- grad_causal_gate: float32 [2048, 5632], P(('dp', 'context'), 'tensor')
- grad_causal_up: float32 [2048, 5632], P(('dp', 'context'), 'tensor')
- grad_causal_down: float32 [2048, 5632], P(('dp', 'context'), 'tensor')
All inputs are finite; a program needn't handle non-finite values.
Results may differ from a plain program's by a relative error of at most 0.033.
Values may be sent and summed in bfloat16 or wider, within the bound.
No kernel may reach another device: no remote copies, remote signals or barrier semaphores. Data moves between devices by JAX's collectives and lax.ppermute only.
A program may use at most 320 MiB of HBM per device.

v0:
```python
import jax
import jax.numpy as jnp
from jax import lax
from jax.sharding import PartitionSpec as P

H = 32
KV = 4
HD = 64
WINDOW = 512
EPSILON = 1e-05
THETA = 10000.0
NEGATIVE = -1e30
BF = jnp.bfloat16
F32 = jnp.float32


def swap(value, axis, bits):
    count = lax.axis_size(axis)
    return lax.ppermute(value, axis, [(source, source ^ bits) for source in range(count)])


def row_index():
    return lax.axis_index("dp") * lax.axis_size("context") + lax.axis_index("context")


def relative(values):
    index = row_index()
    count = lax.axis_size("dp") * lax.axis_size("context")
    block = values.shape[-1] // count
    lead = values.shape[:-1]
    bit = 1
    while bit < count:
        paired = values.reshape(*lead, count // (2 * bit), 2, bit * block)
        other = jnp.flip(paired, axis=-2).reshape(values.shape)
        values = jnp.where((index & bit) != 0, other, values)
        bit *= 2
    return values


def gather_rows(piece):
    count = lax.axis_size("context")
    if count != 4:
        parts, bit = [piece], 1
        while bit < count:
            parts = parts + [swap(part, "context", bit) for part in parts]
            bit *= 2
        return jnp.concatenate(parts + [swap(part, "dp", 1) for part in parts], axis=0)
    half = piece.shape[0] // 2
    by_x = swap(piece, "context", 1)
    by_y = swap(piece, "context", 2)
    far_low = swap(by_y[:half], "context", 1)
    far_high = swap(by_x[half:], "context", 2)
    parts = [piece, by_x, by_y, far_low, far_high]
    others = [swap(part, "dp", 1) for part in parts]
    return jnp.concatenate(parts + others, axis=0)


def scatter_rows(keep, send):
    both = keep.astype(F32) + swap(send, "dp", 1).astype(F32)
    count = lax.axis_size("context")
    if count != 4:
        bit = count // 2
        while bit:
            middle = both.shape[0] // 2
            both = both[:middle] + swap(both[middle:].astype(BF), "context", bit).astype(F32)
            bit //= 2
        return both
    quarter = both.shape[0] // 4
    half = quarter // 2
    blocks = [both[i * quarter : (i + 1) * quarter] for i in range(4)]
    low = [block[:half] for block in blocks]
    high = [block[half:] for block in blocks]
    low_send = jnp.concatenate([low[1], low[3]], axis=0).astype(BF)
    high_send = jnp.concatenate([high[2], high[3]], axis=0).astype(BF)
    low_got = swap(low_send, "context", 1).astype(F32)
    high_got = swap(high_send, "context", 2).astype(F32)
    low_own = low[0] + low_got[:half]
    low_next = (low[2] + low_got[half:]).astype(BF)
    high_own = high[0] + high_got[:half]
    high_next = (high[1] + high_got[half:]).astype(BF)
    low_own = low_own + swap(low_next, "context", 2).astype(F32)
    high_own = high_own + swap(high_next, "context", 1).astype(F32)
    return jnp.concatenate([low_own, high_own], axis=0)


def gather_tokens(piece):
    return lax.all_gather(piece, "tensor", axis=0, tiled=True)


def scatter_tokens(term):
    count = lax.axis_size("tensor")
    me = lax.axis_index("tensor")
    rows = term.shape[0] // count
    chunks = term.astype(BF).reshape(count, rows, term.shape[1])
    pick = lambda k: lax.dynamic_index_in_dim(chunks, me ^ k, 0, keepdims=False)
    total = pick(0).astype(F32)
    for k in range(1, count):
        total = total + swap(pick(k), "tensor", k).astype(F32)
    return total


def gather_blocks(pair):
    parts = [pair] + [swap(pair, "context", r) for r in range(1, lax.axis_size("context"))]
    return jnp.concatenate(parts, axis=0)


def scatter_blocks(both):
    count = lax.axis_size("context")
    rows = both.shape[0] // count
    total = both[:rows]
    for r in range(1, count):
        total = total + swap(both[r * rows : (r + 1) * rows].astype(BF), "context", r).astype(F32)
    return total


def dot(left, right, left_dim, right_dim):
    return lax.dot_general(
        left, right, (((left_dim,), (right_dim,)), ((), ())), preferred_element_type=F32
    )


def rotate(values, cosine, sine):
    half = values.shape[-1] // 2
    first, second = values[..., :half], values[..., half:]
    return jnp.concatenate(
        [first * cosine - second * sine, second * cosine + first * sine], axis=-1
    )


def normalize(values, gain):
    scale = lax.rsqrt(jnp.mean(values * values, axis=-1, keepdims=True) + EPSILON)
    return (values * scale * gain).astype(BF)


def norm_back(incoming, values, gain):
    scale = lax.rsqrt(jnp.mean(values * values, axis=-1, keepdims=True) + EPSILON)
    weighted = incoming * gain
    unit = values * scale
    return scale * (weighted - unit * jnp.mean(weighted * unit, axis=-1, keepdims=True))


def project(first_in, qkv_w, cosine, sine):
    heads = (qkv_w.shape[1] - 2 * HD) // HD
    pre = dot(first_in, qkv_w, 1, 0)
    turned = rotate(
        pre[:, : (heads + 1) * HD].reshape(pre.shape[0], heads + 1, HD),
        cosine[:, None],
        sine[:, None],
    )
    query = turned[:, :heads].astype(BF)
    pair = jnp.concatenate([turned[:, heads], pre[:, (heads + 1) * HD :]], axis=1).astype(BF)
    return query, pair


def scores_of(query, keys, allowed):
    raw = jnp.einsum("qhd,kd->hqk", query, keys, preferred_element_type=F32) * HD ** (-0.5)
    return jnp.where(allowed[None], raw, NEGATIVE)


def attend(query, block, allowed):
    scores = scores_of(query, block[:, :HD], allowed)
    row_max = jnp.max(scores, axis=-1, keepdims=True)
    expo = jnp.exp(scores - row_max)
    total = jnp.sum(expo, axis=-1, keepdims=True)
    probs_low = (expo / total).astype(BF)
    mixed = jnp.einsum("hqk,kd->qhd", probs_low, block[:, HD:], preferred_element_type=F32)
    return mixed.astype(BF).reshape(query.shape[0], -1), (row_max, total)


def attend_back(grad_mixed, query, block, allowed, stats):
    row_max, total = stats
    scale = HD ** (-0.5)
    grad_mixed = grad_mixed.reshape(query.shape)
    probs = jnp.exp(scores_of(query, block[:, :HD], allowed) - row_max) / total
    probs_low = probs.astype(BF)
    grad_probs = jnp.einsum("qhd,kd->hqk", grad_mixed, block[:, HD:], preferred_element_type=F32)
    inner = jnp.sum(probs * grad_probs, axis=-1, keepdims=True)
    grad_scores = (probs * (grad_probs - inner)).astype(BF)
    key_part = jnp.einsum("hqk,qhd->kd", grad_scores, query, preferred_element_type=F32) * scale
    value_part = jnp.einsum("hqk,qhd->kd", probs_low, grad_mixed, preferred_element_type=F32)
    query_part = (
        jnp.einsum("hqk,kd->qhd", grad_scores, block[:, :HD], preferred_element_type=F32) * scale
    )
    return query_part, jnp.concatenate([key_part, value_part], axis=1)


def feed(second_in, gate_up_w):
    units = gate_up_w.shape[1] // 2
    both = dot(second_in, gate_up_w, 1, 0)
    gate, up = both[:, :units], both[:, units:]
    hidden = (jax.nn.silu(gate) * up).astype(BF)
    return hidden, both


def feed_back(grad_hidden, both):
    units = both.shape[1] // 2
    gate, up = both[:, :units], both[:, units:]
    sigma = jax.nn.sigmoid(gate)
    grad_gate = grad_hidden * up * sigma * (1.0 + gate * (1.0 - sigma))
    grad_up = grad_hidden * gate * sigma
    return jnp.concatenate([grad_gate, grad_up], axis=1).astype(BF)


def weight_grad(lefts, rights):
    left = jnp.concatenate(lefts, axis=0)
    right = jnp.concatenate(rights, axis=0)
    half = left.shape[1] // 2
    keep = dot(left[:, :half], right, 0, 0).astype(BF)
    send = dot(left[:, half:], right, 0, 0).astype(BF)
    return scatter_rows(keep, send)


def per_device(hidden_input, cotangent, *params):
    layers = (params[:9], params[9:])
    tensor_count = lax.axis_size("tensor")
    rows = hidden_input.shape[2]
    block_len = rows * tensor_count
    head_count = params[1].shape[1] // HD
    heads_of = [j * head_count // (H // KV) for j in range(tensor_count)]
    context = lax.axis_index("context")
    positions = context * block_len + jnp.arange(block_len, dtype=jnp.int32)
    key_pos = jnp.concatenate(
        [
            (context ^ r) * block_len + jnp.arange(block_len, dtype=jnp.int32)
            for r in range(lax.axis_size("context"))
        ]
    )
    causal = key_pos[None, :] <= positions[:, None]
    masks = (causal & (positions[:, None] - key_pos[None, :] < WINDOW), causal)
    freq = THETA ** (-2.0 * jnp.arange(HD // 2, dtype=F32) / HD)
    angle = positions.astype(F32)[:, None] * freq[None, :]
    cosine, sine = jnp.cos(angle), jnp.sin(angle)

    streams = range(hidden_input.shape[0])
    first_low = [relative(hidden_input[i, 0]) for i in streams]
    first_all = [gather_tokens(low) for low in first_low]

    small = []
    gains = jnp.stack([layers[0][0], layers[0][5], layers[1][0], layers[1][5]], axis=1)
    gains = jnp.pad(gains, ((0, 0), (0, 2 * HD - 4)))
    for head in heads_of:
        columns = []
        for layer in layers:
            columns += [layer[2][:, head * HD : (head + 1) * HD]]
            columns += [layer[3][:, head * HD : (head + 1) * HD]]
        small.append(jnp.concatenate(columns + [gains], axis=1))
    small = lax.all_to_all(
        jnp.concatenate(small, axis=0), "tensor", split_axis=0, concat_axis=0, tiled=True
    )
    pairs_w = (small[:, : 2 * HD], small[:, 2 * HD : 4 * HD])
    gain_rows = small[:, 4 * HD :]

    weights = []
    head_group = gather_rows(jnp.concatenate([layers[0][1], pairs_w[0], gain_rows], axis=1))
    width = head_group.shape[1]
    pick = jnp.eye(8, 2 * HD, dtype=BF)
    gain_all = dot(pick, head_group[:, width - 2 * HD :], 1, 1)
    for number, layer in enumerate(layers):
        if number == 0:
            qkv_w = head_group[:, : width - 2 * HD]
        else:
            qkv_w = gather_rows(jnp.concatenate([layer[1], pairs_w[1]], axis=1))
        weights.append(
            (
                gain_all[2 * number : 2 * number + 1],
                gain_all[2 * number + 1 : 2 * number + 2],
                qkv_w,
                gather_rows(layer[4]),
                gather_rows(jnp.concatenate([layer[6], layer[7]], axis=1)),
                gather_rows(layer[8]),
            )
        )

    saved = [[None, None] for _ in streams]
    state = [low.astype(F32) for low in first_low]
    for number in range(2):
        before, middle, qkv_w, output_w, gate_up_w, down_w = weights[number]
        for i in streams:
            stream = state[i]
            if number == 0:
                first_in = normalize(first_all[i].astype(F32), before)
            else:
                first_in = gather_tokens(normalize(stream, before))
            query, pair = project(first_in, qkv_w, cosine, sine)
            block = gather_blocks(pair)
            mixed, stats = attend(query, block, masks[number])
            middle_state = stream + scatter_tokens(dot(mixed, output_w, 1, 1))
            second_in = gather_tokens(normalize(middle_state, middle))
            hidden, both = feed(second_in, gate_up_w)
            state[i] = middle_state + scatter_tokens(dot(hidden, down_w, 1, 1))
            saved[i][number] = (
                stream, first_in, query, block, stats, mixed, middle_state, second_in, both, hidden
            )
    outputs = [relative(value.astype(BF)) for value in state]

    incoming = [relative(cotangent[i, 0]) for i in streams]
    large = [None, None]
    for number in (1, 0):
        before, middle, qkv_w, output_w, gate_up_w, down_w = weights[number]
        kept = []
        for i in streams:
            stream, first_in, query, block, stats, mixed, middle_state, second_in, both, hidden = (
                saved[i][number]
            )
            grad_low = gather_tokens(incoming[i].astype(BF))
            grad_both = feed_back(dot(grad_low, down_w, 1, 0), both)
            reduced_two = scatter_tokens(dot(grad_both, gate_up_w, 1, 1))
            grad_mid = incoming[i].astype(F32) + norm_back(reduced_two, middle_state, middle)
            mid_low = gather_tokens(grad_mid.astype(BF))
            grad_mixed = dot(mid_low, output_w, 1, 0).astype(BF)
            query_part, pair_part = attend_back(grad_mixed, query, block, masks[number], stats)
            pair_part = scatter_blocks(pair_part)
            grad_query = rotate(query_part, cosine[:, None], -sine[:, None]).reshape(block_len, -1)
            grad_key = rotate(pair_part[:, :HD], cosine, -sine)
            grad_qkv = jnp.concatenate(
                [grad_query, grad_key, pair_part[:, HD:]], axis=1
            ).astype(BF)
            reduced_one = scatter_tokens(dot(grad_qkv, qkv_w, 1, 1))
            incoming[i] = grad_mid + norm_back(reduced_one, stream, before)
            kept.append((first_in, grad_qkv, mid_low, mixed, second_in, grad_both, grad_low, hidden))
        kept = list(zip(*kept))
        large[number] = (
            weight_grad(kept[0], kept[1]),
            weight_grad(kept[2], kept[3]),
            weight_grad(kept[4], kept[5]),
            weight_grad(kept[6], kept[7]),
        )
    in_grads = [relative(value) for value in incoming]

    columns = []
    sums = []
    for number, layer in enumerate(layers):
        qkv_g, _, gate_up_g, _ = large[number]
        own_qkv = jnp.concatenate([layer[1], pairs_w[number]], axis=1).astype(F32)
        own_gate_up = jnp.concatenate([layer[6], layer[7]], axis=1).astype(F32)
        own_gains = gain_rows[:, 2 * number : 2 * number + 2].astype(F32)
        sums.append(jnp.sum(own_qkv * qkv_g, axis=1, keepdims=True) / own_gains[:, :1])
        sums.append(jnp.sum(own_gate_up * gate_up_g, axis=1, keepdims=True) / own_gains[:, 1:])
        columns.append(qkv_g[:, qkv_g.shape[1] - 2 * HD :])
    tail = jnp.pad(jnp.concatenate(sums, axis=1), ((0, 0), (0, 2 * HD - 4)))
    small_g = lax.all_to_all(
        jnp.concatenate(columns + [tail], axis=1), "tensor", split_axis=0, concat_axis=0, tiled=True
    ).reshape(tensor_count, -1, 6 * HD)
    gain_g = jnp.sum(small_g[:, :, 4 * HD : 4 * HD + 4], axis=0)

    results = [jnp.stack(outputs)[:, None], jnp.stack(in_grads)[:, None]]
    for number, layer in enumerate(layers):
        qkv_g, output_g, gate_up_g, down_g = large[number]
        units = layer[6].shape[1]
        pair_g = []
        for part in range(2):
            at = (2 * number + part) * HD
            heads = []
            for head in range(KV):
                pieces = [
                    small_g[j, :, at : at + HD] for j in range(tensor_count) if heads_of[j] == head
                ]
                heads.append(sum(pieces))
            pair_g.append(jnp.concatenate(heads, axis=1))
        results += [
            gain_g[:, 2 * number],
            qkv_g[:, : layer[1].shape[1]],
            pair_g[0],
            pair_g[1],
            output_g,
            gain_g[:, 2 * number + 1],
            gate_up_g[:, :units],
            gate_up_g[:, units:],
            down_g,
        ]
    return tuple(results)


def solution(mesh):
    rows = P(("dp", "context", "tensor"))
    tall = P(("dp", "context", "tensor"), None)
    wide = P(("dp", "context"), "tensor")
    tokens = P(None, "dp", ("context", "tensor"), None)
    layer = (rows, wide, tall, tall, wide, rows, wide, wide, wide)
    return jax.shard_map(
        per_device,
        mesh=mesh,
        in_specs=(tokens, tokens) + layer + layer,
        out_specs=(tokens, tokens) + layer + layer,
        check_vma=False,
    )
```

profile of v0, /device:TPU:0, one launch (start us, length us, event | category | flops | bytes accessed | tf_op | source)
XLA Modules:
  0.0 1558.2 jit_solution(2655771379367464531)
XLA Ops:
  73.8 13.8 all-gather.25.cloned.1.call-done
  126.4 7.0 collective-permute-done.23
  133.4 13.3 collective-permute-done.22
  149.7 13.0 all-gather.33.cloned.1.call-start
  246.6 9.9 collective-permute-done.34
  260.8 10.8 collective-permute-done.79
  276.6 16.1 %collective-permute-done.47 = bf16[128,640]{1,0:T(8,128)(2,1)S(1)} collective-permute-done((bf16[128,640]{1,0:T(8,128)(2,1)S(1)}, bf16[128,640]{1,0:T(8,128)(2,1)S(1)}, u32[]{:S(2)}, u32[]{:S(2)}) %collective-permute-start.47) | collective-permute-done | bytes 163872 | tf_op jit(solution)/shard_map/ppermute | solution.py:19
  315.9 29.1 %collective-permute-done.81 = bf16[128,1408]{1,0:T(8,128)(2,1)} collective-permute-done((bf16[128,1408]{1,0:T(8,128)(2,1)S(1)}, bf16[128,1408]{1,0:T(8,128)(2,1)}, u32[]{:S(2)}, u32[]{:S(2)}) %collective-permute-start.81) | collective-permute-done | bytes 360480 | tf_op jit(solution)/shard_map/ppermute | solution.py:19
  358.3 25.4 %collective-permute-done.69 = bf16[256,2816]{1,0:T(8,128)(2,1)} collective-permute-done((bf16[256,2816]{1,0:T(8,128)(2,1)}, bf16[256,2816]{1,0:T(8,128)(2,1)}, u32[]{:S(2)}, u32[]{:S(2)}) %collective-permute-start.69) | collective-permute-done | bytes 1441824 | tf_op jit(solution)/shard_map/ppermute | solution.py:19
  388.1 10.3 collective-permute-done.26
  435.2 10.3 collective-permute-done.43
  498.4 7.0 fusion.411
  522.0 13.4 collective-permute-done.94
  552.8 12.1 all-gather.27.cloned.1.call-done
  583.5 6.9 fusion.410
  590.6 14.4 collective-permute-done.97
  615.4 19.6 %all-gather.29.cloned.1.call-done = bf16[256,2048]{1,0:T(8,128)(2,1)} async-done(((bf16[64,2048]{1,0:T(8,128)(2,1)}), bf16[256,2048]{1,0:T(8,128)(2,1)}) %all-gather.29.cloned.1.call-update) | async-done | bytes 1048592 | tf_op jit(solution)/shard_map/all_gather | solution.py:87
  660.7 7.2 fusion.412
  675.0 11.7 collective-permute-done.67
  690.8 11.6 collective-permute-done.103
  712.6 19.0 %all-gather.23.cloned.1.call-done = bf16[256,2048]{1,0:T(8,128)(2,1)} async-done(((bf16[64,2048]{1,0:T(8,128)(2,1)}), bf16[256,2048]{1,0:T(8,128)(2,1)}) %all-gather.23.cloned.1.call-update) | async-done | bytes 1048592 | tf_op jit(solution)/shard_map/all_gather | solution.py:87
  744.0 8.0 convolution_convert_fusion.9
  758.3 16.4 %all-gather.31.cloned.1.call-done = bf16[256,2048]{1,0:T(8,128)(2,1)} async-done(((bf16[64,2048]{1,0:T(8,128)(2,1)}), bf16[256,2048]{1,0:T(8,128)(2,1)}) %all-gather.31.cloned.1.call-update) | async-done | bytes 1048592 | tf_op jit(solution)/shard_map/all_gather | solution.py:87
  786.3 8.2 convolution_convert_fusion.7
  801.1 14.7 convolution_convert_fusion
  836.7 7.9 collective-permute-start.87
  844.6 16.3 %collective-permute-done.106 = bf16[64,2048]{1,0:T(8,128)(2,1)S(1)} collective-permute-done((bf16[64,2048]{1,0:T(8,128)(2,1)S(1)}, bf16[64,2048]{1,0:T(8,128)(2,1)S(1)}, u32[]{:S(2)}, u32[]{:S(2)}) %collective-permute-start.106) | collective-permute-done | bytes 262176 | tf_op jit(solution)/shard_map/ppermute | solution.py:19
  913.5 8.0 fusion.13
  921.5 12.9 all-gather.43.cloned.1.call-done
  938.1 8.1 fusion.7
  951.0 7.1 fusion.9
  990.1 16.4 %collective-permute-start.132 = (bf16[64,2048]{1,0:T(8,128)(2,1)}, bf16[64,2048]{1,0:T(8,128)(2,1)}, u32[]{:S(2)}, u32[]{:S(2)}) collective-permute-start(bf16[64,2048]{1,0:T(8,128)(2,1)} %get-tuple-element.138), channel_id=1, source_target_pairs={{0,1},{1,0},{2,3},{3,2},{4,5},{5,4},{6,7},{7,6},{8,9},{9,8},{10,11... | collective-permute-start | bytes 786440 | tf_op jit(solution)/shard_map/ppermute | solution.py:19
  1015.0 9.7 collective-permute-done.133
  1055.4 12.8 collective-permute-done.176
  1092.3 8.0 convolution_convert_fusion.8
  1112.4 8.2 convolution_convert_fusion.6
  1125.3 15.8 %convolution_convert_fusion.1 = bf16[1024,2816]{1,0:T(8,128)(2,1)} fusion(bf16[512,2048]{1,0:T(8,128)(2,1)} %constant_dynamic-update-slice_fusion.108, bf16[256,1408]{1,0:T(8,128)(2,1)S(1)} %get-tuple-element.73, bf16[256,1408]{1,0:T(8,128)(2,1)S(1)} %get-tuple-element.72, bf16[256,1408]{1,0:T(8,128)(2,1)S(1)} %copy-done.151, ...), kind=kOutput, calls=%fused_computation.41 | convolution fusion | flops 2967207936 | bytes 9699328 | tf_op jit(solution)/shard_map/dot_general | solution.py:117
  1194.0 12.6 all-gather.47.cloned.1.call-done
  1242.6 17.7 %fusion.414 = (bf16[1024,2816]{1,0:T(8,128)(2,1)S(1)}, f32[1024,2816]{1,0:T(8,128)}) fusion(bf16[1024,2816]{1,0:T(8,128)(2,1)} %collective-permute-done.159, bf16[256,1408]{1,0:T(8,128)(2,1)S(1)} %copy-done.147, bf16[256,1408]{1,0:T(8,128)(2,1)S(1)} %copy-done.145, bf16[256,1408]{1,0:T(8,128)(2,1)S(1)} %copy-done.143, ...), kind=kOutput, calls=%fused_computation.941 | convolution fusion | flops 2978742272 | bytes 27000832 | tf_op jit(solution)/shard_map/dot_general | solution.py:117
  1269.7 9.5 collective-permute-done.142
  1365.2 42.4 %collective-permute-done.168 = bf16[128,512]{1,0:T(8,128)(2,1)S(1)} collective-permute-done((bf16[128,512]{1,0:T(8,128)(2,1)S(1)}, bf16[128,512]{1,0:T(8,128)(2,1)S(1)}, u32[]{:S(2)}, u32[]{:S(2)}) %collective-permute-start.168) | collective-permute-done | bytes 131104 | tf_op jit(solution)/shard_map/ppermute | solution.py:19
  1428.2 11.0 collective-permute-done.172
  1441.8 7.2 fusion.416
  1450.8 9.2 collective-permute-done.171
  1468.0 15.9 %collective-permute-done.155 = bf16[256,2816]{1,0:T(8,128)(2,1)S(1)} collective-permute-done((bf16[256,2816]{1,0:T(8,128)(2,1)S(1)}, bf16[256,2816]{1,0:T(8,128)(2,1)S(1)}, u32[]{:S(2)}, u32[]{:S(2)}) %collective-permute-start.155) | collective-permute-done | bytes 1441824 | tf_op jit(solution)/shard_map/ppermute | solution.py:19
  1494.0 6.8 collective-permute-done.157
  1501.1 12.0 collective-permute-done.156
  1519.9 9.6 collective-permute-done.158
  (1464 shorter events, 924.4 us)
Async XLA Ops:
  7.2 65.0 %all-gather.17.cloned.1.call-start = ((), (), s32[]{:S(2)}) async-start(), calls=%async_computation.2 | async-start | bytes 1310720 | tf_op jit(solution)/shard_map/all_gather | solution.py:87
  11.8 39.8 %collective-permute-start.16 = (bf16[256,512]{1,0:T(8,128)(2,1)}, bf16[256,512]{1,0:T(8,128)(2,1)}, u32[]{:S(2)}, u32[]{:S(2)}) collective-permute-start(bf16[256,512]{1,0:T(8,128)(2,1)} %param.26), channel_id=1, source_target_pairs={{0,16},{16,0},{1,17},{17,1},{2,18},{18,2},{3,19},{19,3},{4,20},{20... | collective-permute-start | bytes 786440 | tf_op jit(solution)/shard_map/ppermute | solution.py:19
  35.6 52.1 %all-gather.25.cloned.1.call-start = ((), (), s32[]{:S(2)}) async-start(), calls=%async_computation.6 | async-start | bytes 1310720 | tf_op jit(solution)/shard_map/all_gather | solution.py:87
  36.3 372.0 %all-gather.19.cloned.1.call-start = ((), (), s32[]{:S(2)}) async-start(), calls=%async_computation.3 | async-start | bytes 1310720 | tf_op jit(solution)/shard_map/all_gather | solution.py:87
  149.7 312.3 %all-gather.33.cloned.1.call-start = ((), (), s32[]{:S(2)}) async-start(), calls=%async_computation.10 | async-start | bytes 1310720 | tf_op jit(solution)/shard_map/all_gather | solution.py:87
  202.8 261.5 %all-gather.41.cloned.1.call-start = ((), (), s32[]{:S(2)}) async-start(), calls=%async_computation.14 | async-start | bytes 1310720 | tf_op jit(solution)/shard_map/all_gather | solution.py:87
  206.5 37.4 %collective-permute-start.33 = (bf16[256,1408]{1,0:T(8,128)(2,1)}, bf16[256,1408]{1,0:T(8,128)(2,1)}, u32[]{:S(2)}, u32[]{:S(2)}) collective-permute-start(bf16[256,1408]{1,0:T(8,128)(2,1)} %param.30), channel_id=1, source_target_pairs={{0,4},{4,0},{8,12},{12,8},{1,5},{5,1},{9,13},{13,9},{2,6},{6,2},{1... | collective-permute-start | bytes 2162696 | tf_op jit(solution)/shard_map/ppermute | solution.py:19
  207.3 267.2 %all-gather.21.cloned.1.call-start = ((), (), s32[]{:S(2)}) async-start(), calls=%async_computation.4 | async-start | bytes 1310720 | tf_op jit(solution)/shard_map/all_gather | solution.py:87
  235.1 73.2 %collective-permute-start.37 = (bf16[256,1408]{1,0:T(8,128)(2,1)S(1)}, bf16[256,1408]{1,0:T(8,128)(2,1)S(1)}, u32[]{:S(2)}, u32[]{:S(2)}) collective-permute-start(bf16[256,1408]{1,0:T(8,128)(2,1)S(1)} %copy-done.162), channel_id=1, source_target_pairs={{0,16},{16,0},{1,17},{17,1},{2,18},{18,2},{3,19},{19,3},{4,20},{20... | collective-permute-start | bytes 2162696 | tf_op jit(solution)/shard_map/ppermute | solution.py:19
  243.9 108.0 %collective-permute-start.24 = (bf16[256,2816]{1,0:T(8,128)(2,1)S(1)}, bf16[256,2816]{1,0:T(8,128)(2,1)S(1)}, u32[]{:S(2)}, u32[]{:S(2)}) collective-permute-start(bf16[256,2816]{1,0:T(8,128)(2,1)S(1)} %get-tuple-element.178), channel_id=1, source_target_pairs={{0,4},{4,0},{8,12},{12,8},{1,5},{5,1},{9,13},{13,9},{2,6},{6,2},{1... | collective-permute-start | bytes 4325384 | tf_op jit(solution)/shard_map/ppermute | solution.py:19
  256.4 37.0 %collective-permute-start.49 = (bf16[256,640]{1,0:T(8,128)(2,1)S(1)}, bf16[256,640]{1,0:T(8,128)(2,1)S(1)}, u32[]{:S(2)}, u32[]{:S(2)}) collective-permute-start(bf16[256,640]{1,0:T(8,128)(2,1)S(1)} %get-tuple-element.226), channel_id=1, source_target_pairs={{0,16},{16,0},{1,17},{17,1},{2,18},{18,2},{3,19},{19,3},{4,20},{20... | collective-permute-start | bytes 983048 | tf_op jit(solution)/shard_map/ppermute | solution.py:19
  297.3 54.5 %collective-permute-start.25 = (bf16[256,2816]{1,0:T(8,128)(2,1)S(1)}, bf16[256,2816]{1,0:T(8,128)(2,1)S(1)}, u32[]{:S(2)}, u32[]{:S(2)}) collective-permute-start(bf16[256,2816]{1,0:T(8,128)(2,1)S(1)} %get-tuple-element.178), channel_id=1, source_target_pairs={{0,8},{4,12},{8,0},{12,4},{1,9},{5,13},{9,1},{13,5},{2,10},{6,14},... | collective-permute-start | bytes 4325384 | tf_op jit(solution)/shard_map/ppermute | solution.py:19
  303.8 42.2 %collective-permute-start.82 = (bf16[256,1408]{1,0:T(8,128)(2,1)S(1)}, bf16[256,1408]{1,0:T(8,128)(2,1)S(1)}, u32[]{:S(2)}, u32[]{:S(2)}) collective-permute-start(bf16[256,1408]{1,0:T(8,128)(2,1)S(1)} %copy-done.163), channel_id=1, source_target_pairs={{0,16},{16,0},{1,17},{17,1},{2,18},{18,2},{3,19},{19,3},{4,20},{20... | collective-permute-start | bytes 2162696 | tf_op jit(solution)/shard_map/ppermute | solution.py:19
  351.8 49.9 %collective-permute-start.28 = (bf16[256,2816]{1,0:T(8,128)(2,1)S(1)}, bf16[256,2816]{1,0:T(8,128)(2,1)S(1)}, u32[]{:S(2)}, u32[]{:S(2)}) collective-permute-start(bf16[256,2816]{1,0:T(8,128)(2,1)S(1)} %get-tuple-element.178), channel_id=1, source_target_pairs={{0,16},{16,0},{1,17},{17,1},{2,18},{18,2},{3,19},{19,3},{4,20},{20... | collective-permute-start | bytes 4325384 | tf_op jit(solution)/shard_map/ppermute | solution.py:19
  354.2 183.1 %collective-permute-start.73 = (bf16[256,2816]{1,0:T(8,128)(2,1)}, bf16[256,2816]{1,0:T(8,128)(2,1)}, u32[]{:S(2)}, u32[]{:S(2)}) collective-permute-start(bf16[256,2816]{1,0:T(8,128)(2,1)} %get-tuple-element.174), channel_id=1, source_target_pairs={{0,16},{16,0},{1,17},{17,1},{2,18},{18,2},{3,19},{19,3},{4,20},{20... | collective-permute-start | bytes 4325384 | tf_op jit(solution)/shard_map/ppermute | solution.py:19
  354.3 44.2 %collective-permute-start.26 = (bf16[128,2816]{1,0:T(8,128)(2,1)S(1)}, bf16[128,2816]{1,0:T(8,128)(2,1)S(1)}, u32[]{:S(2)}, u32[]{:S(2)}) collective-permute-start(bf16[128,2816]{1,0:T(8,128)(2,1)S(1)} %slice.1278), channel_id=1, source_target_pairs={{0,4},{4,0},{8,12},{12,8},{1,5},{5,1},{9,13},{13,9},{2,6},{6,2},{1... | collective-permute-start | bytes 2162696 | tf_op jit(solution)/shard_map/ppermute | solution.py:19
  445.5 68.2 %collective-permute-start.72 = (bf16[128,2816]{1,0:T(8,128)(2,1)}, bf16[128,2816]{1,0:T(8,128)(2,1)}, u32[]{:S(2)}, u32[]{:S(2)}) collective-permute-start(bf16[128,2816]{1,0:T(8,128)(2,1)} %slice.1298), channel_id=1, source_target_pairs={{0,8},{4,12},{8,0},{12,4},{1,9},{5,13},{9,1},{13,5},{2,10},{6,14},... | collective-permute-start | bytes 2162696 | tf_op jit(solution)/shard_map/ppermute | solution.py:19
  448.1 116.8 %all-gather.27.cloned.1.call-start = ((), (), s32[]{:S(2)}) async-start(), calls=%async_computation.7 | async-start | bytes 1310720 | tf_op jit(solution)/shard_map/all_gather | solution.py:87
  495.7 44.2 %collective-permute-start.74 = (bf16[256,2816]{1,0:T(8,128)(2,1)}, bf16[256,2816]{1,0:T(8,128)(2,1)}, u32[]{:S(2)}, u32[]{:S(2)}) collective-permute-start(bf16[256,2816]{1,0:T(8,128)(2,1)} %collective-permute-done.69), channel_id=1, source_target_pairs={{0,16},{16,0},{1,17},{17,1},{2,18},{18,2},{3,19},{19,3},{4,20},{20... | collective-permute-start | bytes 4325384 | tf_op jit(solution)/shard_map/ppermute | solution.py:19
  535.4 168.3 %collective-permute-start.76 = (bf16[128,2816]{1,0:T(8,128)(2,1)}, bf16[128,2816]{1,0:T(8,128)(2,1)}, u32[]{:S(2)}, u32[]{:S(2)}) collective-permute-start(bf16[128,2816]{1,0:T(8,128)(2,1)} %collective-permute-done.71), channel_id=1, source_target_pairs={{0,16},{16,0},{1,17},{17,1},{2,18},{18,2},{3,19},{19,3},{4,20},{20... | collective-permute-start | bytes 2162696 | tf_op jit(solution)/shard_map/ppermute | solution.py:19
  535.4 170.5 %collective-permute-start.77 = (bf16[128,2816]{1,0:T(8,128)(2,1)}, bf16[128,2816]{1,0:T(8,128)(2,1)}, u32[]{:S(2)}, u32[]{:S(2)}) collective-permute-start(bf16[128,2816]{1,0:T(8,128)(2,1)} %collective-permute-done.72), channel_id=1, source_target_pairs={{0,16},{16,0},{1,17},{17,1},{2,18},{18,2},{3,19},{19,3},{4,20},{20... | collective-permute-start | bytes 2162696 | tf_op jit(solution)/shard_map/ppermute | solution.py:19
  537.1 98.0 %all-gather.29.cloned.1.call-start = ((), (), s32[]{:S(2)}) async-start(), calls=%async_computation.8 | async-start | bytes 1310720 | tf_op jit(solution)/shard_map/all_gather | solution.py:87
  607.3 124.3 %all-gather.23.cloned.1.call-start = ((), (), s32[]{:S(2)}) async-start(), calls=%async_computation.5 | async-start | bytes 1310720 | tf_op jit(solution)/shard_map/all_gather | solution.py:87
  703.7 71.0 %all-gather.31.cloned.1.call-start = ((), (), s32[]{:S(2)}) async-start(), calls=%async_computation.9 | async-start | bytes 1310720 | tf_op jit(solution)/shard_map/all_gather | solution.py:87
  712.1 193.1 %all-gather.35.cloned.1.call-start = ((), (), s32[]{:S(2)}) async-start(), calls=%async_computation.11 | async-start | bytes 1310720 | tf_op jit(solution)/shard_map/all_gather | solution.py:87
  754.0 65.3 %collective-permute-start.110 = (bf16[64,2048]{1,0:T(8,128)(2,1)}, bf16[64,2048]{1,0:T(8,128)(2,1)S(1)}, u32[]{:S(2)}, u32[]{:S(2)}) collective-permute-start(bf16[64,2048]{1,0:T(8,128)(2,1)} %get-tuple-element.148), channel_id=1, source_target_pairs={{0,3},{1,2},{2,1},{3,0},{4,7},{5,6},{6,5},{7,4},{8,11},{9,10},{10,... | collective-permute-start | bytes 786440 | tf_op jit(solution)/shard_map/ppermute | solution.py:19
  755.7 68.5 %collective-permute-start.109 = (bf16[64,2048]{1,0:T(8,128)(2,1)}, bf16[64,2048]{1,0:T(8,128)(2,1)}, u32[]{:S(2)}, u32[]{:S(2)}) collective-permute-start(bf16[64,2048]{1,0:T(8,128)(2,1)} %get-tuple-element.149), channel_id=1, source_target_pairs={{0,2},{1,3},{2,0},{3,1},{4,6},{5,7},{6,4},{7,5},{8,10},{9,11},{10,... | collective-permute-start | bytes 786440 | tf_op jit(solution)/shard_map/ppermute | solution.py:19
  756.8 68.0 %collective-permute-start.108 = (bf16[64,2048]{1,0:T(8,128)(2,1)}, bf16[64,2048]{1,0:T(8,128)(2,1)}, u32[]{:S(2)}, u32[]{:S(2)}) collective-permute-start(bf16[64,2048]{1,0:T(8,128)(2,1)} %get-tuple-element.147), channel_id=1, source_target_pairs={{0,1},{1,0},{2,3},{3,2},{4,5},{5,4},{6,7},{7,6},{8,9},{9,8},{10,11... | collective-permute-start | bytes 786440 | tf_op jit(solution)/shard_map/ppermute | solution.py:19
  828.6 39.9 %collective-permute-start.89 = (bf16[64,2048]{1,0:T(8,128)(2,1)}, bf16[64,2048]{1,0:T(8,128)(2,1)}, u32[]{:S(2)}, u32[]{:S(2)}) collective-permute-start(bf16[64,2048]{1,0:T(8,128)(2,1)} %get-tuple-element.151), channel_id=1, source_target_pairs={{0,3},{1,2},{2,1},{3,0},{4,7},{5,6},{6,5},{7,4},{8,11},{9,10},{10,... | collective-permute-start | bytes 786440 | tf_op jit(solution)/shard_map/ppermute | solution.py:19
  873.1 61.3 %all-gather.43.cloned.1.call-start = ((), (), s32[]{:S(2)}) async-start(), calls=%async_computation.15 | async-start | bytes 1310720 | tf_op jit(solution)/shard_map/all_gather | solution.py:87
  905.1 181.3 %all-gather.37.cloned.1.call-start = ((), (), s32[]{:S(2)}) async-start(), calls=%async_computation.12 | async-start | bytes 1310720 | tf_op jit(solution)/shard_map/all_gather | solution.py:87
  987.4 37.3 %collective-permute-start.133 = (bf16[64,2048]{1,0:T(8,128)(2,1)}, bf16[64,2048]{1,0:T(8,128)(2,1)}, u32[]{:S(2)}, u32[]{:S(2)}) collective-permute-start(bf16[64,2048]{1,0:T(8,128)(2,1)} %get-tuple-element.140), channel_id=1, source_target_pairs={{0,2},{1,3},{2,0},{3,1},{4,6},{5,7},{6,4},{7,5},{8,10},{9,11},{10,... | collective-permute-start | bytes 786440 | tf_op jit(solution)/shard_map/ppermute | solution.py:19
  1029.7 76.8 %all-gather.45.cloned.1.call-start = ((), (), s32[]{:S(2)}) async-start(), calls=%async_computation.16 | async-start | bytes 1310720 | tf_op jit(solution)/shard_map/all_gather | solution.py:87
  1038.2 139.5 %all-gather.39.cloned.1.call-start = ((), (), s32[]{:S(2)}) async-start(), calls=%async_computation.13 | async-start | bytes 1310720 | tf_op jit(solution)/shard_map/all_gather | solution.py:87
  1104.0 38.1 %collective-permute-start.118 = (bf16[64,2048]{1,0:T(8,128)(2,1)}, bf16[64,2048]{1,0:T(8,128)(2,1)}, u32[]{:S(2)}, u32[]{:S(2)}) collective-permute-start(bf16[64,2048]{1,0:T(8,128)(2,1)} %get-tuple-element.137), channel_id=1, source_target_pairs={{0,2},{1,3},{2,0},{3,1},{4,6},{5,7},{6,4},{7,5},{8,10},{9,11},{10,... | collective-permute-start | bytes 786440 | tf_op jit(solution)/shard_map/ppermute | solution.py:19
  1104.0 38.1 %collective-permute-start.117 = (bf16[64,2048]{1,0:T(8,128)(2,1)}, bf16[64,2048]{1,0:T(8,128)(2,1)}, u32[]{:S(2)}, u32[]{:S(2)}) collective-permute-start(bf16[64,2048]{1,0:T(8,128)(2,1)} %get-tuple-element.135), channel_id=1, source_target_pairs={{0,1},{1,0},{2,3},{3,2},{4,5},{5,4},{6,7},{7,6},{8,9},{9,8},{10,11... | collective-permute-start | bytes 786440 | tf_op jit(solution)/shard_map/ppermute | solution.py:19
  1142.1 100.3 %collective-permute-start.159 = (bf16[1024,2816]{1,0:T(8,128)(2,1)}, bf16[1024,2816]{1,0:T(8,128)(2,1)}, u32[]{:S(2)}, u32[]{:S(2)}) collective-permute-start(bf16[1024,2816]{1,0:T(8,128)(2,1)} %convolution_convert_fusion), channel_id=1, source_target_pairs={{0,16},{16,0},{1,17},{17,1},{2,18},{18,2},{3,19},{19,3},{4,20},{20... | collective-permute-start | bytes 17301512 | tf_op jit(solution)/shard_map/ppermute | solution.py:19
  1150.8 55.7 %all-gather.47.cloned.1.call-start = ((), (), s32[]{:S(2)}) async-start(), calls=%async_computation.17 | async-start | bytes 1310720 | tf_op jit(solution)/shard_map/all_gather | solution.py:87
  1269.1 172.7 %collective-permute-start.154 = (bf16[1024,2816]{1,0:T(8,128)(2,1)}, bf16[1024,2816]{1,0:T(8,128)(2,1)}, u32[]{:S(2)}, u32[]{:S(2)}) collective-permute-start(bf16[1024,2816]{1,0:T(8,128)(2,1)} %convolution_convert_fusion.1), channel_id=1, source_target_pairs={{0,16},{16,0},{1,17},{17,1},{2,18},{18,2},{3,19},{19,3},{4,20},{20... | collective-permute-start | bytes 17301512 | tf_op jit(solution)/shard_map/ppermute | solution.py:19
  1269.1 70.0 %collective-permute-start.169 = (bf16[1024,1408]{1,0:T(8,128)(2,1)}, bf16[1024,1408]{1,0:T(8,128)(2,1)S(1)}, u32[]{:S(2)}, u32[]{:S(2)}) collective-permute-start(bf16[1024,1408]{1,0:T(8,128)(2,1)} %convolution_convert_fusion.4), channel_id=1, source_target_pairs={{0,16},{16,0},{1,17},{17,1},{2,18},{18,2},{3,19},{19,3},{4,20},{20... | collective-permute-start | bytes 8650760 | tf_op jit(solution)/shard_map/ppermute | solution.py:19
  1269.6 72.5 %collective-permute-start.164 = (bf16[1024,512]{1,0:T(8,128)(2,1)}, bf16[1024,512]{1,0:T(8,128)(2,1)}, u32[]{:S(2)}, u32[]{:S(2)}) collective-permute-start(bf16[1024,512]{1,0:T(8,128)(2,1)} %convolution_convert_fusion.28), channel_id=1, source_target_pairs={{0,16},{16,0},{1,17},{17,1},{2,18},{18,2},{3,19},{19,3},{4,20},{20... | collective-permute-start | bytes 3145736 | tf_op jit(solution)/shard_map/ppermute | solution.py:19
  1279.1 80.2 %collective-permute-start.144 = (bf16[1024,640]{1,0:T(8,128)(2,1)}, bf16[1024,640]{1,0:T(8,128)(2,1)}, u32[]{:S(2)}, u32[]{:S(2)}) collective-permute-start(bf16[1024,640]{1,0:T(8,128)(2,1)} %convolution_convert_fusion.24), channel_id=1, source_target_pairs={{0,16},{16,0},{1,17},{17,1},{2,18},{18,2},{3,19},{19,3},{4,20},{20... | collective-permute-start | bytes 3932168 | tf_op jit(solution)/shard_map/ppermute | solution.py:19
  1279.1 140.9 %collective-permute-start.162 = (bf16[256,2816]{1,0:T(8,128)(2,1)}, bf16[256,2816]{1,0:T(8,128)(2,1)}, u32[]{:S(2)}, u32[]{:S(2)}) collective-permute-start(bf16[256,2816]{1,0:T(8,128)(2,1)} %pad_maximum_fusion.5), channel_id=1, source_target_pairs={{0,8},{4,12},{8,0},{12,4},{1,9},{5,13},{9,1},{13,5},{2,10},{6,14},... | collective-permute-start | bytes 4325384 | tf_op jit(solution)/shard_map/ppermute | solution.py:19
  1356.3 53.5 %collective-permute-start.160 = (bf16[256,2816]{1,0:T(8,128)(2,1)S(1)}, bf16[256,2816]{1,0:T(8,128)(2,1)S(1)}, u32[]{:S(2)}, u32[]{:S(2)}) collective-permute-start(bf16[256,2816]{1,0:T(8,128)(2,1)S(1)} %copy-done.84), channel_id=1, source_target_pairs={{0,4},{4,0},{8,12},{12,8},{1,5},{5,1},{9,13},{13,9},{2,6},{6,2},{1... | collective-permute-start | bytes 4325384 | tf_op jit(solution)/shard_map/ppermute | solution.py:19
  1357.7 67.6 %collective-permute-start.170 = (bf16[256,1408]{1,0:T(8,128)(2,1)S(1)}, bf16[256,1408]{1,0:T(8,128)(2,1)S(1)}, u32[]{:S(2)}, u32[]{:S(2)}) collective-permute-start(bf16[256,1408]{1,0:T(8,128)(2,1)S(1)} %pad_maximum_fusion.22), channel_id=1, source_target_pairs={{0,4},{4,0},{8,12},{12,8},{1,5},{5,1},{9,13},{13,9},{2,6},{6,2},{1... | collective-permute-start | bytes 2162696 | tf_op jit(solution)/shard_map/ppermute | solution.py:19
  1364.4 43.1 %collective-permute-start.168 = (bf16[128,512]{1,0:T(8,128)(2,1)S(1)}, bf16[128,512]{1,0:T(8,128)(2,1)S(1)}, u32[]{:S(2)}, u32[]{:S(2)}) collective-permute-start(bf16[128,512]{1,0:T(8,128)(2,1)S(1)} %get-tuple-element.109), channel_id=1, source_target_pairs={{0,4},{4,0},{8,12},{12,8},{1,5},{5,1},{9,13},{13,9},{2,6},{6,2},{1... | collective-permute-start | bytes 393224 | tf_op jit(solution)/shard_map/ppermute | solution.py:19
  1423.6 39.4 %collective-permute-start.161 = (bf16[128,2816]{1,0:T(8,128)(2,1)}, bf16[128,2816]{1,0:T(8,128)(2,1)}, u32[]{:S(2)}, u32[]{:S(2)}) collective-permute-start(bf16[128,2816]{1,0:T(8,128)(2,1)} %fusion.70), channel_id=1, source_target_pairs={{0,8},{4,12},{8,0},{12,4},{1,9},{5,13},{9,1},{13,5},{2,10},{6,14},... | collective-permute-start | bytes 2162696 | tf_op jit(solution)/shard_map/ppermute | solution.py:19
  1465.4 49.6 %collective-permute-start.163 = (bf16[128,2816]{1,0:T(8,128)(2,1)S(1)}, bf16[128,2816]{1,0:T(8,128)(2,1)S(1)}, u32[]{:S(2)}, u32[]{:S(2)}) collective-permute-start(bf16[128,2816]{1,0:T(8,128)(2,1)S(1)} %get-tuple-element.59), channel_id=1, source_target_pairs={{0,4},{4,0},{8,12},{12,8},{1,5},{5,1},{9,13},{13,9},{2,6},{6,2},{1... | collective-permute-start | bytes 2162696 | tf_op jit(solution)/shard_map/ppermute | solution.py:19
  (413 other events, 7290.7 us)
Sparse Core Ops, SparseCore 0:
  27.6 32.2 all-gather.16
  61.4 26.1 all-gather.24
  149.8 26.7 all-gather.18
  202.9 28.1 all-gather.32
  232.5 27.4 all-gather.40
  448.2 26.2 all-gather.20
  537.2 27.6 all-gather.26
  607.4 27.6 all-gather.28
  703.8 27.7 all-gather.22
  733.5 41.1 all-gather.30
  873.2 27.2 all-gather.34
  905.2 29.1 all-gather.42
  1029.8 27.2 all-gather.36
  1058.6 27.4 all-gather.44
  1150.9 26.7 all-gather.38
  1179.1 27.4 all-gather.46
where the time goes:
time: 1570 us; the launch traced here: 1560 us
  waiting for transfers between devices  587 us (37%)
  matrix products  302 us (19%)
  local copies, waits for them, and re-layouts  292 us (19%)
  starting transfers between devices  226 us (14%)
  other arithmetic  133 us (8%)
  between operations  19.6 us (1%)
    ppermute x184, waiting for transfers between devices, swap(): lax.ppermute(value, axis, [(source, source ^ bits) for source in range(co...  461 us
    dot_general x49, matrix products, dot(): lax.dot_general(left, right, (((left_dim,), (right_dim,)), ((), ())), pre...  209 us
    ppermute x184, starting transfers between devices, swap(): lax.ppermute(value, axis, [(source, source ^ bits) for source in range(co...  202 us
    all_gather x16, waiting for transfers between devices, gather_tokens(): return lax.all_gather(piece, 'tensor', axis=0, tiled=True)  117 us
    unnamed x642, local copies, waits for them, and re-layouts  109 us
    rev x24, local copies, waits for them, and re-layouts, relative(): other = jnp.flip(paired, axis=-2).reshape(values.shape)  69.6 us
  transfers between devices with their start and end apart: 202, of which 88 were waited for; matrix products, arithmetic and copies ran while one was open for 40% of the time, Pallas kernels for 0%

commit v1 on v0

v1 whole, which is shorter than its diff:
```python
import functools

import jax
import jax.numpy as jnp
from jax import lax
from jax.experimental import pallas as pl
from jax.experimental.pallas import tpu as pltpu
from jax.sharding import PartitionSpec as P

H = 32
KV = 4
HD = 64
WINDOW = 512
EPSILON = 1e-05
THETA = 10000.0
NEGATIVE = -1e30
BF = jnp.bfloat16
F32 = jnp.float32
PAIR = 2 * HD
COST = {
    "project": 5.0,
    "attend": 12.0,
    "attend_back": 13.0,
    "project_back": 5.0,
    "feed": 13.0,
    "feed_back": 15.0,
    "weight_grads": 11.0,
    "keep_kernel": 13.0,
    "fold": 6.0,
    "finish_ffn": 6.0,
    "stacked": 4.0,
}
WEIGHT = 3.0e6
VMEM_LIMIT = 60 * 1024 * 1024


def swap(value, axis, bits):
    count = lax.axis_size(axis)
    return lax.ppermute(value, axis, [(source, source ^ bits) for source in range(count)])


def gather_near(stack):
    if lax.axis_size("context") != 4:
        return [stack]
    return [stack, swap(stack, "context", 1), swap(stack, "context", 2)]


def gather_far(parts, queue):
    count = lax.axis_size("context")
    if count == 4:
        low, high = halves(parts[2], parts[1], queue)
        parts = parts + [swap(low, "context", 1), swap(high, "context", 2)]
    else:
        bit = 1
        while bit < count:
            parts = parts + [swap(part, "context", bit) for part in parts]
            bit *= 2
    return parts + [swap(part, "dp", 1) for part in parts]


def segments(parts, low, high, block):
    found = []
    side = len(parts) // 2
    full = parts[0].shape[0]
    for core in range(2):
        feature = core * (side - (1 if side == 5 else 0)) * block
        for number in range(side):
            at = core * side + number
            if side == 5 and number >= 3:
                cut = full // 2
                start, stop = (0, cut) if number == 3 else (cut, full)
                first, last = max(low, start), min(high, stop)
                if first < last:
                    found.append((at, first - start, last - first, feature + 3 * block + first - low))
            else:
                found.append((at, low, high - low, feature + number * block))
    return found


def gather_tokens(piece):
    return lax.all_gather(piece, "tensor", axis=0, tiled=True)


def exchange_tokens(chunks):
    return [chunks[0]] + [swap(chunks[k], "tensor", k) for k in range(1, len(chunks))]


def exchange_blocks(pieces):
    return [pieces[0]] + [swap(pieces[r], "context", r) for r in range(1, len(pieces))]


def dot(left, right, left_dim, right_dim):
    return lax.dot_general(
        left, right, (((left_dim,), (right_dim,)), ((), ())), preferred_element_type=F32
    )


class Queue:
    def __init__(self, place):
        self.place = place
        self.last = None
        self.due = []


def call(kernel, outs, ins, queue, grid=(1,), in_specs=None, out_specs=None, scratch=()):
    whole = lambda x: pl.BlockSpec(x.shape, lambda *i, n=len(x.shape): (0,) * n)
    in_specs = [whole(x) if s is None else s for x, s in zip(ins, in_specs or [None] * len(ins))]
    out_specs = [whole(x) if s is None else s for x, s in zip(outs, out_specs or [None] * len(outs))]
    before = [x for x in [queue.last] + queue.due if x is not None]
    queue.due = []
    count = len(ins)
    name = kernel.__qualname__.split(".")[0]
    if "fold" in kernel.__qualname__ or "keep" in kernel.__qualname__:
        name = kernel.__qualname__.split(".")[-1]

    def ordered(place, *refs):
        kernel(place, *refs[:count], *refs[count + len(before) :])

    found = list(pl.pallas_call(
        ordered,
        name=name,
        out_shape=outs,
        grid_spec=pltpu.PrefetchScalarGridSpec(
            num_scalar_prefetch=1,
            grid=grid,
            in_specs=in_specs + [pl.BlockSpec(memory_space=pl.ANY)] * len(before),
            out_specs=out_specs,
            scratch_shapes=list(scratch),
        ),
        compiler_params=pltpu.CompilerParams(
            vmem_limit_bytes=VMEM_LIMIT, dimension_semantics=("arbitrary",) * len(grid)
        ),
        cost_estimate=pl.CostEstimate(
            flops=int(COST.get(name, 3.0) * 1 * 1.0e9), bytes_accessed=int(COST.get(name, 3.0) * 1 * 3.0e6), transcendentals=0
        ),
    )(queue.place, *ins, *before))
    queue.last = min(found, key=lambda x: x.size)
    return found


def shape(dims, dtype=BF):
    return jax.ShapeDtypeStruct(dims, dtype)


def stacked(pieces, queue):
    rows, columns = pieces[0].shape

    def kernel(place, *refs):
        for number, source in enumerate(refs[:-1]):
            @pl.when(pl.program_id(0) == number)
            def _(source=source):
                refs[-1][...] = source[...]

    return call(
        kernel,
        [shape((len(pieces) * rows, columns))],
        pieces,
        queue,
        grid=(len(pieces),),
        out_specs=[pl.BlockSpec((rows, columns), lambda i, place: (i, 0))],
    )[0]


def halves(first, second, queue):
    rows, columns = first.shape
    half = rows // 2

    def kernel(place, first_ref, second_ref, upper, lower):
        upper[...] = first_ref[...]
        lower[...] = second_ref[...]

    return call(
        kernel,
        [shape((half, columns))] * 2,
        [first, second],
        queue,
        in_specs=[
            pl.BlockSpec((half, columns), lambda i, place: (0, 0)),
            pl.BlockSpec((half, columns), lambda i, place: (1, 0)),
        ],
    )


def placed(pieces, queue):
    rows, columns = pieces[0].shape

    def kernel(place, *refs):
        for k, source in enumerate(refs[:-1]):
            at = pl.multiple_of((place[2] ^ k) * rows, rows)
            refs[-1][pl.ds(at, rows), :] = source[...]

    return call(kernel, [shape((len(pieces) * rows, columns))], pieces, queue)[0]


def gain_vectors(kvg, kv_at, width, queue):
    def kernel(place, *refs):
        row = lax.broadcasted_iota(jnp.int32, (8, PAIR), 0)
        pick = (row == lax.broadcasted_iota(jnp.int32, (8, PAIR), 1)).astype(BF)
        for at, low, rows, feature in kv_at:
            refs[-1][:, feature : feature + rows] = dot(pick, refs[at][low : low + rows, :], 1, 1)

    return call(
        kernel,
        [shape((8, width), F32)],
        kvg,
        queue,
        in_specs=[pl.BlockSpec((p.shape[0], PAIR), lambda i, place: (0, 2)) for p in kvg],
    )[0]


def reorder(pieces, queue):
    width = pieces[0].shape[-1]
    count = 2 * lax.axis_size("context")
    block = width // count

    def kernel(place, *refs):
        for source, target in zip(refs[: len(pieces)], refs[len(pieces) :]):
            for r in range(count):
                at = pl.multiple_of((place[0] ^ r) * block, block)
                target[:, r * block : (r + 1) * block] = source[:, pl.ds(at, block)]

    return call(kernel, [shape(p.shape, p.dtype) for p in pieces], pieces, queue)


def turned(tile, cosine, sine):
    lane = lax.broadcasted_iota(jnp.int32, tile.shape, 1)
    half = HD // 2
    other = jnp.where(
        lane % HD < half, pltpu.roll(tile, PAIR - half, 1), pltpu.roll(tile, half, 1)
    )
    return tile * cosine + other * sine


def keys_only(table, fill):
    lane = lax.broadcasted_iota(jnp.int32, table.shape, 1)
    return jnp.where(lane < HD, table, fill)


def put_chunks(place, outs, total):
    rows = outs[0].shape[0]
    for k, out in enumerate(outs):
        at = pl.multiple_of((place[2] ^ k) * rows, rows)
        out[...] = total[pl.ds(at, rows), :].astype(BF)


def project(sources, gain, qo, qo_at, kvg, kv_at, tables, queue):
    piece_rows, width = sources[0].shape
    tokens = piece_rows * len(sources)
    columns = qo[0].shape[1]
    raw = gain is not None
    count = len(qo)

    def kernel(place, *refs):
        if raw:
            refs, (query, pair, normed) = refs[:-3], refs[-3:]
            gain_ref, refs = refs[0], refs[1:]
        else:
            refs, (query, pair) = refs[:-2], refs[-2:]
        source_refs, refs = refs[: len(sources)], refs[len(sources) :]
        source = source_refs[0]
        qo_refs, kv_refs, (cos_ref, sin_ref) = refs[:count], refs[count:-2], refs[-2:]
        if raw:
            for k, piece in enumerate(source_refs):
                values = piece[...].astype(F32)
                scale = lax.rsqrt(jnp.mean(values * values, axis=1, keepdims=True) + EPSILON)
                at = 0
                if len(sources) > 1:
                    at = pl.multiple_of((place[2] ^ k) * piece_rows, piece_rows)
                normed[pl.ds(at, piece_rows), :] = (values * scale * gain_ref[...]).astype(BF)
            source = normed
        cosine, sine = cos_ref[...], sin_ref[...]
        pre = 0.0
        for at, low, rows, feature in qo_at:
            pre += dot(source[:, feature : feature + rows], qo_refs[at][low : low + rows, :], 1, 0)
        for tile in range(columns // PAIR):
            part = slice(tile * PAIR, (tile + 1) * PAIR)
            query[:, part] = turned(pre[:, part], cosine, sine).astype(BF)
        pre = 0.0
        for at, low, rows, feature in kv_at:
            pre += dot(source[:, feature : feature + rows], kv_refs[at][low : low + rows, :], 1, 0)
        pair[...] = turned(pre, keys_only(cosine, 1.0), keys_only(sine, 0.0)).astype(BF)

    outs = [shape((tokens, columns)), shape((tokens, PAIR))]
    if raw:
        outs.append(shape((tokens, width)))
    ins = ([gain] if raw else []) + list(sources) + list(qo) + list(kvg[1]) + list(tables)
    layer = kvg[0]
    in_specs = [None] * (len(ins) - len(kvg[1]) - 2)
    in_specs += [
        pl.BlockSpec((part.shape[0], PAIR), lambda i, place: (0, layer)) for part in kvg[1]
    ]
    in_specs += [None, None]
    found = call(
        kernel,
        outs,
        ins,
        queue,
        in_specs=in_specs,
    )
    return found if raw else found + [sources[0]]


def mask_bias(place, bias, tokens, blocks, is_window):
    query_pos = place[1] * tokens + lax.broadcasted_iota(jnp.int32, (tokens, tokens), 1)
    key_row = lax.broadcasted_iota(jnp.int32, (tokens, tokens), 0)
    for r in range(blocks):
        key_pos = (place[1] ^ r) * tokens + key_row
        allowed = key_pos <= query_pos
        if is_window:
            allowed = allowed & (query_pos - key_pos < WINDOW)
        bias[r * tokens : (r + 1) * tokens, :] = jnp.where(allowed, 0.0, NEGATIVE)


def head_masks(tokens):
    lane = lax.broadcasted_iota(jnp.int32, (tokens, PAIR), 1)
    return (lane < HD, lane >= HD)


def attend(query, blocks, qo, o_at, is_window, width, queue):
    tokens, columns = query.shape
    heads = columns // HD
    count, many = len(blocks), len(qo)
    total_keys = count * tokens
    chunks = lax.axis_size("tensor")

    def kernel(place, query_ref, *refs):
        block_refs, refs = refs[:count], refs[count:]
        qo_refs, refs = refs[:many], refs[many:]
        mixed, stats, refs = refs[0], refs[1], refs[2:]
        outs, (bias, keys_twice, values_t, total) = refs[:chunks], refs[chunks:]
        mask_bias(place, bias, tokens, count, is_window)
        for r in range(count):
            rows = slice(r * tokens, (r + 1) * tokens)
            both = block_refs[r][...].astype(F32)
            first = keys_only(both, 0.0)
            keys_twice[rows, :] = (first + pltpu.roll(first, HD, 1)).astype(BF)
            values_t[:, rows] = pltpu.roll(both, HD, 1).T[:HD, :].astype(BF)
        masks = head_masks(tokens)

        def one_pair(number, carry):
            at = pl.multiple_of(number * PAIR, PAIR)
            queries = query_ref[:, pl.ds(at, PAIR)].astype(F32) * HD ** (-0.5)
            parts = []
            for side in range(2):
                own = jnp.where(masks[side], queries, 0.0).astype(BF)
                scores = dot(keys_twice[...], own, 1, 1) + bias[...]
                top = jnp.max(scores, axis=0, keepdims=True)
                expo = jnp.exp(scores - top)
                amount = jnp.sum(expo, axis=0, keepdims=True)
                parts.append(dot(values_t[...], expo.astype(BF), 1, 0) * (1.0 / amount))
                stats[2 * number + side] = top + jnp.log(amount)
            mixed[:, pl.ds(at, PAIR)] = jnp.concatenate(parts, axis=0).T.astype(BF)
            return carry

        lax.fori_loop(0, heads // 2, one_pair, 0)
        for at, low, rows, feature in o_at:
            total[:, feature : feature + rows] = dot(
                mixed[...], qo_refs[at][low : low + rows, :], 1, 1
            )
        put_chunks(place, outs, total)

    outs = [shape((tokens, columns)), shape((heads, 1, tokens), F32)]
    outs += [shape((tokens // chunks, width)) for _ in range(chunks)]
    found = call(
        kernel,
        outs,
        [query] + list(blocks) + list(qo),
        queue,
        scratch=[
            pltpu.VMEM((total_keys, tokens), F32),
            pltpu.VMEM((total_keys, PAIR), BF),
            pltpu.VMEM((HD, total_keys), BF),
            pltpu.VMEM((tokens, width), F32),
        ],
    )
    return found[0], found[1], found[2:]


def attend_back(mid_low, query, blocks, stats, qo, o_at, tables, is_window, queue):
    tokens, columns = query.shape
    width = mid_low.shape[1]
    heads = columns // HD
    count, many = len(blocks), len(qo)
    total_keys = count * tokens

    def kernel(place, mid_ref, query_ref, stats_ref, cos_ref, sin_ref, *refs):
        block_refs, refs = refs[:count], refs[count:]
        qo_refs, refs = refs[:many], refs[many:]
        grad_query, refs = refs[0], refs[1:]
        outs, refs = refs[:count], refs[count:]
        bias, keys_twice, values_twice, keys_t, grad_mixed, key_sum, value_sum = refs
        pre = 0.0
        for at, low, rows, feature in o_at:
            pre += dot(mid_ref[:, feature : feature + rows], qo_refs[at][low : low + rows, :], 1, 0)
        grad_mixed[...] = pre.astype(BF)
        mask_bias(place, bias, tokens, count, is_window)
        for r in range(count):
            rows = slice(r * tokens, (r + 1) * tokens)
            both = block_refs[r][...].astype(F32)
            first = keys_only(both, 0.0)
            last = both - first
            keys_twice[rows, :] = (first + pltpu.roll(first, HD, 1)).astype(BF)
            values_twice[rows, :] = (last + pltpu.roll(last, HD, 1)).astype(BF)
            keys_t[:, rows] = both.T[:HD, :].astype(BF)
        key_sum[...] = jnp.zeros_like(key_sum)
        value_sum[...] = jnp.zeros_like(value_sum)
        masks = head_masks(tokens)
        cosine, sine = cos_ref[...], sin_ref[...]

        def one_pair(number, carry):
            at = pl.multiple_of(number * PAIR, PAIR)
            queries = query_ref[:, pl.ds(at, PAIR)].astype(F32) * HD ** (-0.5)
            grads = grad_mixed[:, pl.ds(at, PAIR)].astype(F32)
            parts = []
            for side in range(2):
                own = jnp.where(masks[side], queries, 0.0).astype(BF)
                grad_own = jnp.where(masks[side], grads, 0.0).astype(BF)
                scores = dot(keys_twice[...], own, 1, 1) + bias[...]
                probs = jnp.exp(scores - stats_ref[2 * number + side])
                grad_probs = dot(values_twice[...], grad_own, 1, 1)
                inner = jnp.sum(probs * grad_probs, axis=0, keepdims=True)
                grad_scores = (probs * (grad_probs - inner)).astype(BF)
                key_sum[...] += dot(grad_scores, own, 1, 0)
                value_sum[...] += dot(probs.astype(BF), grad_own, 1, 0)
                parts.append(dot(keys_t[...], grad_scores, 1, 0))
            back = jnp.concatenate(parts, axis=0).T * HD ** (-0.5)
            grad_query[:, pl.ds(at, PAIR)] = turned(back, cosine, -sine).astype(BF)
            return carry

        lax.fori_loop(0, heads // 2, one_pair, 0)
        for r in range(count):
            rows = slice(r * tokens, (r + 1) * tokens)
            keys_part, values_part = key_sum[rows, :], value_sum[rows, :]
            keys_part = keys_part + pltpu.roll(keys_part, HD, 1)
            values_part = values_part + pltpu.roll(values_part, HD, 1)
            lane = lax.broadcasted_iota(jnp.int32, keys_part.shape, 1)
            outs[r][...] = jnp.where(lane < HD, keys_part, values_part).astype(BF)

    found = call(
        kernel,
        [shape((tokens, columns))] + [shape((tokens, PAIR)) for _ in blocks],
        [mid_low, query, stats] + list(tables) + list(blocks) + list(qo),
        queue,
        scratch=[
            pltpu.VMEM((total_keys, tokens), F32),
            pltpu.VMEM((total_keys, PAIR), BF),
            pltpu.VMEM((total_keys, PAIR), BF),
            pltpu.VMEM((HD, total_keys), BF),
            pltpu.VMEM((tokens, columns), BF),
            pltpu.VMEM((total_keys, PAIR), F32),
            pltpu.VMEM((total_keys, PAIR), F32),
        ],
    )
    return found[0], found[1:]


def project_back(grad_query, pieces, qo, q_at, kvg, kv_at, tables, width, queue):
    tokens, columns = grad_query.shape
    count, many = len(pieces), len(qo)
    chunks = lax.axis_size("tensor")
    layer = kvg[0]

    def kernel(place, query_ref, *refs):
        piece_refs, refs = refs[:count], refs[count:]
        qo_refs, refs = refs[:many], refs[many:]
        kv_refs, (cos_ref, sin_ref), refs = refs[:many], refs[many : many + 2], refs[many + 2 :]
        grad_pair, outs, total = refs[0], refs[1 : 1 + chunks], refs[-1]
        pair = piece_refs[0][...].astype(F32)
        for piece in piece_refs[1:]:
            pair += piece[...].astype(F32)
        pair = turned(pair, keys_only(cos_ref[...], 1.0), keys_only(-sin_ref[...], 0.0))
        grad_pair[...] = pair.astype(BF)
        for at, low, rows, feature in q_at:
            total[:, feature : feature + rows] = dot(
                query_ref[...], qo_refs[at][low : low + rows, :], 1, 1
            )
        for at, low, rows, feature in kv_at:
            total[:, feature : feature + rows] += dot(
                grad_pair[...], kv_refs[at][low : low + rows, :], 1, 1
            )
        put_chunks(place, outs, total)

    ins = [grad_query] + list(pieces) + list(qo)
    in_specs = [None] * len(ins)
    in_specs += [
        pl.BlockSpec((part.shape[0], PAIR), lambda i, place: (0, layer)) for part in kvg[1]
    ]
    in_specs += [None, None]
    found = call(
        kernel,
        [shape((tokens, PAIR))] + [shape((tokens // chunks, width)) for _ in range(chunks)],
        ins + list(kvg[1]) + list(tables),
        queue,
        in_specs=in_specs,
        scratch=[pltpu.VMEM((tokens, width), F32)],
    )
    return found[0], found[1:]


UNIT_TILE = 256


def unit_mask(tile, units, value):
    if units % UNIT_TILE == 0:
        return value
    column = tile * UNIT_TILE + lax.broadcasted_iota(jnp.int32, value.shape, 1)
    return jnp.where(column < units, value, jnp.zeros_like(value))


def joined(weights, places):
    ordered = sorted(places, key=lambda p: p[3])
    return jnp.concatenate([weights[at][low : low + rows, :] for at, low, rows, _ in ordered], axis=0)


def feed(second_in, ffn, at_of, queue):
    tokens, width = second_in.shape
    units = ffn[0].shape[1]
    many = len(ffn)
    chunks = lax.axis_size("tensor")
    steps = pl.cdiv(units, UNIT_TILE)
    gate_at, up_at, down_at = at_of

    def kernel(place, source, *refs):
        weights, refs = refs[:many], refs[many:]
        gate_ref, up_ref, hidden_ref, outs, total = refs[0], refs[1], refs[2], refs[3:-1], refs[-1]
        tile = pl.program_id(0)

        @pl.when(tile == 0)
        def _():
            total[...] = jnp.zeros_like(total)

        gate = dot(source[...], joined(weights, gate_at), 1, 0)
        up = dot(source[...], joined(weights, up_at), 1, 0)
        hidden = gate * (1.0 / (1.0 + jnp.exp(-gate))) * up
        hidden = unit_mask(tile, units, hidden).astype(BF)
        gate_ref[...] = gate.astype(BF)
        up_ref[...] = up.astype(BF)
        hidden_ref[...] = hidden
        total[...] += dot(hidden, unit_mask(tile, units, joined(weights, down_at)), 1, 1)

        @pl.when(tile == steps - 1)
        def _():
            put_chunks(place, outs, total)

    by_tile = lambda rows: pl.BlockSpec((rows, UNIT_TILE), lambda f, place: (0, f))
    found = call(
        kernel,
        [shape((tokens, units))] * 3 + [shape((tokens // chunks, width)) for _ in range(chunks)],
        [second_in] + list(ffn),
        queue,
        grid=(steps,),
        in_specs=[None] + [by_tile(part.shape[0]) for part in ffn],
        out_specs=[by_tile(tokens)] * 3 + [None] * chunks,
        scratch=[pltpu.VMEM((tokens, width), F32)],
    )
    return found[:3], found[3:]


def feed_back(grad_low, gate, up, ffn, at_of, queue):
    tokens, width = grad_low.shape
    units = gate.shape[1]
    many = len(ffn)
    chunks = lax.axis_size("tensor")
    steps = pl.cdiv(units, UNIT_TILE)
    gate_at, up_at, down_at = at_of

    def kernel(place, source, gate_ref, up_ref, *refs):
        weights, refs = refs[:many], refs[many:]
        grad_gate_ref, grad_up_ref, outs, total = refs[0], refs[1], refs[2:-1], refs[-1]
        tile = pl.program_id(0)

        @pl.when(tile == 0)
        def _():
            total[...] = jnp.zeros_like(total)

        grad_hidden = dot(source[...], joined(weights, down_at), 1, 0)
        gate, up = gate_ref[...].astype(F32), up_ref[...].astype(F32)
        sigma = 1.0 / (1.0 + jnp.exp(-gate))
        grad_gate = grad_hidden * up * sigma * (1.0 + gate * (1.0 - sigma))
        grad_up = grad_hidden * gate * sigma
        grad_gate = unit_mask(tile, units, grad_gate).astype(BF)
        grad_up = unit_mask(tile, units, grad_up).astype(BF)
        grad_gate_ref[...] = grad_gate
        grad_up_ref[...] = grad_up
        both = jnp.concatenate([grad_gate, grad_up], axis=1)
        gate_w = unit_mask(tile, units, joined(weights, gate_at))
        up_w = unit_mask(tile, units, joined(weights, up_at))
        total[...] += dot(both, jnp.concatenate([gate_w, up_w], axis=1), 1, 1)

        @pl.when(tile == steps - 1)
        def _():
            put_chunks(place, outs, total)

    by_tile = lambda rows: pl.BlockSpec((rows, UNIT_TILE), lambda f, place: (0, f))
    found = call(
        kernel,
        [shape((tokens, units))] * 2 + [shape((tokens // chunks, width)) for _ in range(chunks)],
        [grad_low, gate, up] + list(ffn),
        queue,
        grid=(steps,),
        in_specs=[None, by_tile(tokens), by_tile(tokens)] + [by_tile(p.shape[0]) for p in ffn],
        out_specs=[by_tile(tokens)] * 2 + [None] * chunks,
        scratch=[pltpu.VMEM((tokens, width), F32)],
    )
    return found[:2], found[2:]


def add_and_norm(stream, chunks, gain, queue):
    def kernel(place, stream_ref, gain_ref, *refs):
        total, normed = refs[-2:]
        values = stream_ref[...].astype(F32)
        for chunk in refs[:-2]:
            values += chunk[...].astype(F32)
        total[...] = values
        scale = lax.rsqrt(jnp.mean(values * values, axis=1, keepdims=True) + EPSILON)
        normed[...] = (values * scale * gain_ref[...]).astype(BF)

    outs = [shape(stream.shape, F32), shape(stream.shape)]
    return call(kernel, outs, [stream, gain] + list(chunks), queue)


def add_last(stream, chunks, queue):
    def kernel(place, stream_ref, *refs):
        values = stream_ref[...]
        for chunk in refs[:-1]:
            values += chunk[...].astype(F32)
        refs[-1][...] = values.astype(BF)

    return call(kernel, [shape(stream.shape)], [stream] + list(chunks), queue)[0]


def norm_back(incoming, values, gain, chunks, queue):
    def kernel(place, incoming_ref, values_ref, gain_ref, *refs):
        total, low = refs[-2:]
        grad = refs[0][...].astype(F32)
        for chunk in refs[1:-2]:
            grad += chunk[...].astype(F32)
        values = values_ref[...].astype(F32)
        scale = lax.rsqrt(jnp.mean(values * values, axis=1, keepdims=True) + EPSILON)
        unit = values * scale
        weighted = grad * gain_ref[...]
        inner = jnp.mean(weighted * unit, axis=1, keepdims=True)
        result = incoming_ref[...].astype(F32) + scale * (weighted - unit * inner)
        total[...] = result
        low[...] = result.astype(BF)

    outs = [shape(values.shape, F32), shape(values.shape)]
    ins = [incoming, values, gain] + list(chunks)
    return call(kernel, outs, ins, queue)


def weight_grads(groups, layout, block, queue):
    width = groups[0][0][0].shape[1]
    sides = width // block // 2
    tall = max(row for row, _ in layout) + block
    wide = max(col + g[1][0].shape[1] for g, (_, col) in zip(groups, layout))
    lefts, rights, left_of = [], [], []
    for left, right in groups:
        known = [k for k, other in enumerate(lefts) if other[0] is left[0]]
        left_of.append(known[0] if known else len(lefts))
        if not known:
            lefts.append(left)
        rights.append(right)
    many = len(lefts[0])
    def terms(refs):
        left_refs = [refs[k * many : (k + 1) * many] for k in range(len(lefts))]
        refs = refs[len(lefts) * many :]
        right_refs = [refs[k * many : (k + 1) * many] for k in range(len(rights))]
        left_all = [jnp.concatenate([x[...] for x in group], axis=0).T for group in left_refs]
        found = []
        for k, group in enumerate(right_refs):
            right = jnp.concatenate([x[...] for x in group], axis=0)
            found.append(dot(left_all[left_of[k]], right, 1, 0))
        return found

    ins = [x for left in lefts for x in left] + [x for right in rights for x in right]
    read = len(ins)

    def specs(first):
        tokens = lefts[0][0].shape[0]
        cut = pl.BlockSpec((tokens, block), lambda i, place: (0, first + i))
        return [cut] * (len(lefts) * many) + [None] * (len(rights) * many)

    def send_kernel(place, *refs):
        for value, (row, col), group in zip(terms(refs[:read]), layout, groups):
            columns = group[1][0].shape[1]
            refs[-1][row : row + block, col : col + columns] = value.astype(BF)

    row_block = pl.BlockSpec((tall, wide), lambda i, place: (i, 0))
    send = call(
        send_kernel,
        [shape((sides * tall, wide))],
        ins,
        queue,
        grid=(sides,),
        in_specs=specs(sides),
        out_specs=[row_block],
    )[0]
    got = swap(send, "dp", 1)
    half = tall // 2
    yield None
    if sides != 4:
        keep = call(
            send_kernel,
            [shape((sides * tall, wide))],
            ins,
            queue,
            grid=(sides,),
            in_specs=specs(0),
            out_specs=[row_block],
        )[0]
        both = keep.astype(F32) + got.astype(F32)
        bit = sides // 2
        while bit:
            middle = both.shape[0] // 2
            both = both[:middle] + swap(both[middle:].astype(BF), "context", bit).astype(F32)
            bit //= 2
        yield None
        none = jnp.zeros_like(both[:half])
        yield [both[:half], none, both[half:], none]
        return

    def keep_kernel(place, *refs):
        got_ref = refs[read]
        low_keep, low_send, high_keep, high_send = refs[read + 1 :]
        step = pl.program_id(0)
        found = terms(refs[:read])

        def write(target, start):
            for value, (row, col), group in zip(found, layout, groups):
                columns = slice(col, col + group[1][0].shape[1])
                first, last = max(row, start), min(row + block, start + half)
                if first < last:
                    target[first - start : last - start, columns] = (
                        value[first - row : last - row] + got_ref[first:last, columns].astype(F32)
                    ).astype(BF)

        for number, (low, high) in enumerate(
            ((low_keep, high_keep), (low_send, high_keep), (low_keep, high_send), (low_send, high_send))
        ):
            @pl.when(step == number)
            def _(low=low, high=high):
                write(low, 0)
                write(high, half)

    piece = lambda index: pl.BlockSpec((half, wide), index)
    low_keep, low_send, high_keep, high_send = call(
        keep_kernel,
        [shape((tall, wide))] * 4,
        ins + [got],
        queue,
        grid=(sides,),
        in_specs=specs(0) + [row_block],
        out_specs=[
            piece(lambda i, place: (i // 2, 0)),
            piece(lambda i, place: (i // 3, 0)),
            piece(lambda i, place: (jnp.minimum(i, 1), 0)),
            piece(lambda i, place: (i // 3, 0)),
        ],
    )
    low_got = swap(low_send, "context", 1)
    high_got = swap(high_send, "context", 2)
    yield None

    def fold(place, a, b, c, d, low_own, low_next, high_own, high_next):
        for first, second, own, next_ref in ((a, b, low_own, low_next), (c, d, high_own, high_next)):
            both = first[...].astype(F32) + second[...].astype(F32)
            own[...] = both[:half].astype(BF)
            next_ref[...] = both[half:].astype(BF)

    columns = PAIR if wide % PAIR == 0 else wide
    by_columns = lambda rows: pl.BlockSpec((rows, columns), lambda i, place: (0, i))
    low_own, low_next, high_own, high_next = call(
        fold,
        [shape((half, wide))] * 4,
        [low_keep, low_got, high_keep, high_got],
        queue,
        grid=(wide // columns,),
        in_specs=[by_columns(tall)] * 4,
        out_specs=[by_columns(half)] * 4,
    )
    yield [low_own, swap(low_next, "context", 2), high_own, swap(high_next, "context", 1)]


def finish_ffn(parts, gate_w, up_w, queue):
    block, units = gate_w.shape
    half = parts[0].shape[0]

    def kernel(place, a, b, c, d, gate_ref, up_ref, gate_out, up_out, down_out, sums):
        def part(first, last):
            found = []
            for start, x, y in ((0, a, b), (half, c, d)):
                low, high = max(first, start), min(last, start + half)
                if low < high:
                    rows = slice(low - start, high - start)
                    found.append(x[rows, :].astype(F32) + y[rows, :].astype(F32))
            return jnp.concatenate(found, axis=0)

        gate_out[...] = part(0, block)
        up_out[...] = part(block, 2 * block)
        down_out[...] = part(2 * block, 3 * block)
        product = gate_out[...] * gate_ref[...].astype(F32) + up_out[...] * up_ref[...].astype(F32)
        sums[...] = jnp.broadcast_to(jnp.sum(product, axis=1, keepdims=True), sums.shape)

    outs = [shape((block, units), F32)] * 3 + [shape((block, PAIR), F32)]
    return call(kernel, outs, list(parts) + [gate_w, up_w], queue)


def finish_heads(parts, query_w, pair_w, queue):
    block, columns = query_w.shape
    half = parts[0].shape[0]

    def kernel(place, a, b, c, d, query_ref, pair_ref, query_out, output_out, pair_out, sums):
        for start, x, y in ((0, a, b), (half, c, d)):
            both = x[...].astype(F32) + y[...].astype(F32)
            rows = slice(start, start + half)
            query_out[rows, :] = both[:, :columns]
            output_out[rows, :] = both[:, columns : 2 * columns]
            pair_out[rows, :] = both[:, 2 * columns :]
        total = jnp.sum(query_out[...] * query_ref[...].astype(F32), axis=1, keepdims=True)
        total += jnp.sum(pair_out[...] * pair_ref[...].astype(F32), axis=1, keepdims=True)
        sums[...] = jnp.broadcast_to(total, sums.shape)

    outs = [shape((block, columns), F32)] * 2 + [shape((block, PAIR), F32)] * 2
    return call(kernel, outs, list(parts) + [query_w, pair_w], queue)


def per_device(hidden_input, cotangent, *params):
    layers = (params[:9], params[9:])
    tensor_count = lax.axis_size("tensor")
    context_count = lax.axis_size("context")
    sequences, _, rows, width = hidden_input.shape
    tokens = rows * tensor_count
    block = layers[0][1].shape[0]
    query_width = layers[0][1].shape[1]
    heads = query_width // HD
    heads_of = [j * heads // (H // KV) for j in range(tensor_count)]
    context = lax.axis_index("context")
    place = jnp.stack(
        [lax.axis_index("dp") * context_count + context, context, lax.axis_index("tensor")]
    ).astype(jnp.int32)
    streams = range(sequences)

    positions = context * tokens + jnp.arange(tokens, dtype=jnp.int32)
    freq = THETA ** (-2.0 * jnp.arange(HD // 2, dtype=F32) / HD)
    angle = positions.astype(F32)[:, None] * freq[None, :]
    cosine, sine = jnp.cos(angle), jnp.sin(angle)
    tables = (
        jnp.concatenate([cosine] * 4, axis=1),
        jnp.concatenate([-sine, sine] * 2, axis=1),
    )

    queue = Queue(place)

    me = lax.axis_index("tensor")
    gains = jnp.stack([layers[0][0], layers[0][5], layers[1][0], layers[1][5]], axis=1)
    gains = jnp.pad(gains, ((0, 0), (0, PAIR - 4)))
    wide_w = [w for layer in layers for w in (layer[2], layer[3])]
    small = []
    for k in range(tensor_count):
        head = ((me ^ k) * heads) // (H // KV)
        cut = [lax.dynamic_slice_in_dim(w, head * HD, HD, 1) for w in wide_w]
        piece = jnp.concatenate(cut + [gains], axis=1)
        small.append(swap(piece, "tensor", k) if k else piece)

    moved = reorder([hidden_input[i, 0] for i in streams] + [cotangent[i, 0] for i in streams], queue)
    first_low, incoming = moved[:sequences], moved[sequences:]
    normed = [[gather_tokens(low)] for low in first_low]
    grad_all = [gather_tokens(low) for low in incoming]

    stack_qo = lambda layer: gather_near(stacked([layer[1], layer[4]], queue))
    stack_ffn = lambda layer: gather_near(stacked([layer[6], layer[7], layer[8]], queue))
    qo_of, ffn_of = [stack_qo(layers[0]), None], [None, None]
    small = placed(small, queue)
    kvg = gather_near(small)
    qo_of[0] = gather_far(qo_of[0], queue)
    kvg = gather_far(kvg, queue)
    pairs_w = (small[:, :PAIR], small[:, PAIR : 2 * PAIR])
    gain_rows = small[:, 2 * PAIR :]
    kv_at = segments(kvg, 0, block, block)
    q_at = segments(qo_of[0], 0, block, block)
    o_at = segments(qo_of[0], block, 2 * block, block)
    gain_all = gain_vectors(kvg, kv_at, width, queue)
    gain_of = lambda number, part: gain_all[2 * number + part : 2 * number + part + 1]

    saved = [[{}, {}] for _ in streams]
    state = list(first_low)
    chunks = [None for _ in streams]

    def enter(number, i):
        keep = saved[i][number]
        keep["stream"] = state[i]
        gain = gain_of(0, 0) if number == 0 else None
        keep["query"], pair, keep["first_in"] = project(
            normed[i], gain, qo_of[number], q_at, (number, kvg), kv_at, tables, queue
        )
        keep["blocks"] = exchange_blocks([pair] * context_count)

    def mix(number, i):
        keep = saved[i][number]
        keep["mixed"], keep["stats"], out = attend(
            keep["query"], keep["blocks"], qo_of[number], o_at, number == 0, width, queue
        )
        chunks[i] = exchange_tokens(out)

    def between(number, i):
        keep = saved[i][number]
        keep["middle"], low = add_and_norm(state[i], chunks[i], gain_of(number, 1), queue)
        keep["second_in"] = gather_tokens(low)

    def forward_units(number, i):
        keep = saved[i][number]
        (keep["gate"], keep["up"], keep["hidden"]), out = feed(
            keep["second_in"], ffn_of[number], ffn_at, queue
        )
        chunks[i] = exchange_tokens(out)

    first, last = 0, sequences - 1
    for i in streams:
        enter(0, i)
        mix(0, i)
    queue.due = [x for i in streams for x in saved[i][0]["blocks"]] + [grad_all[0]]
    ffn_of[0] = stack_ffn(layers[0])
    between(0, 0)
    ffn_of[0] = gather_far(ffn_of[0], queue)
    ffn_at = [segments(ffn_of[0], k * block, (k + 1) * block, block) for k in range(3)]
    qo_of[1] = stack_qo(layers[1])
    for i in streams[1:]:
        between(0, i)
    for i in streams:
        forward_units(0, i)
        if i == 0:
            qo_of[1] = gather_far(qo_of[1], queue)
            ffn_of[1] = stack_ffn(layers[1])
    for i in streams:
        state[i], low = add_and_norm(saved[i][0]["middle"], chunks[i], gain_of(1, 0), queue)
        normed[i] = [gather_tokens(low)]
    for i in streams:
        enter(1, i)
        mix(1, i)
    queue.due = [x for i in streams for x in saved[i][1]["blocks"]]
    ffn_of[1] = gather_far(ffn_of[1], queue)
    for i in streams:
        if i == last:
            queue.due = list(ffn_of[1])
        between(1, i)
    for i in streams:
        forward_units(1, i)

    last_chunks = list(chunks)
    ffn_work, head_work = [None, None], [None, None]
    summed = [None, None]

    def add_out(i):
        state[i] = add_last(saved[i][1]["middle"], last_chunks[i], queue)

    def back_units(number, i):
        keep = saved[i][number]
        keep["grad_all"] = grad_all[i]
        (keep["grad_gate"], keep["grad_up"]), out = feed_back(
            grad_all[i], keep["gate"], keep["up"], ffn_of[number], ffn_at, queue
        )
        chunks[i] = exchange_tokens(out)

    def back_between(number, i):
        keep = saved[i][number]
        keep["grad_mid"], low = norm_back(
            incoming[i], keep["middle"], gain_of(number, 1), chunks[i], queue
        )
        keep["mid_all"] = gather_tokens(low)

    pieces = [None for _ in streams]

    def back_mix(number, i):
        keep = saved[i][number]
        keep["grad_query"], pieces[i] = attend_back(
            keep["mid_all"], keep["query"], keep["blocks"], keep["stats"], qo_of[number], o_at,
            tables, number == 0, queue,
        )
        pieces[i] = exchange_blocks(pieces[i])

    def back_enter(number, i):
        keep = saved[i][number]
        keep["grad_pair"], out = project_back(
            keep["grad_query"], pieces[i], qo_of[number], q_at, (number, kvg), kv_at, tables,
            width, queue,
        )
        chunks[i] = exchange_tokens(out)

    def leave(number, i):
        keep = saved[i][number]
        incoming[i], low = norm_back(
            keep["grad_mid"], keep["stream"], gain_of(number, 0), chunks[i], queue
        )
        if number == 1:
            grad_all[i] = gather_tokens(low)

    def ffn_grads(number):
        both = lambda name: tuple(saved[i][number][name] for i in streams)
        ffn_work[number] = weight_grads(
            [
                (both("second_in"), both("grad_gate")),
                (both("second_in"), both("grad_up")),
                (both("grad_all"), both("hidden")),
            ],
            [(0, 0), (block, 0), (2 * block, 0)],
            block,
            queue,
        )
        next(ffn_work[number])

    def head_grads(number):
        both = lambda name: tuple(saved[i][number][name] for i in streams)
        head_work[number] = weight_grads(
            [
                (both("first_in"), both("grad_query")),
                (both("mid_all"), both("mixed")),
                (both("first_in"), both("grad_pair")),
            ],
            [(0, 0), (0, query_width), (0, 2 * query_width)],
            block,
            queue,
        )
        next(head_work[number])

    def fold_ffn(number):
        summed[number] = [next(ffn_work[number]), None]

    def fold_heads(number):
        summed[number][1] = next(head_work[number])

    def end_ffn(number):
        layer = layers[number]
        summed[number][0] = finish_ffn(summed[number][0], layer[6], layer[7], queue)

    def end_heads(number):
        summed[number][1] = finish_heads(
            summed[number][1], layers[number][1], pairs_w[number], queue
        )

    for i in streams:
        back_units(1, i)
        if i == 0:
            add_out(0)
    ffn_grads(1)
    for i in streams:
        back_between(1, i)
    for i in streams:
        back_mix(1, i)
    for i in streams[1:]:
        add_out(i)
    next(ffn_work[1])
    for i in streams:
        back_enter(1, i)
    head_grads(1)
    next(head_work[1])
    for i in streams:
        leave(1, i)
    fold_ffn(1)
    fold_heads(1)
    for i in streams:
        back_units(0, i)
    end_ffn(1)
    end_heads(1)
    ffn_grads(0)
    back_between(0, 0)
    next(ffn_work[0])
    for i in streams[1:]:
        back_between(0, i)
    for i in streams:
        back_mix(0, i)
    fold_ffn(0)
    for i in streams:
        back_enter(0, i)
    head_grads(0)
    next(head_work[0])
    end_ffn(0)
    for i in streams:
        leave(0, i)
    fold_heads(0)
    outputs = jnp.stack(reorder(state, queue))
    in_grads = jnp.stack(reorder(incoming, queue))
    end_heads(0)

    sums = []
    for number in range(2):
        own_gains = gain_rows[:, 2 * number : 2 * number + 2].astype(F32)
        sums.append(summed[number][1][3][:, :1] / own_gains[:, :1])
        sums.append(summed[number][0][3][:, :1] / own_gains[:, 1:])
    tail = jnp.pad(jnp.concatenate(sums, axis=1), ((0, 0), (0, PAIR - 4)))
    small_g = lax.all_to_all(
        jnp.concatenate([summed[0][1][2], summed[1][1][2], tail], axis=1),
        "tensor", split_axis=0, concat_axis=0, tiled=True,
    ).reshape(tensor_count, -1, 3 * PAIR)
    gain_g = jnp.sum(small_g[:, :, 2 * PAIR : 2 * PAIR + 4], axis=0)

    results = [
        outputs.reshape(hidden_input.shape),
        in_grads.reshape(hidden_input.shape),
    ]
    for number in range(2):
        ffn_g, head_g = summed[number]
        pair_g = []
        for part in range(2):
            at = (2 * number + part) * HD
            by_head = []
            for head in range(KV):
                pieces = [
                    small_g[j, :, at : at + HD] for j in range(tensor_count) if heads_of[j] == head
                ]
                by_head.append(sum(pieces))
            pair_g.append(jnp.concatenate(by_head, axis=1))
        results += [
            gain_g[:, 2 * number],
            head_g[0],
            pair_g[0],
            pair_g[1],
            head_g[1],
            gain_g[:, 2 * number + 1],
            ffn_g[0],
            ffn_g[1],
            ffn_g[2],
        ]
    return tuple(results)


def solution(mesh):
    rows = P(("dp", "context", "tensor"))
    tall = P(("dp", "context", "tensor"), None)
    wide = P(("dp", "context"), "tensor")
    tokens = P(None, "dp", ("context", "tensor"), None)
    layer = (rows, wide, tall, tall, wide, rows, wide, wide, wide)
    return jax.shard_map(
        per_device,
        mesh=mesh,
        in_specs=(tokens, tokens) + layer + layer,
        out_specs=(tokens, tokens) + layer + layer,
        check_vma=False,
    )
```

time: 1570 us -> 1160 us (0.74)
  Pallas kernels: 0 us -> 477 us
  matrix products: 302 us -> 0 us
  local copies, waits for them, and re-layouts: 292 us -> 36.2 us
  waiting for transfers between devices: 587 us -> 428 us
  other arithmetic: 133 us -> 8.77 us
  starting transfers between devices: 226 us -> 187 us
    pallas_call x0 -> x70, Pallas kernels: none -> 477 us  [call(): pl.pallas_call(ordered, name=name, out_shape=outs, grid_spec=pltpu.Prefet...]
    dot_general x69 -> x0, matrix products: 275 us -> none  [the longest x49 209 us: dot(): lax.dot_general(left, right, (((left_dim,), (right_dim,)), ((), ())), pre...]
    ppermute x184 -> x140, waiting for transfers between devices: 461 us -> 320 us  [swap(): lax.ppermute(value, axis, [(source, source ^ bits) for source in range(co...]
    unnamed x642 -> x356, local copies, waits for them, and re-layouts: 109 us -> 27 us
    rev x24 -> x0, local copies, waits for them, and re-layouts: 69.6 us -> none  [relative(): other = jnp.flip(paired, axis=-2).reshape(values.shape)]
    reshape x40 -> x0, local copies, waits for them, and re-layouts: 47.6 us -> none  [the longest x28 27.5 us: relative(): other = jnp.flip(paired, axis=-2).reshape(values.shape)]
    convert_element_type x40 -> x1, other arithmetic: 37.3 us -> 0.01 us  [per_device(): angle = positions.astype(F32)[:, None] * freq[None, :]]
    sub x4 -> x0, matrix products: 27 us -> none  [attend(): expo = jnp.exp(scores - row_max)]
  transfers between devices with their start and end apart: 202 -> 157, of which waited for: 88 -> 53; matrix products, arithmetic and copies ran while one was open for 40% -> 1% of each run, Pallas kernels for 0% -> 34%
where the time goes in v1:
time: 1160 us; the launch traced here: 1150 us
  Pallas kernels  477 us (41%)
  waiting for transfers between devices  428 us (37%)
  starting transfers between devices  187 us (16%)
  local copies, waits for them, and re-layouts  36.2 us (3%)
  between operations  15.9 us (1%)
    pallas_call x70, Pallas kernels, call(): pl.pallas_call(ordered, name=name, out_shape=outs, grid_spec=pltpu.Prefet...  477 us
    ppermute x140, waiting for transfers between devices, swap(): lax.ppermute(value, axis, [(source, source ^ bits) for source in range(co...  320 us
    ppermute x140, starting transfers between devices, swap(): lax.ppermute(value, axis, [(source, source ^ bits) for source in range(co...  180 us
    all_gather x16, waiting for transfers between devices, gather_tokens(): return lax.all_gather(piece, 'tensor', axis=0, tiled=True)  99.3 us
    unnamed x356, local copies, waits for them, and re-layouts  27 us
  transfers between devices with their start and end apart: 157, of which 53 were waited for; matrix products, arithmetic and copies ran while one was open for 1% of the time, Pallas kernels for 34%

profile of v1, /device:TPU:0, one launch (start us, length us, event | category | flops | bytes accessed | tf_op | source)
XLA Modules:
  0.0 1152.5 jit_solution(4240687121653114939)
XLA Ops:
  30.9 10.3 collective-permute-done.3.refs_1_.refs_13_.refs_12_.refs_16_
  82.1 11.8 %attend.4 = (bf16[256,512]{1,0:T(8,128)(2,1)}, f32[8,1,256]{2,1,0:T(1,128)}, bf16[64,2048]{1,0:T(8,128)(2,1)}, bf16[64,2048]{1,0:T(8,128)(2,1)}, bf16[64,2048]{1,0:T(8,128)(2,1)}, /*index=5*/bf16[64,2048]{1,0:T(8,128)(2,1)}) custom-call(s32[3]{0:T(128)} %pad_add_fusion.place, bf16[256,512]{1,0:T(8,128)(2,1)} %get-tuple-element.243.refs_0_.refs_1_, ...), custom_call_target="tpu_custom_call" | custom-call | flops 12000000000 | bytes 36000000 | tf_op jit(solution)/shard_map/attend/pallas_call | solution.py:119
  107.8 11.7 %attend.5 = (bf16[256,512]{1,0:T(8,128)(2,1)}, f32[8,1,256]{2,1,0:T(1,128)}, bf16[64,2048]{1,0:T(8,128)(2,1)}, bf16[64,2048]{1,0:T(8,128)(2,1)}, bf16[64,2048]{1,0:T(8,128)(2,1)}, /*index=5*/bf16[64,2048]{1,0:T(8,128)(2,1)}) custom-call(s32[3]{0:T(128)} %pad_add_fusion.place, bf16[256,512]{1,0:T(8,128)(2,1)} %get-tuple-element.251.refs_0_.refs_1_, ...), custom_call_target="tpu_custom_call" | custom-call | flops 12000000000 | bytes 36000000 | tf_op jit(solution)/shard_map/attend/pallas_call | solution.py:119
  135.1 12.5 %collective-permute-done.25.refs_4_ = bf16[64,2048]{1,0:T(8,128)(2,1)S(1)} collective-permute-done((bf16[64,2048]{1,0:T(8,128)(2,1)S(1)}, bf16[64,2048]{1,0:T(8,128)(2,1)S(1)}, u32[]{:S(2)}, u32[]{:S(2)}) %collective-permute-start.25) | collective-permute-done | bytes 262176 | tf_op jit(solution)/shard_map/ppermute | solution.py:39
  156.2 14.5 %collective-permute-done.30.refs_1_.refs_2_.refs_4_ = bf16[768,1408]{1,0:T(8,128)(2,1)S(1)} collective-permute-done((bf16[768,1408]{1,0:T(8,128)(2,1)}, bf16[768,1408]{1,0:T(8,128)(2,1)S(1)}, u32[]{:S(2)}, u32[]{:S(2)}) %collective-permute-start.30) | collective-permute-done | bytes 2162720 | tf_op jit(solution)/shard_map/ppermute | solution.py:39
  180.7 19.4 %collective-permute-done.32.refs_4_.refs_6_ = bf16[384,1408]{1,0:T(8,128)(2,1)S(1)} collective-permute-done((bf16[384,1408]{1,0:T(8,128)(2,1)}, bf16[384,1408]{1,0:T(8,128)(2,1)S(1)}, u32[]{:S(2)}, u32[]{:S(2)}) %collective-permute-start.32) | collective-permute-done | bytes 1081376 | tf_op jit(solution)/shard_map/ppermute | solution.py:39
  210.7 12.8 %feed.4 = (bf16[256,1408]{1,0:T(8,128)(2,1)}, bf16[256,1408]{1,0:T(8,128)(2,1)}, bf16[256,1408]{1,0:T(8,128)(2,1)}, bf16[64,2048]{1,0:T(8,128)(2,1)}, bf16[64,20...) custom-call(s32[3]{0:T(128)} %pad_add_fusion.place, ...), custom_call_target="tpu_custom_call" | custom-call | flops 12999999488 | bytes 39000000 | tf_op jit(solution)/shard_map/feed/pallas_call | solution.py:119
  235.4 15.3 %all-gather.25.cloned.1.call-done.refs_0_.refs_1_ = bf16[256,2048]{1,0:T(8,128)(2,1)} async-done(((bf16[64,2048]{1,0:T(8,128)(2,1)}), bf16[256,2048]{1,0:T(8,128)(2,1)}) %all-gather.25.cloned.1.call-update) | async-done | bytes 1048592 | tf_op jit(solution)/shard_map/all_gather | solution.py:81
  250.8 12.8 %feed.5 = (bf16[256,1408]{1,0:T(8,128)(2,1)}, bf16[256,1408]{1,0:T(8,128)(2,1)}, bf16[256,1408]{1,0:T(8,128)(2,1)}, bf16[64,2048]{1,0:T(8,128)(2,1)}, bf16[64,20...) custom-call(s32[3]{0:T(128)} %pad_add_fusion.place, ...), custom_call_target="tpu_custom_call" | custom-call | flops 12999999488 | bytes 39000000 | tf_op jit(solution)/shard_map/feed/pallas_call | solution.py:119
  276.9 21.6 %collective-permute-done.55.refs_4_ = bf16[64,2048]{1,0:T(8,128)(2,1)S(1)} collective-permute-done((bf16[64,2048]{1,0:T(8,128)(2,1)S(1)}, bf16[64,2048]{1,0:T(8,128)(2,1)S(1)}, u32[]{:S(2)}, u32[]{:S(2)}) %collective-permute-start.55) | collective-permute-done | bytes 262176 | tf_op jit(solution)/shard_map/ppermute | solution.py:39
  325.4 11.6 %attend.6 = (bf16[256,512]{1,0:T(8,128)(2,1)}, f32[8,1,256]{2,1,0:T(1,128)}, bf16[64,2048]{1,0:T(8,128)(2,1)}, bf16[64,2048]{1,0:T(8,128)(2,1)}, bf16[64,2048]{1,0:T(8,128)(2,1)}, /*index=5*/bf16[64,2048]{1,0:T(8,128)(2,1)}) custom-call(s32[3]{0:T(128)} %pad_add_fusion.place, bf16[256,512]{1,0:T(8,128)(2,1)} %get-tuple-element.278.refs_0_.refs_1_, ...), custom_call_target="tpu_custom_call" | custom-call | flops 12000000000 | bytes 36000000 | tf_op jit(solution)/shard_map/attend/pallas_call | solution.py:119
  350.4 21.0 %collective-permute-done.65.refs_2_.refs_8_.refs_6_ = bf16[256,128]{1,0:T(8,128)(2,1)S(1)} collective-permute-done((bf16[256,128]{1,0:T(8,128)(2,1)}, bf16[256,128]{1,0:T(8,128)(2,1)S(1)}, u32[]{:S(2)}, u32[]{:S(2)}) %collective-permute-start.65) | collective-permute-done | bytes 65568 | tf_op jit(solution)/shard_map/ppermute | solution.py:39
  379.6 11.8 %attend.7 = (bf16[256,512]{1,0:T(8,128)(2,1)}, f32[8,1,256]{2,1,0:T(1,128)}, bf16[64,2048]{1,0:T(8,128)(2,1)}, bf16[64,2048]{1,0:T(8,128)(2,1)}, bf16[64,2048]{1,0:T(8,128)(2,1)}, /*index=5*/bf16[64,2048]{1,0:T(8,128)(2,1)}) custom-call(s32[3]{0:T(128)} %pad_add_fusion.place, bf16[256,512]{1,0:T(8,128)(2,1)} %get-tuple-element.286.refs_0_.refs_1_, ...), custom_call_target="tpu_custom_call" | custom-call | flops 12000000000 | bytes 36000000 | tf_op jit(solution)/shard_map/attend/pallas_call | solution.py:119
  404.1 17.7 %collective-permute-done.68.refs_10_.refs_4_.refs_6_ = bf16[384,1408]{1,0:T(8,128)(2,1)S(1)} collective-permute-done((bf16[384,1408]{1,0:T(8,128)(2,1)}, bf16[384,1408]{1,0:T(8,128)(2,1)S(1)}, u32[]{:S(2)}, u32[]{:S(2)}) %collective-permute-start.68) | collective-permute-done | bytes 1081376 | tf_op jit(solution)/shard_map/ppermute | solution.py:39
  422.8 16.4 %collective-permute-done.75.refs_3_ = bf16[64,2048]{1,0:T(8,128)(2,1)S(1)} collective-permute-done((bf16[64,2048]{1,0:T(8,128)(2,1)}, bf16[64,2048]{1,0:T(8,128)(2,1)S(1)}, u32[]{:S(2)}, u32[]{:S(2)}) %collective-permute-start.75) | collective-permute-done | bytes 262176 | tf_op jit(solution)/shard_map/ppermute | solution.py:39
  439.8 14.1 %collective-permute-done.76.refs_4_ = bf16[64,2048]{1,0:T(8,128)(2,1)S(1)} collective-permute-done((bf16[64,2048]{1,0:T(8,128)(2,1)}, bf16[64,2048]{1,0:T(8,128)(2,1)S(1)}, u32[]{:S(2)}, u32[]{:S(2)}) %collective-permute-start.76) | collective-permute-done | bytes 262176 | tf_op jit(solution)/shard_map/ppermute | solution.py:39
  470.3 12.9 %feed.6 = (bf16[256,1408]{1,0:T(8,128)(2,1)}, bf16[256,1408]{1,0:T(8,128)(2,1)}, bf16[256,1408]{1,0:T(8,128)(2,1)}, bf16[64,2048]{1,0:T(8,128)(2,1)}, bf16[64,20...) custom-call(s32[3]{0:T(128)} %pad_add_fusion.place, ...), custom_call_target="tpu_custom_call" | custom-call | flops 12999999488 | bytes 39000000 | tf_op jit(solution)/shard_map/feed/pallas_call | solution.py:119
  488.4 20.1 %all-gather.33.cloned.1.call-done.refs_0_.refs_1_ = bf16[256,2048]{1,0:T(8,128)(2,1)} async-done(((bf16[64,2048]{1,0:T(8,128)(2,1)}), bf16[256,2048]{1,0:T(8,128)(2,1)}) %all-gather.33.cloned.1.call-update) | async-done | bytes 1048592 | tf_op jit(solution)/shard_map/all_gather | solution.py:81
  508.5 12.9 %feed.7 = (bf16[256,1408]{1,0:T(8,128)(2,1)}, bf16[256,1408]{1,0:T(8,128)(2,1)}, bf16[256,1408]{1,0:T(8,128)(2,1)}, bf16[64,2048]{1,0:T(8,128)(2,1)}, bf16[64,20...) custom-call(s32[3]{0:T(128)} %pad_add_fusion.place, ...), custom_call_target="tpu_custom_call" | custom-call | flops 12999999488 | bytes 39000000 | tf_op jit(solution)/shard_map/feed/pallas_call | solution.py:119
  521.4 15.2 %feed_back.4 = (bf16[256,1408]{1,0:T(8,128)(2,1)}, bf16[256,1408]{1,0:T(8,128)(2,1)}, bf16[64,2048]{1,0:T(8,128)(2,1)}, bf16[64,2048]{1,0:T(8,128)(2,1)}, bf16[6...) custom-call(s32[3]{0:T(128)} %pad_add_fusion.place, ...), custom_call_target="tpu_custom_call" | custom-call | flops 15000000512 | bytes 45000000 | tf_op jit(solution)/shard_map/feed_back/pallas_call | solution.py:119
  540.4 15.1 %feed_back.5 = (bf16[256,1408]{1,0:T(8,128)(2,1)}, bf16[256,1408]{1,0:T(8,128)(2,1)}, bf16[64,2048]{1,0:T(8,128)(2,1)}, bf16[64,2048]{1,0:T(8,128)(2,1)}, bf16[6...) custom-call(s32[3]{0:T(128)} %pad_add_fusion.place, bf16[256,2048]{1,0:T(8,128)(2,1)} %all-gather.35.cloned.1.call-done.refs_0_.refs_3_, ...), custom_call_target="tpu_custom_call" | custom-call | flops 15000000512 | bytes 45000000 | tf_op jit(solution)/shard_map/feed_back/pallas_call | solution.py:119
  555.6 10.8 weight_grads.4.refs_7_
  571.0 9.5 collective-permute-done.87.refs_4_
  580.4 8.8 collective-permute-done.88.refs_5_
  601.6 10.3 collective-permute-done.84.refs_4_
  612.0 13.1 %collective-permute-done.85.refs_5_ = bf16[64,2048]{1,0:T(8,128)(2,1)S(1)} collective-permute-done((bf16[64,2048]{1,0:T(8,128)(2,1)S(1)}, bf16[64,2048]{1,0:T(8,128)(2,1)S(1)}, u32[]{:S(2)}, u32[]{:S(2)}) %collective-permute-start.85) | collective-permute-done | bytes 262176 | tf_op jit(solution)/shard_map/ppermute | solution.py:39
  631.9 13.2 %collective-permute-start.81 = (bf16[64,2048]{1,0:T(8,128)(2,1)S(1)}, bf16[64,2048]{1,0:T(8,128)(2,1)S(1)}, u32[]{:S(2)}, u32[]{:S(2)}) collective-permute-start(bf16[64,2048]{1,0:T(8,128)(2,1)S(1)} %copy-done.63), channel_id=1, source_target_pairs={{0,1},{1,0},{2,3},{3,2},{4,5},{5,4},{6,7},{7,6},{8,9},{9,8},{10,11... | collective-permute-start | bytes 786440 | tf_op jit(solution)/shard_map/ppermute | solution.py:39
  648.5 13.4 %attend_back.4 = (bf16[256,512]{1,0:T(8,128)(2,1)}, bf16[256,128]{1,0:T(8,128)(2,1)}, bf16[256,128]{1,0:T(8,128)(2,1)}, bf16[256,128]{1,0:T(8,128)(2,1)}, bf16[256,128]{1,0:T(8,128)(2,1)}) custom-call(s32[3]{0:T(128)} %pad_add_fusion.place, bf16[256,2048]{1,0:T(8,128)(2,1)} %all-gather.39.cloned.1.call-done.refs_0_.refs_2_, ...), custom_call_target="tpu_custom_call" | custom-call | flops 12999999488 | bytes 39000000 | tf_op jit(solution)/shard_map/attend_back/pallas_call | solution.py:119
  663.3 17.2 %all-gather.37.cloned.1.call-done.refs_0_.refs_3_ = bf16[256,2048]{1,0:T(8,128)(2,1)} async-done(((bf16[64,2048]{1,0:T(8,128)(2,1)}), bf16[256,2048]{1,0:T(8,128)(2,1)}) %all-gather.37.cloned.1.call-update) | async-done | bytes 1048592 | tf_op jit(solution)/shard_map/all_gather | solution.py:81
  680.5 13.3 %attend_back.5 = (bf16[256,512]{1,0:T(8,128)(2,1)}, bf16[256,128]{1,0:T(8,128)(2,1)}, bf16[256,128]{1,0:T(8,128)(2,1)}, bf16[256,128]{1,0:T(8,128)(2,1)}, bf16[256,128]{1,0:T(8,128)(2,1)}) custom-call(s32[3]{0:T(128)} %pad_add_fusion.place, bf16[256,2048]{1,0:T(8,128)(2,1)} %all-gather.37.cloned.1.call-done.refs_0_.refs_3_, ...), custom_call_target="tpu_custom_call" | custom-call | flops 12999999488 | bytes 39000000 | tf_op jit(solution)/shard_map/attend_back/pallas_call | solution.py:119
  702.1 13.7 %keep_kernel.4 = (bf16[768,1408]{1,0:T(8,128)(2,1)}, bf16[768,1408]{1,0:T(8,128)(2,1)}, bf16[768,1408]{1,0:T(8,128)(2,1)}, bf16[768,1408]{1,0:T(8,128)(2,1)}) custom-call(s32[3]{0:T(128)} %pad_add_fusion.place, bf16[256,2048]{1,0:T(8,128)(2,1)} %all-gather.31.cloned.1.call-done.refs_0_, bf16[256,2048]{1,0:T(8,128)(2,1)} %all-gather.33.cloned.1.call-done.refs_0_.refs_1_, ...), custom_call_target="tpu_custom_call" | custom-call | flops 12999999488 | bytes 39000000 | tf_op jit(solution)/shard_map/keep_kernel/pallas_call | solution.py:119
  770.1 12.4 %collective-permute-done.105.refs_4_ = bf16[64,2048]{1,0:T(8,128)(2,1)S(1)} collective-permute-done((bf16[64,2048]{1,0:T(8,128)(2,1)S(1)}, bf16[64,2048]{1,0:T(8,128)(2,1)S(1)}, u32[]{:S(2)}, u32[]{:S(2)}) %collective-permute-start.105) | collective-permute-done | bytes 262176 | tf_op jit(solution)/shard_map/ppermute | solution.py:39
  782.5 10.9 collective-permute-done.106.refs_5_
  800.8 9.7 fold.4
  821.3 15.3 %feed_back.6 = (bf16[256,1408]{1,0:T(8,128)(2,1)}, bf16[256,1408]{1,0:T(8,128)(2,1)}, bf16[64,2048]{1,0:T(8,128)(2,1)}, bf16[64,2048]{1,0:T(8,128)(2,1)}, bf16[6...) custom-call(s32[3]{0:T(128)} %pad_add_fusion.place, bf16[256,2048]{1,0:T(8,128)(2,1)} %all-gather.41.cloned.1.call-done.refs_0_.refs_2_, ...), custom_call_target="tpu_custom_call" | custom-call | flops 15000000512 | bytes 45000000 | tf_op jit(solution)/shard_map/feed_back/pallas_call | solution.py:119
  836.6 14.8 %all-gather.43.cloned.1.call-done.refs_0_.refs_3_ = bf16[256,2048]{1,0:T(8,128)(2,1)} async-done(((bf16[64,2048]{1,0:T(8,128)(2,1)}), bf16[256,2048]{1,0:T(8,128)(2,1)}) %all-gather.43.cloned.1.call-update) | async-done | bytes 1048592 | tf_op jit(solution)/shard_map/all_gather | solution.py:81
  851.3 15.1 %feed_back.7 = (bf16[256,1408]{1,0:T(8,128)(2,1)}, bf16[256,1408]{1,0:T(8,128)(2,1)}, bf16[64,2048]{1,0:T(8,128)(2,1)}, bf16[64,2048]{1,0:T(8,128)(2,1)}, bf16[6...) custom-call(s32[3]{0:T(128)} %pad_add_fusion.place, bf16[256,2048]{1,0:T(8,128)(2,1)} %all-gather.43.cloned.1.call-done.refs_0_.refs_3_, ...), custom_call_target="tpu_custom_call" | custom-call | flops 15000000512 | bytes 45000000 | tf_op jit(solution)/shard_map/feed_back/pallas_call | solution.py:119
  877.7 10.8 weight_grads.6.refs_7_
  893.0 9.1 collective-permute-done.108.refs_4_
  902.1 9.2 collective-permute-done.109.refs_5_
  923.5 14.3 %keep_kernel.6 = (bf16[768,1408]{1,0:T(8,128)(2,1)}, bf16[768,1408]{1,0:T(8,128)(2,1)}, bf16[768,1408]{1,0:T(8,128)(2,1)}, bf16[768,1408]{1,0:T(8,128)(2,1)}) custom-call(s32[3]{0:T(128)} %pad_add_fusion.place, bf16[256,2048]{1,0:T(8,128)(2,1)} %all-gather.23.cloned.1.call-done.refs_0_, bf16[256,2048]{1,0:T(8,128)(2,1)} %all-gather.25.cloned.1.call-done.refs_0_.refs_1_, ...), custom_call_target="tpu_custom_call" | custom-call | flops 12999999488 | bytes 39000000 | tf_op jit(solution)/shard_map/keep_kernel/pallas_call | solution.py:119
  937.9 12.0 %collective-permute-done.116.refs_5_ = bf16[64,2048]{1,0:T(8,128)(2,1)S(1)} collective-permute-done((bf16[64,2048]{1,0:T(8,128)(2,1)S(1)}, bf16[64,2048]{1,0:T(8,128)(2,1)S(1)}, u32[]{:S(2)}, u32[]{:S(2)}) %collective-permute-start.116) | collective-permute-done | bytes 262176 | tf_op jit(solution)/shard_map/ppermute | solution.py:39
  963.3 13.2 %attend_back.6 = (bf16[256,512]{1,0:T(8,128)(2,1)}, bf16[256,128]{1,0:T(8,128)(2,1)}, bf16[256,128]{1,0:T(8,128)(2,1)}, bf16[256,128]{1,0:T(8,128)(2,1)}, bf16[256,128]{1,0:T(8,128)(2,1)}) custom-call(s32[3]{0:T(128)} %pad_add_fusion.place, bf16[256,2048]{1,0:T(8,128)(2,1)} %all-gather.45.cloned.1.call-done.refs_0_.refs_2_, ...), custom_call_target="tpu_custom_call" | custom-call | flops 12999999488 | bytes 39000000 | tf_op jit(solution)/shard_map/attend_back/pallas_call | solution.py:119
  980.1 13.8 %all-gather.47.cloned.1.call-done.refs_0_.refs_3_ = bf16[256,2048]{1,0:T(8,128)(2,1)} async-done(((bf16[64,2048]{1,0:T(8,128)(2,1)}), bf16[256,2048]{1,0:T(8,128)(2,1)}) %all-gather.47.cloned.1.call-update) | async-done | bytes 1048592 | tf_op jit(solution)/shard_map/all_gather | solution.py:81
  993.9 13.3 %attend_back.7 = (bf16[256,512]{1,0:T(8,128)(2,1)}, bf16[256,128]{1,0:T(8,128)(2,1)}, bf16[256,128]{1,0:T(8,128)(2,1)}, bf16[256,128]{1,0:T(8,128)(2,1)}, bf16[256,128]{1,0:T(8,128)(2,1)}) custom-call(s32[3]{0:T(128)} %pad_add_fusion.place, bf16[256,2048]{1,0:T(8,128)(2,1)} %all-gather.47.cloned.1.call-done.refs_0_.refs_3_, ...), custom_call_target="tpu_custom_call" | custom-call | flops 12999999488 | bytes 39000000 | tf_op jit(solution)/shard_map/attend_back/pallas_call | solution.py:119
  1010.2 9.9 fold.6
  1055.2 11.1 collective-permute-done.136.refs_1_
  1089.3 11.6 %collective-permute-done.131.refs_5_ = bf16[64,2048]{1,0:T(8,128)(2,1)S(1)} collective-permute-done((bf16[64,2048]{1,0:T(8,128)(2,1)S(1)}, bf16[64,2048]{1,0:T(8,128)(2,1)S(1)}, u32[]{:S(2)}, u32[]{:S(2)}) %collective-permute-start.131) | collective-permute-done | bytes 262176 | tf_op jit(solution)/shard_map/ppermute | solution.py:39
  (748 shorter events, 495.1 us)
Async XLA Ops:
  7.2 60.4 %all-gather.17.cloned.1.call-start = ((), (), s32[]{:S(2)}) async-start(), calls=%async_computation.1 | async-start | bytes 1310720 | tf_op jit(solution)/shard_map/all_gather | solution.py:81
  13.2 80.8 %all-gather.19.cloned.1.call-start = ((), (), s32[]{:S(2)}) async-start(), calls=%async_computation.2 | async-start | bytes 1310720 | tf_op jit(solution)/shard_map/all_gather | solution.py:81
  25.7 93.8 %all-gather.21.cloned.1.call-start = ((), (), s32[]{:S(2)}) async-start(), calls=%async_computation.3 | async-start | bytes 1310720 | tf_op jit(solution)/shard_map/all_gather | solution.py:81
  77.7 131.7 %all-gather.23.cloned.1.call-start = ((), (), s32[]{:S(2)}) async-start(), calls=%async_computation.4 | async-start | bytes 1310720 | tf_op jit(solution)/shard_map/all_gather | solution.py:81
  123.8 46.9 %collective-permute-start.30 = (bf16[768,1408]{1,0:T(8,128)(2,1)}, bf16[768,1408]{1,0:T(8,128)(2,1)S(1)}, u32[]{:S(2)}, u32[]{:S(2)}) collective-permute-start(bf16[768,1408]{1,0:T(8,128)(2,1)} %stacked.5.refs_6_.refs_1_.refs_3_), channel_id=1, source_target_pairs={{0,4},{4,0},{8,12},{12,8},{1,5},{5,1},{9,13},{13,9},{2,6},{6,2},{1... | collective-permute-start | bytes 6488072 | tf_op jit(solution)/shard_map/ppermute | solution.py:39
  125.3 48.7 %collective-permute-start.31 = (bf16[768,1408]{1,0:T(8,128)(2,1)}, bf16[768,1408]{1,0:T(8,128)(2,1)}, u32[]{:S(2)}, u32[]{:S(2)}) collective-permute-start(bf16[768,1408]{1,0:T(8,128)(2,1)} %stacked.5.refs_6_.refs_1_.refs_3_), channel_id=1, source_target_pairs={{0,8},{4,12},{8,0},{12,4},{1,9},{5,13},{9,1},{13,5},{2,10},{6,14},... | collective-permute-start | bytes 6488072 | tf_op jit(solution)/shard_map/ppermute | solution.py:39
  135.1 72.5 %collective-permute-start.34 = (bf16[768,1408]{1,0:T(8,128)(2,1)}, bf16[768,1408]{1,0:T(8,128)(2,1)}, u32[]{:S(2)}, u32[]{:S(2)}) collective-permute-start(bf16[768,1408]{1,0:T(8,128)(2,1)} %stacked.5.refs_6_.refs_1_.refs_3_), channel_id=1, source_target_pairs={{0,16},{16,0},{1,17},{17,1},{2,18},{18,2},{3,19},{19,3},{4,20},{20... | collective-permute-start | bytes 6488072 | tf_op jit(solution)/shard_map/ppermute | solution.py:39
  180.7 70.1 %all-gather.25.cloned.1.call-start = ((), (), s32[]{:S(2)}) async-start(), calls=%async_computation.5 | async-start | bytes 1310720 | tf_op jit(solution)/shard_map/all_gather | solution.py:81
  207.3 103.1 %all-gather.27.cloned.1.call-start = ((), (), s32[]{:S(2)}) async-start(), calls=%async_computation.6 | async-start | bytes 1310720 | tf_op jit(solution)/shard_map/all_gather | solution.py:81
  223.6 40.0 %collective-permute-start.42 = (bf16[64,2048]{1,0:T(8,128)(2,1)}, bf16[64,2048]{1,0:T(8,128)(2,1)S(1)}, u32[]{:S(2)}, u32[]{:S(2)}) collective-permute-start(bf16[64,2048]{1,0:T(8,128)(2,1)} %get-tuple-element.265), channel_id=1, source_target_pairs={{0,1},{1,0},{2,3},{3,2},{4,5},{5,4},{6,7},{7,6},{8,9},{9,8},{10,11... | collective-permute-start | bytes 786440 | tf_op jit(solution)/shard_map/ppermute | solution.py:39
  224.7 38.9 %collective-permute-start.43 = (bf16[64,2048]{1,0:T(8,128)(2,1)}, bf16[64,2048]{1,0:T(8,128)(2,1)S(1)}, u32[]{:S(2)}, u32[]{:S(2)}) collective-permute-start(bf16[64,2048]{1,0:T(8,128)(2,1)} %get-tuple-element.266), channel_id=1, source_target_pairs={{0,2},{1,3},{2,0},{3,1},{4,6},{5,7},{6,4},{7,5},{8,10},{9,11},{10,... | collective-permute-start | bytes 786440 | tf_op jit(solution)/shard_map/ppermute | solution.py:39
  267.8 73.9 %all-gather.29.cloned.1.call-start = ((), (), s32[]{:S(2)}) async-start(), calls=%async_computation.7 | async-start | bytes 1310720 | tf_op jit(solution)/shard_map/all_gather | solution.py:81
  302.9 167.4 %all-gather.31.cloned.1.call-start = ((), (), s32[]{:S(2)}) async-start(), calls=%async_computation.8 | async-start | bytes 1310720 | tf_op jit(solution)/shard_map/all_gather | solution.py:81
  319.1 72.3 %collective-permute-start.63 = (bf16[768,1408]{1,0:T(8,128)(2,1)S(1)}, bf16[768,1408]{1,0:T(8,128)(2,1)}, u32[]{:S(2)}, u32[]{:S(2)}) collective-permute-start(bf16[768,1408]{1,0:T(8,128)(2,1)S(1)} %copy-done), channel_id=1, source_target_pairs={{0,8},{4,12},{8,0},{12,4},{1,9},{5,13},{9,1},{13,5},{2,10},{6,14},... | collective-permute-start | bytes 6488072 | tf_op jit(solution)/shard_map/ppermute | solution.py:39
  320.7 71.6 %collective-permute-start.64 = (bf16[768,1408]{1,0:T(8,128)(2,1)S(1)}, bf16[768,1408]{1,0:T(8,128)(2,1)}, u32[]{:S(2)}, u32[]{:S(2)}) collective-permute-start(bf16[768,1408]{1,0:T(8,128)(2,1)S(1)} %copy-done), channel_id=1, source_target_pairs={{0,4},{4,0},{8,12},{12,8},{1,5},{5,1},{9,13},{13,9},{2,6},{6,2},{1... | collective-permute-start | bytes 6488072 | tf_op jit(solution)/shard_map/ppermute | solution.py:39
  371.4 51.3 %collective-permute-start.70 = (bf16[768,1408]{1,0:T(8,128)(2,1)S(1)}, bf16[768,1408]{1,0:T(8,128)(2,1)}, u32[]{:S(2)}, u32[]{:S(2)}) collective-permute-start(bf16[768,1408]{1,0:T(8,128)(2,1)S(1)} %copy-done), channel_id=1, source_target_pairs={{0,16},{16,0},{1,17},{17,1},{2,18},{18,2},{3,19},{19,3},{4,20},{20... | collective-permute-start | bytes 6488072 | tf_op jit(solution)/shard_map/ppermute | solution.py:39
  398.0 68.0 %collective-permute-start.71 = (bf16[768,1408]{1,0:T(8,128)(2,1)}, bf16[768,1408]{1,0:T(8,128)(2,1)}, u32[]{:S(2)}, u32[]{:S(2)}) collective-permute-start(bf16[768,1408]{1,0:T(8,128)(2,1)} %collective-permute-done.64.refs_1_.refs_8_.refs_2_.refs_4_), channel_id=1, source_target_pairs={{0,16},{16,0},{1,17},{17,1},{2,18},{18,2},{3,19},{19,3},{4,20},{20... | collective-permute-start | bytes 6488072 | tf_op jit(solution)/shard_map/ppermute | solution.py:39
  400.8 65.3 %collective-permute-start.72 = (bf16[768,1408]{1,0:T(8,128)(2,1)}, bf16[768,1408]{1,0:T(8,128)(2,1)}, u32[]{:S(2)}, u32[]{:S(2)}) collective-permute-start(bf16[768,1408]{1,0:T(8,128)(2,1)} %collective-permute-done.63.refs_0_.refs_9_.refs_3_.refs_5_), channel_id=1, source_target_pairs={{0,16},{16,0},{1,17},{17,1},{2,18},{18,2},{3,19},{19,3},{4,20},{20... | collective-permute-start | bytes 6488072 | tf_op jit(solution)/shard_map/ppermute | solution.py:39
  404.1 104.4 %all-gather.33.cloned.1.call-start = ((), (), s32[]{:S(2)}) async-start(), calls=%async_computation.9 | async-start | bytes 1310720 | tf_op jit(solution)/shard_map/all_gather | solution.py:81
  421.9 42.2 %collective-permute-start.73 = (bf16[384,1408]{1,0:T(8,128)(2,1)S(1)}, bf16[384,1408]{1,0:T(8,128)(2,1)S(1)}, u32[]{:S(2)}, u32[]{:S(2)}) collective-permute-start(bf16[384,1408]{1,0:T(8,128)(2,1)S(1)} %collective-permute-done.68.refs_10_.refs_4_.refs_6_), channel_id=1, source_target_pairs={{0,16},{16,0},{1,17},{17,1},{2,18},{18,2},{3,19},{19,3},{4,20},{20... | collective-permute-start | bytes 3244040 | tf_op jit(solution)/shard_map/ppermute | solution.py:39
  422.7 42.4 %collective-permute-start.74 = (bf16[384,1408]{1,0:T(8,128)(2,1)}, bf16[384,1408]{1,0:T(8,128)(2,1)S(1)}, u32[]{:S(2)}, u32[]{:S(2)}) collective-permute-start(bf16[384,1408]{1,0:T(8,128)(2,1)} %collective-permute-done.69.refs_11_.refs_5_.refs_7_), channel_id=1, source_target_pairs={{0,16},{16,0},{1,17},{17,1},{2,18},{18,2},{3,19},{19,3},{4,20},{20... | collective-permute-start | bytes 3244040 | tf_op jit(solution)/shard_map/ppermute | solution.py:39
  469.2 71.2 %all-gather.35.cloned.1.call-start = ((), (), s32[]{:S(2)}) async-start(), calls=%async_computation.10 | async-start | bytes 1310720 | tf_op jit(solution)/shard_map/all_gather | solution.py:81
  469.8 178.7 %all-gather.39.cloned.1.call-start = ((), (), s32[]{:S(2)}) async-start(), calls=%async_computation.12 | async-start | bytes 1310720 | tf_op jit(solution)/shard_map/all_gather | solution.py:81
  483.2 53.4 %collective-permute-start.78 = (bf16[64,2048]{1,0:T(8,128)(2,1)}, bf16[64,2048]{1,0:T(8,128)(2,1)S(1)}, u32[]{:S(2)}, u32[]{:S(2)}) collective-permute-start(bf16[64,2048]{1,0:T(8,128)(2,1)} %get-tuple-element.299), channel_id=1, source_target_pairs={{0,1},{1,0},{2,3},{3,2},{4,5},{5,4},{6,7},{7,6},{8,9},{9,8},{10,11... | collective-permute-start | bytes 786440 | tf_op jit(solution)/shard_map/ppermute | solution.py:39
  486.0 50.7 %collective-permute-start.79 = (bf16[64,2048]{1,0:T(8,128)(2,1)}, bf16[64,2048]{1,0:T(8,128)(2,1)S(1)}, u32[]{:S(2)}, u32[]{:S(2)}) collective-permute-start(bf16[64,2048]{1,0:T(8,128)(2,1)} %get-tuple-element.300), channel_id=1, source_target_pairs={{0,2},{1,3},{2,0},{3,1},{4,6},{5,7},{6,4},{7,5},{8,10},{9,11},{10,... | collective-permute-start | bytes 786440 | tf_op jit(solution)/shard_map/ppermute | solution.py:39
  486.7 50.0 %collective-permute-start.80 = (bf16[64,2048]{1,0:T(8,128)(2,1)}, bf16[64,2048]{1,0:T(8,128)(2,1)S(1)}, u32[]{:S(2)}, u32[]{:S(2)}) collective-permute-start(bf16[64,2048]{1,0:T(8,128)(2,1)} %get-tuple-element.301), channel_id=1, source_target_pairs={{0,3},{1,2},{2,1},{3,0},{4,7},{5,6},{6,5},{7,4},{8,11},{9,10},{10,... | collective-permute-start | bytes 786440 | tf_op jit(solution)/shard_map/ppermute | solution.py:39
  566.4 134.2 %collective-permute-start.93 = (bf16[3072,1408]{1,0:T(8,128)(2,1)}, bf16[3072,1408]{1,0:T(8,128)(2,1)}, u32[]{:S(2)}, u32[]{:S(2)}) collective-permute-start(bf16[3072,1408]{1,0:T(8,128)(2,1)} %weight_grads.4.refs_7_), channel_id=1, source_target_pairs={{0,16},{16,0},{1,17},{17,1},{2,18},{18,2},{3,19},{19,3},{4,20},{20... | collective-permute-start | bytes 25952264 | tf_op jit(solution)/shard_map/ppermute | solution.py:39
  594.1 86.5 %all-gather.37.cloned.1.call-start = ((), (), s32[]{:S(2)}) async-start(), calls=%async_computation.11 | async-start | bytes 1310720 | tf_op jit(solution)/shard_map/all_gather | solution.py:81
  631.8 189.5 %all-gather.41.cloned.1.call-start = ((), (), s32[]{:S(2)}) async-start(), calls=%async_computation.13 | async-start | bytes 1310720 | tf_op jit(solution)/shard_map/all_gather | solution.py:81
  631.9 61.9 %collective-permute-start.81 = (bf16[64,2048]{1,0:T(8,128)(2,1)S(1)}, bf16[64,2048]{1,0:T(8,128)(2,1)S(1)}, u32[]{:S(2)}, u32[]{:S(2)}) collective-permute-start(bf16[64,2048]{1,0:T(8,128)(2,1)S(1)} %copy-done.63), channel_id=1, source_target_pairs={{0,1},{1,0},{2,3},{3,2},{4,5},{5,4},{6,7},{7,6},{8,9},{9,8},{10,11... | collective-permute-start | bytes 786440 | tf_op jit(solution)/shard_map/ppermute | solution.py:39
  645.0 50.3 %collective-permute-start.82 = (bf16[64,2048]{1,0:T(8,128)(2,1)S(1)}, bf16[64,2048]{1,0:T(8,128)(2,1)S(1)}, u32[]{:S(2)}, u32[]{:S(2)}) collective-permute-start(bf16[64,2048]{1,0:T(8,128)(2,1)S(1)} %copy-done.62), channel_id=1, source_target_pairs={{0,2},{1,3},{2,0},{3,1},{4,6},{5,7},{6,4},{7,5},{8,10},{9,11},{10,... | collective-permute-start | bytes 786440 | tf_op jit(solution)/shard_map/ppermute | solution.py:39
  647.0 49.8 %collective-permute-start.83 = (bf16[64,2048]{1,0:T(8,128)(2,1)S(1)}, bf16[64,2048]{1,0:T(8,128)(2,1)S(1)}, u32[]{:S(2)}, u32[]{:S(2)}) collective-permute-start(bf16[64,2048]{1,0:T(8,128)(2,1)S(1)} %copy-done.61), channel_id=1, source_target_pairs={{0,3},{1,2},{2,1},{3,0},{4,7},{5,6},{6,5},{7,4},{8,11},{9,10},{10,... | collective-permute-start | bytes 786440 | tf_op jit(solution)/shard_map/ppermute | solution.py:39
  661.9 53.8 %collective-permute-start.90 = (bf16[256,128]{1,0:T(8,128)(2,1)}, bf16[256,128]{1,0:T(8,128)(2,1)S(1)}, u32[]{:S(2)}, u32[]{:S(2)}) collective-permute-start(bf16[256,128]{1,0:T(8,128)(2,1)} %get-tuple-element.335), channel_id=1, source_target_pairs={{0,4},{4,0},{8,12},{12,8},{1,5},{5,1},{9,13},{13,9},{2,6},{6,2},{1... | collective-permute-start | bytes 196616 | tf_op jit(solution)/shard_map/ppermute | solution.py:39
  739.8 61.0 %collective-permute-start.103 = (bf16[768,1408]{1,0:T(8,128)(2,1)}, bf16[768,1408]{1,0:T(8,128)(2,1)}, u32[]{:S(2)}, u32[]{:S(2)}) collective-permute-start(bf16[768,1408]{1,0:T(8,128)(2,1)} %get-tuple-element.359), channel_id=1, source_target_pairs={{0,4},{4,0},{8,12},{12,8},{1,5},{5,1},{9,13},{13,9},{2,6},{6,2},{1... | collective-permute-start | bytes 6488072 | tf_op jit(solution)/shard_map/ppermute | solution.py:39
  740.5 60.3 %collective-permute-start.104 = (bf16[768,1408]{1,0:T(8,128)(2,1)}, bf16[768,1408]{1,0:T(8,128)(2,1)}, u32[]{:S(2)}, u32[]{:S(2)}) collective-permute-start(bf16[768,1408]{1,0:T(8,128)(2,1)} %get-tuple-element.361), channel_id=1, source_target_pairs={{0,8},{4,12},{8,0},{12,4},{1,9},{5,13},{9,1},{13,5},{2,10},{6,14},... | collective-permute-start | bytes 6488072 | tf_op jit(solution)/shard_map/ppermute | solution.py:39
  761.2 90.1 %all-gather.43.cloned.1.call-start = ((), (), s32[]{:S(2)}) async-start(), calls=%async_computation.14 | async-start | bytes 1310720 | tf_op jit(solution)/shard_map/all_gather | solution.py:81
  810.5 56.0 %collective-permute-start.113 = (bf16[384,1408]{1,0:T(8,128)(2,1)}, bf16[384,1408]{1,0:T(8,128)(2,1)S(1)}, u32[]{:S(2)}, u32[]{:S(2)}) collective-permute-start(bf16[384,1408]{1,0:T(8,128)(2,1)} %get-tuple-element.385), channel_id=1, source_target_pairs={{0,8},{4,12},{8,0},{12,4},{1,9},{5,13},{9,1},{13,5},{2,10},{6,14},... | collective-permute-start | bytes 3244040 | tf_op jit(solution)/shard_map/ppermute | solution.py:39
  811.4 55.1 %collective-permute-start.114 = (bf16[384,1408]{1,0:T(8,128)(2,1)}, bf16[384,1408]{1,0:T(8,128)(2,1)S(1)}, u32[]{:S(2)}, u32[]{:S(2)}) collective-permute-start(bf16[384,1408]{1,0:T(8,128)(2,1)} %get-tuple-element.387), channel_id=1, source_target_pairs={{0,4},{4,0},{8,12},{12,8},{1,5},{5,1},{9,13},{13,9},{2,6},{6,2},{1... | collective-permute-start | bytes 3244040 | tf_op jit(solution)/shard_map/ppermute | solution.py:39
  811.6 151.7 %all-gather.45.cloned.1.call-start = ((), (), s32[]{:S(2)}) async-start(), calls=%async_computation.15 | async-start | bytes 1310720 | tf_op jit(solution)/shard_map/all_gather | solution.py:81
  818.3 55.4 %collective-permute-start.111 = (bf16[128,1152]{1,0:T(8,128)(2,1)}, bf16[128,1152]{1,0:T(8,128)(2,1)S(1)}, u32[]{:S(2)}, u32[]{:S(2)}) collective-permute-start(bf16[128,1152]{1,0:T(8,128)(2,1)} %get-tuple-element.382), channel_id=1, source_target_pairs={{0,8},{4,12},{8,0},{12,4},{1,9},{5,13},{9,1},{13,5},{2,10},{6,14},... | collective-permute-start | bytes 884744 | tf_op jit(solution)/shard_map/ppermute | solution.py:39
  819.3 54.5 %collective-permute-start.112 = (bf16[128,1152]{1,0:T(8,128)(2,1)}, bf16[128,1152]{1,0:T(8,128)(2,1)S(1)}, u32[]{:S(2)}, u32[]{:S(2)}) collective-permute-start(bf16[128,1152]{1,0:T(8,128)(2,1)} %get-tuple-element.384), channel_id=1, source_target_pairs={{0,4},{4,0},{8,12},{12,8},{1,5},{5,1},{9,13},{13,9},{2,6},{6,2},{1... | collective-permute-start | bytes 884744 | tf_op jit(solution)/shard_map/ppermute | solution.py:39
  916.2 77.7 %all-gather.47.cloned.1.call-start = ((), (), s32[]{:S(2)}) async-start(), calls=%async_computation.16 | async-start | bytes 1310720 | tf_op jit(solution)/shard_map/all_gather | solution.py:81
  954.2 52.9 %collective-permute-start.122 = (bf16[768,1408]{1,0:T(8,128)(2,1)}, bf16[768,1408]{1,0:T(8,128)(2,1)}, u32[]{:S(2)}, u32[]{:S(2)}) collective-permute-start(bf16[768,1408]{1,0:T(8,128)(2,1)} %get-tuple-element.407), channel_id=1, source_target_pairs={{0,4},{4,0},{8,12},{12,8},{1,5},{5,1},{9,13},{13,9},{2,6},{6,2},{1... | collective-permute-start | bytes 6488072 | tf_op jit(solution)/shard_map/ppermute | solution.py:39
  955.8 52.9 %collective-permute-start.123 = (bf16[768,1408]{1,0:T(8,128)(2,1)S(1)}, bf16[768,1408]{1,0:T(8,128)(2,1)}, u32[]{:S(2)}, u32[]{:S(2)}) collective-permute-start(bf16[768,1408]{1,0:T(8,128)(2,1)S(1)} %copy-done.28), channel_id=1, source_target_pairs={{0,8},{4,12},{8,0},{12,4},{1,9},{5,13},{9,1},{13,5},{2,10},{6,14},... | collective-permute-start | bytes 6488072 | tf_op jit(solution)/shard_map/ppermute | solution.py:39
  976.6 43.5 %collective-permute-start.119 = (bf16[256,128]{1,0:T(8,128)(2,1)}, bf16[256,128]{1,0:T(8,128)(2,1)S(1)}, u32[]{:S(2)}, u32[]{:S(2)}) collective-permute-start(bf16[256,128]{1,0:T(8,128)(2,1)} %get-tuple-element.404), channel_id=1, source_target_pairs={{0,4},{4,0},{8,12},{12,8},{1,5},{5,1},{9,13},{13,9},{2,6},{6,2},{1... | collective-permute-start | bytes 196616 | tf_op jit(solution)/shard_map/ppermute | solution.py:39
  978.1 42.7 %collective-permute-start.120 = (bf16[256,128]{1,0:T(8,128)(2,1)}, bf16[256,128]{1,0:T(8,128)(2,1)S(1)}, u32[]{:S(2)}, u32[]{:S(2)}) collective-permute-start(bf16[256,128]{1,0:T(8,128)(2,1)} %get-tuple-element.405), channel_id=1, source_target_pairs={{0,8},{4,12},{8,0},{12,4},{1,9},{5,13},{9,1},{13,5},{2,10},{6,14},... | collective-permute-start | bytes 196616 | tf_op jit(solution)/shard_map/ppermute | solution.py:39
  979.5 41.2 %collective-permute-start.121 = (bf16[256,128]{1,0:T(8,128)(2,1)}, bf16[256,128]{1,0:T(8,128)(2,1)S(1)}, u32[]{:S(2)}, u32[]{:S(2)}) collective-permute-start(bf16[256,128]{1,0:T(8,128)(2,1)} %get-tuple-element.406), channel_id=1, source_target_pairs={{0,12},{4,8},{8,4},{12,0},{1,13},{5,9},{9,5},{13,1},{2,14},{6,10},... | collective-permute-start | bytes 196616 | tf_op jit(solution)/shard_map/ppermute | solution.py:39
  1066.4 38.7 %collective-permute-start.128 = (bf16[256,1152]{1,0:T(8,128)(2,1)}, bf16[256,1152]{1,0:T(8,128)(2,1)S(1)}, u32[]{:S(2)}, u32[]{:S(2)}) collective-permute-start(bf16[256,1152]{1,0:T(8,128)(2,1)} %get-tuple-element.418), channel_id=1, source_target_pairs={{0,4},{4,0},{8,12},{12,8},{1,5},{5,1},{9,13},{13,9},{2,6},{6,2},{1... | collective-permute-start | bytes 1769480 | tf_op jit(solution)/shard_map/ppermute | solution.py:39
  (285 other events, 3173.0 us)
Sparse Core Ops, SparseCore 0:
  13.3 30.6 all-gather.16
  45.5 27.4 all-gather.18
  77.9 28.1 all-gather.20
  180.8 28.1 all-gather.22
  211.0 39.7 all-gather.24
  267.9 42.4 all-gather.26
  311.9 29.7 all-gather.28
  404.2 33.2 all-gather.30
  469.4 39.1 all-gather.32
  509.9 28.2 all-gather.34
  594.2 47.1 all-gather.38
  642.8 37.6 all-gather.36
  761.4 48.2 all-gather.40
  811.7 39.5 all-gather.42
  916.3 46.9 all-gather.44
  964.8 29.0 all-gather.46

commit v2 on v1

--- a/solution.py
+++ b/solution.py
@@ -24,9 +24,8 @@
     "project_back": 5.0,
     "feed": 13.0,
     "feed_back": 15.0,
-    "weight_grads": 11.0,
-    "keep_kernel": 13.0,
-    "fold": 6.0,
+    "weights": 6.0,
+    "fold": 3.0,
     "finish_ffn": 6.0,
     "stacked": 4.0,
 }
@@ -45,10 +44,12 @@
     return [stack, swap(stack, "context", 1), swap(stack, "context", 2)]
 
 
-def gather_far(parts, queue):
+def gather_far(parts, queue, due=()):
     count = lax.axis_size("context")
     if count == 4:
-        low, high = halves(parts[2], parts[1], queue)
+        loose = Queue(queue.place)
+        loose.due = list(due)
+        low, high = halves(parts[2], parts[1], loose)
         parts = parts + [swap(low, "context", 1), swap(high, "context", 2)]
     else:
         bit = 1
@@ -82,7 +83,7 @@
 
 
 def exchange_tokens(chunks):
-    return [chunks[0]] + [swap(chunks[k], "tensor", k) for k in range(1, len(chunks))]
+    return [lax.all_to_all(chunks[0], "tensor", split_axis=0, concat_axis=0, tiled=True)]
 
 
 def exchange_blocks(pieces):
@@ -110,7 +111,7 @@
     queue.due = []
     count = len(ins)
     name = kernel.__qualname__.split(".")[0]
-    if "fold" in kernel.__qualname__ or "keep" in kernel.__qualname__:
+    if name == "weight_grads":
         name = kernel.__qualname__.split(".")[-1]
 
     def ordered(place, *refs):
@@ -131,7 +132,7 @@
             vmem_limit_bytes=VMEM_LIMIT, dimension_semantics=("arbitrary",) * len(grid)
         ),
         cost_estimate=pl.CostEstimate(
-            flops=int(COST.get(name, 3.0) * 1 * 1.0e9), bytes_accessed=int(COST.get(name, 3.0) * 1 * 3.0e6), transcendentals=0
+            flops=int(COST.get(name, 3.0) * 0.2 * 1.0e9), bytes_accessed=int(COST.get(name, 3.0) * 1 * 3.0e6), transcendentals=0
         ),
     )(queue.place, *ins, *before))
     queue.last = min(found, key=lambda x: x.size)
@@ -142,7 +143,9 @@
     return jax.ShapeDtypeStruct(dims, dtype)
 
 
-def stacked(pieces, queue):
+def stacked(pieces, place, due=()):
+    queue = Queue(place)
+    queue.due = list(due)
     rows, columns = pieces[0].shape
 
     def kernel(place, *refs):
@@ -237,10 +240,7 @@
 
 
 def put_chunks(place, outs, total):
-    rows = outs[0].shape[0]
-    for k, out in enumerate(outs):
-        at = pl.multiple_of((place[2] ^ k) * rows, rows)
-        out[...] = total[pl.ds(at, rows), :].astype(BF)
+    outs[0][...] = total[...].astype(BF)
 
 
 def project(sources, gain, qo, qo_at, kvg, kv_at, tables, queue):
@@ -321,7 +321,7 @@
     heads = columns // HD
     count, many = len(blocks), len(qo)
     total_keys = count * tokens
-    chunks = lax.axis_size("tensor")
+    chunks = 1
 
     def kernel(place, query_ref, *refs):
         block_refs, refs = refs[:count], refs[count:]
@@ -457,7 +457,7 @@
 def project_back(grad_query, pieces, qo, q_at, kvg, kv_at, tables, width, queue):
     tokens, columns = grad_query.shape
     count, many = len(pieces), len(qo)
-    chunks = lax.axis_size("tensor")
+    chunks = 1
     layer = kvg[0]
 
     def kernel(place, query_ref, *refs):
@@ -516,7 +516,7 @@
     tokens, width = second_in.shape
     units = ffn[0].shape[1]
     many = len(ffn)
-    chunks = lax.axis_size("tensor")
+    chunks = 1
     steps = pl.cdiv(units, UNIT_TILE)
     gate_at, up_at, down_at = at_of
 
@@ -560,7 +560,7 @@
     tokens, width = grad_low.shape
     units = gate.shape[1]
     many = len(ffn)
-    chunks = lax.axis_size("tensor")
+    chunks = 1
     steps = pl.cdiv(units, UNIT_TILE)
     gate_at, up_at, down_at = at_of
 
@@ -605,12 +605,18 @@
     return found[:2], found[2:]
 
 
+def summed_rows(source, rows):
+    total = source[:rows, :].astype(F32)
+    for at in range(rows, source.shape[0], rows):
+        total += source[at : at + rows, :].astype(F32)
+    return total
+
+
 def add_and_norm(stream, chunks, gain, queue):
     def kernel(place, stream_ref, gain_ref, *refs):
         total, normed = refs[-2:]
         values = stream_ref[...].astype(F32)
-        for chunk in refs[:-2]:
-            values += chunk[...].astype(F32)
+        values += summed_rows(refs[0], values.shape[0])
         total[...] = values
         scale = lax.rsqrt(jnp.mean(values * values, axis=1, keepdims=True) + EPSILON)
         normed[...] = (values * scale * gain_ref[...]).astype(BF)
@@ -622,8 +628,7 @@
 def add_last(stream, chunks, queue):
     def kernel(place, stream_ref, *refs):
         values = stream_ref[...]
-        for chunk in refs[:-1]:
-            values += chunk[...].astype(F32)
+        values += summed_rows(refs[0], values.shape[0])
         refs[-1][...] = values.astype(BF)
 
     return call(kernel, [shape(stream.shape)], [stream] + list(chunks), queue)[0]
@@ -632,9 +637,7 @@
 def norm_back(incoming, values, gain, chunks, queue):
     def kernel(place, incoming_ref, values_ref, gain_ref, *refs):
         total, low = refs[-2:]
-        grad = refs[0][...].astype(F32)
-        for chunk in refs[1:-2]:
-            grad += chunk[...].astype(F32)
+        grad = summed_rows(refs[0], incoming_ref.shape[0])
         values = values_ref[...].astype(F32)
         scale = lax.rsqrt(jnp.mean(values * values, axis=1, keepdims=True) + EPSILON)
         unit = values * scale
@@ -649,91 +652,68 @@
     return call(kernel, outs, ins, queue)
 
 
-def weight_grads(groups, layout, block, queue):
+def weight_grads(groups, block, queue):
     width = groups[0][0][0].shape[1]
     sides = width // block // 2
-    tall = max(row for row, _ in layout) + block
-    wide = max(col + g[1][0].shape[1] for g, (_, col) in zip(groups, layout))
-    lefts, rights, left_of = [], [], []
-    for left, right in groups:
+    half = block // 2
+    widths = [rights[0].shape[1] for _, rights in groups]
+    wide = sum(widths)
+    lefts, left_of = [], []
+    for left, _ in groups:
         known = [k for k, other in enumerate(lefts) if other[0] is left[0]]
         left_of.append(known[0] if known else len(lefts))
         if not known:
             lefts.append(left)
-        rights.append(right)
     many = len(lefts[0])
+    ins = [x for left in lefts for x in left] + [x for _, right in groups for x in right]
+    read = len(ins)
+
     def terms(refs):
-        left_refs = [refs[k * many : (k + 1) * many] for k in range(len(lefts))]
-        refs = refs[len(lefts) * many :]
-        right_refs = [refs[k * many : (k + 1) * many] for k in range(len(rights))]
-        left_all = [jnp.concatenate([x[...] for x in group], axis=0).T for group in left_refs]
-        found = []
-        for k, group in enumerate(right_refs):
-            right = jnp.concatenate([x[...] for x in group], axis=0)
-            found.append(dot(left_all[left_of[k]], right, 1, 0))
-        return found
-
-    ins = [x for left in lefts for x in left] + [x for right in rights for x in right]
-    read = len(ins)
-
-    def specs(first):
-        tokens = lefts[0][0].shape[0]
-        cut = pl.BlockSpec((tokens, block), lambda i, place: (0, first + i))
-        return [cut] * (len(lefts) * many) + [None] * (len(rights) * many)
-
-    def send_kernel(place, *refs):
-        for value, (row, col), group in zip(terms(refs[:read]), layout, groups):
-            columns = group[1][0].shape[1]
-            refs[-1][row : row + block, col : col + columns] = value.astype(BF)
-
-    row_block = pl.BlockSpec((tall, wide), lambda i, place: (i, 0))
-    send = call(
-        send_kernel,
-        [shape((sides * tall, wide))],
-        ins,
-        queue,
-        grid=(sides,),
-        in_specs=specs(sides),
-        out_specs=[row_block],
-    )[0]
-    got = swap(send, "dp", 1)
-    half = tall // 2
-    yield None
+        joined_of = lambda k: jnp.concatenate([x[...] for x in refs[k * many : (k + 1) * many]], axis=0)
+        left_all = [joined_of(k).T for k in range(len(lefts))]
+        return [dot(left_all[at], joined_of(len(lefts) + k), 1, 0) for k, at in enumerate(left_of)]
+
+    tokens = lefts[0][0].shape[0]
+    cut = lambda first: pl.BlockSpec((tokens, block), lambda i, place: (0, first + i))
+    in_specs = ([cut(0)] * (many // 2) + [cut(sides)] * (many // 2)) * len(lefts)
+    in_specs += [None] * (len(groups) * many)
+
     if sides != 4:
-        keep = call(
-            send_kernel,
-            [shape((sides * tall, wide))],
+        def kernel(place, *refs):
+            at = 0
+            for value, columns in zip(terms(refs[:read]), widths):
+                refs[-1][:, at : at + columns] = value
+                at += columns
+
+        both = call(
+            kernel,
+            [shape((sides * block, wide), F32)],
             ins,
             queue,
             grid=(sides,),
-            in_specs=specs(0),
-            out_specs=[row_block],
+            in_specs=in_specs,
+            out_specs=[pl.BlockSpec((block, wide), lambda i, place: (i, 0))],
         )[0]
-        both = keep.astype(F32) + got.astype(F32)
+        yield None
         bit = sides // 2
         while bit:
             middle = both.shape[0] // 2
             both = both[:middle] + swap(both[middle:].astype(BF), "context", bit).astype(F32)
             bit //= 2
-        yield None
         none = jnp.zeros_like(both[:half])
         yield [both[:half], none, both[half:], none]
         return
 
-    def keep_kernel(place, *refs):
-        got_ref = refs[read]
-        low_keep, low_send, high_keep, high_send = refs[read + 1 :]
+    def weights(place, *refs):
+        low_keep, low_send, high_keep, high_send = refs[read:]
         step = pl.program_id(0)
         found = terms(refs[:read])
 
         def write(target, start):
-            for value, (row, col), group in zip(found, layout, groups):
-                columns = slice(col, col + group[1][0].shape[1])
-                first, last = max(row, start), min(row + block, start + half)
-                if first < last:
-                    target[first - start : last - start, columns] = (
-                        value[first - row : last - row] + got_ref[first:last, columns].astype(F32)
-                    ).astype(BF)
+            at = 0
+            for value, columns in zip(found, widths):
+                target[:, at : at + columns] = value[start : start + half].astype(BF)
+                at += columns
 
         for number, (low, high) in enumerate(
             ((low_keep, high_keep), (low_send, high_keep), (low_keep, high_send), (low_send, high_send))
@@ -745,12 +725,12 @@
 
     piece = lambda index: pl.BlockSpec((half, wide), index)
     low_keep, low_send, high_keep, high_send = call(
-        keep_kernel,
-        [shape((tall, wide))] * 4,
-        ins + [got],
+        weights,
+        [shape((block, wide))] * 4,
+        ins,
         queue,
         grid=(sides,),
-        in_specs=specs(0) + [row_block],
+        in_specs=in_specs,
         out_specs=[
             piece(lambda i, place: (i // 2, 0)),
             piece(lambda i, place: (i // 3, 0)),
@@ -768,42 +748,31 @@
             own[...] = both[:half].astype(BF)
             next_ref[...] = both[half:].astype(BF)
 
-    columns = PAIR if wide % PAIR == 0 else wide
-    by_columns = lambda rows: pl.BlockSpec((rows, columns), lambda i, place: (0, i))
     low_own, low_next, high_own, high_next = call(
         fold,
         [shape((half, wide))] * 4,
         [low_keep, low_got, high_keep, high_got],
         queue,
-        grid=(wide // columns,),
-        in_specs=[by_columns(tall)] * 4,
-        out_specs=[by_columns(half)] * 4,
     )
     yield [low_own, swap(low_next, "context", 2), high_own, swap(high_next, "context", 1)]
 
 
 def finish_ffn(parts, gate_w, up_w, queue):
     block, units = gate_w.shape
-    half = parts[0].shape[0]
-
-    def kernel(place, a, b, c, d, gate_ref, up_ref, gate_out, up_out, down_out, sums):
-        def part(first, last):
-            found = []
-            for start, x, y in ((0, a, b), (half, c, d)):
-                low, high = max(first, start), min(last, start + half)
-                if low < high:
-                    rows = slice(low - start, high - start)
-                    found.append(x[rows, :].astype(F32) + y[rows, :].astype(F32))
-            return jnp.concatenate(found, axis=0)
-
-        gate_out[...] = part(0, block)
-        up_out[...] = part(block, 2 * block)
-        down_out[...] = part(2 * block, 3 * block)
-        product = gate_out[...] * gate_ref[...].astype(F32) + up_out[...] * up_ref[...].astype(F32)
+    half = block // 2
+
+    def kernel(place, *refs):
+        gate_ref, up_ref = refs[12:14]
+        outs, sums = refs[14:17], refs[17]
+        for k, out in enumerate(outs):
+            a, b, c, d = refs[4 * k : 4 * k + 4]
+            out[:half, :] = a[...].astype(F32) + b[...].astype(F32)
+            out[half:, :] = c[...].astype(F32) + d[...].astype(F32)
+        product = outs[0][...] * gate_ref[...].astype(F32) + outs[1][...] * up_ref[...].astype(F32)
         sums[...] = jnp.broadcast_to(jnp.sum(product, axis=1, keepdims=True), sums.shape)
 
     outs = [shape((block, units), F32)] * 3 + [shape((block, PAIR), F32)]
-    return call(kernel, outs, list(parts) + [gate_w, up_w], queue)
+    return call(kernel, outs, [x for part in parts for x in part] + [gate_w, up_w], queue)
 
 
 def finish_heads(parts, query_w, pair_w, queue):
@@ -868,8 +837,8 @@
     normed = [[gather_tokens(low)] for low in first_low]
     grad_all = [gather_tokens(low) for low in incoming]
 
-    stack_qo = lambda layer: gather_near(stacked([layer[1], layer[4]], queue))
-    stack_ffn = lambda layer: gather_near(stacked([layer[6], layer[7], layer[8]], queue))
+    stack_qo = lambda layer, due=(): gather_near(stacked([layer[1], layer[4]], place, due))
+    stack_ffn = lambda layer, due=(): gather_near(stacked([layer[6], layer[7], layer[8]], place, due))
     qo_of, ffn_of = [stack_qo(layers[0]), None], [None, None]
     small = placed(small, queue)
     kvg = gather_near(small)
@@ -915,41 +884,41 @@
         )
         chunks[i] = exchange_tokens(out)
 
-    first, last = 0, sequences - 1
+    last = sequences - 1
+    blocks_of = lambda number: [x for i in streams for x in saved[i][number]["blocks"]]
     for i in streams:
         enter(0, i)
+    near = stack_ffn(layers[0], blocks_of(0))
+    for i in streams:
         mix(0, i)
-    queue.due = [x for i in streams for x in saved[i][0]["blocks"]] + [grad_all[0]]
-    ffn_of[0] = stack_ffn(layers[0])
-    between(0, 0)
-    ffn_of[0] = gather_far(ffn_of[0], queue)
+    ffn_of[0] = gather_far(near, queue, [saved[last][0]["stats"]])
     ffn_at = [segments(ffn_of[0], k * block, (k + 1) * block, block) for k in range(3)]
-    qo_of[1] = stack_qo(layers[1])
-    for i in streams[1:]:
+    qo_of[1] = gather_far(stack_qo(layers[1], ffn_of[0][1:5]), queue)
+    ffn_of[1] = gather_far(stack_ffn(layers[1], qo_of[1][1:5]), queue)
+    for i in streams:
+        if i == last:
+            queue.due = [grad_all[0]]
         between(0, i)
     for i in streams:
+        if i == last:
+            queue.due = list(qo_of[1])
         forward_units(0, i)
-        if i == 0:
-            qo_of[1] = gather_far(qo_of[1], queue)
-            ffn_of[1] = stack_ffn(layers[1])
     for i in streams:
+        if i == last:
+            queue.due = list(ffn_of[1][1:3])
         state[i], low = add_and_norm(saved[i][0]["middle"], chunks[i], gain_of(1, 0), queue)
         normed[i] = [gather_tokens(low)]
+    queue.due = list(ffn_of[1])
     for i in streams:
         enter(1, i)
+    for i in streams:
         mix(1, i)
-    queue.due = [x for i in streams for x in saved[i][1]["blocks"]]
-    ffn_of[1] = gather_far(ffn_of[1], queue)
     for i in streams:
-        if i == last:
-            queue.due = list(ffn_of[1])
         between(1, i)
     for i in streams:
         forward_units(1, i)
 
     last_chunks = list(chunks)
-    ffn_work, head_work = [None, None], [None, None]
-    summed = [None, None]
 
     def add_out(i):
         state[i] = add_last(saved[i][1]["middle"], last_chunks[i], queue)
@@ -995,92 +964,82 @@
         if number == 1:
             grad_all[i] = gather_tokens(low)
 
-    def ffn_grads(number):
-        both = lambda name: tuple(saved[i][number][name] for i in streams)
-        ffn_work[number] = weight_grads(
-            [
-                (both("second_in"), both("grad_gate")),
-                (both("second_in"), both("grad_up")),
-                (both("grad_all"), both("hidden")),
-            ],
-            [(0, 0), (block, 0), (2 * block, 0)],
-            block,
-            queue,
+    works, parts = [{}, {}], [{}, {}]
+    crossed = {}
+
+    def pair_of(number, name):
+        own = [saved[i][number][name] for i in streams]
+        if (number, name) not in crossed:
+            crossed[number, name] = [swap(x, "dp", 1) for x in own]
+        return own + crossed[number, name]
+
+    def grads(number, key, *names):
+        cache = {}
+        for name in set(sum(names, ())):
+            cache[name] = pair_of(number, name)
+        works[number][key] = weight_grads(
+            [(cache[left], cache[right]) for left, right in names], block, queue
         )
-        next(ffn_work[number])
-
-    def head_grads(number):
-        both = lambda name: tuple(saved[i][number][name] for i in streams)
-        head_work[number] = weight_grads(
-            [
-                (both("first_in"), both("grad_query")),
-                (both("mid_all"), both("mixed")),
-                (both("first_in"), both("grad_pair")),
-            ],
-            [(0, 0), (0, query_width), (0, 2 * query_width)],
-            block,
-            queue,
-        )
-        next(head_work[number])
-
-    def fold_ffn(number):
-        summed[number] = [next(ffn_work[number]), None]
-
-    def fold_heads(number):
-        summed[number][1] = next(head_work[number])
-
-    def end_ffn(number):
+        next(works[number][key])
+
+    def fold(number, key):
+        parts[number][key] = next(works[number][key])
+
+    def end(number, key):
         layer = layers[number]
-        summed[number][0] = finish_ffn(summed[number][0], layer[6], layer[7], queue)
-
-    def end_heads(number):
-        summed[number][1] = finish_heads(
-            summed[number][1], layers[number][1], pairs_w[number], queue
-        )
-
-    for i in streams:
-        back_units(1, i)
-        if i == 0:
-            add_out(0)
-    ffn_grads(1)
-    for i in streams:
-        back_between(1, i)
-    for i in streams:
-        back_mix(1, i)
-    for i in streams[1:]:
-        add_out(i)
-    next(ffn_work[1])
-    for i in streams:
-        back_enter(1, i)
-    head_grads(1)
-    next(head_work[1])
-    for i in streams:
-        leave(1, i)
-    fold_ffn(1)
-    fold_heads(1)
-    for i in streams:
-        back_units(0, i)
-    end_ffn(1)
-    end_heads(1)
-    ffn_grads(0)
-    back_between(0, 0)
-    next(ffn_work[0])
-    for i in streams[1:]:
-        back_between(0, i)
-    for i in streams:
-        back_mix(0, i)
-    fold_ffn(0)
-    for i in streams:
-        back_enter(0, i)
-    head_grads(0)
-    next(head_work[0])
-    end_ffn(0)
-    for i in streams:
-        leave(0, i)
-    fold_heads(0)
+        if key == "ffn":
+            three = [parts[number][name] for name in ("gate", "up", "down")]
+            summed[number][0] = finish_ffn(three, layer[6], layer[7], queue)
+        else:
+            summed[number][1] = finish_heads(parts[number][key], layer[1], pairs_w[number], queue)
+
+    GATE = ("gate", ("second_in", "grad_gate"))
+    UP = ("up", ("second_in", "grad_up"))
+    DOWN = ("down", ("grad_all", "hidden"))
+    HEADS = ("heads", ("first_in", "grad_query"), ("mid_all", "mixed"), ("first_in", "grad_pair"))
+    summed = [[None, None], [None, None]]
+    for number in (1, 0):
+        for i in streams:
+            back_units(number, i)
+            if number == 1 and i == 0:
+                add_out(0)
+        if number == 0:
+            fold(1, "down")
+            fold(1, "heads")
+        for i in streams:
+            back_between(number, i)
+        if number == 0:
+            end(1, "ffn")
+            end(1, "heads")
+        grads(number, *GATE)
+        grads(number, *UP)
+        for i in streams:
+            back_mix(number, i)
+        fold(number, "gate")
+        if number == 1:
+            fold(1, "up")
+            for i in streams[1:]:
+                add_out(i)
+        back_enter(number, 0)
+        if number == 0:
+            fold(0, "up")
+        for i in streams[1:]:
+            back_enter(number, i)
+        grads(number, *DOWN)
+        leave(number, 0)
+        if number == 0:
+            grads(0, *HEADS)
+            fold(0, "down")
+        for i in streams[1:]:
+            leave(number, i)
+        if number == 1:
+            grads(1, *HEADS)
+        else:
+            end(0, "ffn")
+            fold(0, "heads")
     outputs = jnp.stack(reorder(state, queue))
     in_grads = jnp.stack(reorder(incoming, queue))
-    end_heads(0)
+    end(0, "heads")
 
     sums = []
     for number in range(2):

time: 1160 us -> 1070 us (0.922)
  waiting for transfers between devices: 428 us -> 362 us
  Pallas kernels: 477 us -> 464 us
  starting transfers between devices: 187 us -> 174 us
    ppermute x140 -> x144, waiting for transfers between devices: 320 us -> 160 us  [swap(): lax.ppermute(value, axis, [(source, source ^ bits) for source in range(co...]
    all_to_all x0 -> x16, waiting for transfers between devices: none -> 148 us  [exchange_tokens(): lax.all_to_all(chunks[0], 'tensor', split_axis=0, concat_axis=0, tiled=True)]
    ppermute x140 -> x144, starting transfers between devices: 180 us -> 97.7 us  [swap(): lax.ppermute(value, axis, [(source, source ^ bits) for source in range(co...]
    all_to_all x0 -> x16, starting transfers between devices: none -> 68.8 us  [exchange_tokens(): lax.all_to_all(chunks[0], 'tensor', split_axis=0, concat_axis=0, tiled=True)]
    all_gather x16, waiting for transfers between devices: 99.3 us -> 44.8 us  [gather_tokens(): return lax.all_gather(piece, 'tensor', axis=0, tiled=True)]
    pallas_call x70 -> x74, Pallas kernels: 477 us -> 464 us  [call(): pl.pallas_call(ordered, name=name, out_shape=outs, grid_spec=pltpu.Prefet...]
    unnamed x356 -> x300, local copies, waits for them, and re-layouts: 27 us -> 27.2 us
  transfers between devices with their start and end apart: 157 -> 177, of which waited for: 53 -> 65; matrix products, arithmetic and copies ran while one was open for 1% -> 1% of each run, Pallas kernels for 34% -> 40%
where the time goes in v2:
time: 1070 us; the launch traced here: 1060 us
  Pallas kernels  464 us (43%)
  waiting for transfers between devices  362 us (34%)
  starting transfers between devices  174 us (16%)
  local copies, waits for them, and re-layouts  35.6 us (3%)
  between operations  16 us (1%)
    pallas_call x74, Pallas kernels, call(): pl.pallas_call(ordered, name=name, out_shape=outs, grid_spec=pltpu.Prefet...  464 us
    ppermute x144, waiting for transfers between devices, swap(): lax.ppermute(value, axis, [(source, source ^ bits) for source in range(co...  160 us
    all_to_all x16, waiting for transfers between devices, exchange_tokens(): lax.all_to_all(chunks[0], 'tensor', split_axis=0, concat_axis=0, tiled=True)  148 us
    ppermute x144, starting transfers between devices, swap(): lax.ppermute(value, axis, [(source, source ^ bits) for source in range(co...  97.7 us
    all_to_all x16, starting transfers between devices, exchange_tokens(): lax.all_to_all(chunks[0], 'tensor', split_axis=0, concat_axis=0, tiled=True)  68.8 us
    all_gather x16, waiting for transfers between devices, gather_tokens(): return lax.all_gather(piece, 'tensor', axis=0, tiled=True)  44.8 us
    unnamed x300, local copies, waits for them, and re-layouts  27.2 us
  transfers between devices with their start and end apart: 177, of which 65 were waited for; matrix products, arithmetic and copies ran while one was open for 1% of the time, Pallas kernels for 40%

profile of v2, /device:TPU:0, one launch (start us, length us, event | category | flops | bytes accessed | tf_op | source)
XLA Modules:
  0.0 1059.9 jit_solution(16438334411662805041)
XLA Ops:
  30.8 9.3 collective-permute-done.3.refs_1_.refs_13_.refs_12_.refs_16_
  66.2 5.7 project.4
  73.0 5.9 project.5
  96.7 11.7 %attend.4 = (bf16[256,512]{1,0:T(8,128)(2,1)}, f32[8,1,256]{2,1,0:T(1,128)}, bf16[256,2048]{1,0:T(8,128)(2,1)}) custom-call(s32[3]{0:T(128)} %pad_add_fusion.place, bf16[256,512]{1,0:T(8,128)(2,1)} %get-tuple-element.227.refs_0_.refs_1_, bf16[256,128]{1,0:T(8,128)(2,1)} %get-tuple-element.228.refs_24_.refs_1_.refs_3_.refs_5_, bf16[256,128]{1,0:T(8,128)(2,1)} %copy-done.106, ...), custom_call_target="tpu_custom_call" | custom-call | flops 2400000000 | bytes 36000000 | tf_op jit(solution)/shard_map/attend/pallas_call | solution.py:120
  113.5 11.8 %attend.5 = (bf16[256,512]{1,0:T(8,128)(2,1)}, f32[8,1,256]{2,1,0:T(1,128)}, bf16[256,2048]{1,0:T(8,128)(2,1)}) custom-call(s32[3]{0:T(128)} %pad_add_fusion.place, bf16[256,512]{1,0:T(8,128)(2,1)} %get-tuple-element.232.refs_0_.refs_1_, bf16[256,128]{1,0:T(8,128)(2,1)} %get-tuple-element.230.refs_15_.refs_1_.refs_7_.refs_5_, bf16[256,128]{1,0:T(8,128)(2,1)} %copy-done.103, ...), custom_call_target="tpu_custom_call" | custom-call | flops 2400000000 | bytes 36000000 | tf_op jit(solution)/shard_map/attend/pallas_call | solution.py:120
  125.2 17.0 %collective-permute-done.27.refs_1_.refs_2_.refs_4_ = bf16[768,1408]{1,0:T(8,128)(2,1)S(1)} collective-permute-done((bf16[768,1408]{1,0:T(8,128)(2,1)}, bf16[768,1408]{1,0:T(8,128)(2,1)S(1)}, u32[]{:S(2)}, u32[]{:S(2)}) %collective-permute-start.27) | collective-permute-done | bytes 2162720 | tf_op jit(solution)/shard_map/ppermute | solution.py:38
  159.3 10.9 %collective-permute-done.29.refs_4_.refs_6_ = bf16[384,1408]{1,0:T(8,128)(2,1)S(1)} collective-permute-done((bf16[384,1408]{1,0:T(8,128)(2,1)}, bf16[384,1408]{1,0:T(8,128)(2,1)S(1)}, u32[]{:S(2)}, u32[]{:S(2)}) %collective-permute-start.29) | collective-permute-done | bytes 1081376 | tf_op jit(solution)/shard_map/ppermute | solution.py:38
  176.1 7.9 collective-permute-done.36.refs_1_.refs_13_.refs_3_.refs_2_.refs_6_.refs_10_
  184.8 10.8 %all-to-all-done.1 = bf16[4,64,2048]{2,1,0:T(8,128)(2,1)} async-done(((bf16[4,64,2048]{2,1,0:T(8,128)(2,1)}), bf16[4,64,2048]{2,1,0:T(8,128)(2,1)}, u32[]{:S(2)}, u32[]{:S(2)}) %all-to-all-start.1) | async-done | bytes 1048608 | tf_op jit(solution)/shard_map/all_to_all | solution.py:86
  203.0 12.9 %feed.4 = (bf16[256,1408]{1,0:T(8,128)(2,1)}, bf16[256,1408]{1,0:T(8,128)(2,1)}, bf16[256,1408]{1,0:T(8,128)(2,1)}, bf16[256,2048]{1,0:T(8,128)(2,1)}) custom-call(s32[3]{0:T(128)} %pad_add_fusion.place, bf16[256,2048]{1,0:T(8,128)(2,1)} %all-gather.21.cloned.1.call-done.refs_0_, bf16[768,1408]{1,0:T(8,128)(2,1)} %stacked.5.refs_1_.refs_3_, ...), custom_call_target="tpu_custom_call" | custom-call | flops 2600000000 | bytes 39000000 | tf_op jit(solution)/shard_map/feed/pallas_call | solution.py:120
  236.3 12.7 %feed.5 = (bf16[256,1408]{1,0:T(8,128)(2,1)}, bf16[256,1408]{1,0:T(8,128)(2,1)}, bf16[256,1408]{1,0:T(8,128)(2,1)}, bf16[256,2048]{1,0:T(8,128)(2,1)}) custom-call(s32[3]{0:T(128)} %pad_add_fusion.place, bf16[256,2048]{1,0:T(8,128)(2,1)} %all-gather.25.cloned.1.call-done.refs_0_.refs_1_, bf16[768,1408]{1,0:T(8,128)(2,1)} %stacked.5.refs_1_.refs_3_, ...), custom_call_target="tpu_custom_call" | custom-call | flops 2600000000 | bytes 39000000 | tf_op jit(solution)/shard_map/feed/pallas_call | solution.py:120
  256.9 12.1 %collective-permute-done.45.refs_4_.refs_1_.refs_25_.refs_2_ = bf16[768,1408]{1,0:T(8,128)(2,1)S(1)} collective-permute-done((bf16[768,1408]{1,0:T(8,128)(2,1)}, bf16[768,1408]{1,0:T(8,128)(2,1)S(1)}, u32[]{:S(2)}, u32[]{:S(2)}) %collective-permute-start.45) | collective-permute-done | bytes 2162720 | tf_op jit(solution)/shard_map/ppermute | solution.py:38
  276.7 16.4 %all-to-all-done.3 = bf16[4,64,2048]{2,1,0:T(8,128)(2,1)} async-done(((bf16[4,64,2048]{2,1,0:T(8,128)(2,1)}), bf16[4,64,2048]{2,1,0:T(8,128)(2,1)}, u32[]{:S(2)}, u32[]{:S(2)}) %all-to-all-start.3) | async-done | bytes 1048608 | tf_op jit(solution)/shard_map/all_to_all | solution.py:86
  311.3 14.0 %all-gather.29.cloned.1.call-done.refs_0_.refs_1_ = bf16[256,2048]{1,0:T(8,128)(2,1)} async-done(((bf16[64,2048]{1,0:T(8,128)(2,1)}), bf16[256,2048]{1,0:T(8,128)(2,1)}) %all-gather.29.cloned.1.call-update) | async-done | bytes 1048592 | tf_op jit(solution)/shard_map/all_gather | solution.py:82
  331.1 11.6 %attend.6 = (bf16[256,512]{1,0:T(8,128)(2,1)}, f32[8,1,256]{2,1,0:T(1,128)}, bf16[256,2048]{1,0:T(8,128)(2,1)}) custom-call(s32[3]{0:T(128)} %pad_add_fusion.place, bf16[256,512]{1,0:T(8,128)(2,1)} %get-tuple-element.254.refs_0_.refs_1_, bf16[256,128]{1,0:T(8,128)(2,1)} %get-tuple-element.255.refs_23_.refs_1_.refs_5_, bf16[256,128]{1,0:T(8,128)(2,1)} %copy-done.132, ...), custom_call_target="tpu_custom_call" | custom-call | flops 2400000000 | bytes 36000000 | tf_op jit(solution)/shard_map/attend/pallas_call | solution.py:120
  355.2 11.6 %attend.7 = (bf16[256,512]{1,0:T(8,128)(2,1)}, f32[8,1,256]{2,1,0:T(1,128)}, bf16[256,2048]{1,0:T(8,128)(2,1)}) custom-call(s32[3]{0:T(128)} %pad_add_fusion.place, bf16[256,512]{1,0:T(8,128)(2,1)} %get-tuple-element.259.refs_0_.refs_1_, bf16[256,128]{1,0:T(8,128)(2,1)} %get-tuple-element.257.refs_15_.refs_1_.refs_5_, bf16[256,128]{1,0:T(8,128)(2,1)} %copy-done.135, ...), custom_call_target="tpu_custom_call" | custom-call | flops 2400000000 | bytes 36000000 | tf_op jit(solution)/shard_map/attend/pallas_call | solution.py:120
  366.7 5.4 all-to-all-done.4
  379.0 36.5 %all-to-all-done.5 = bf16[4,64,2048]{2,1,0:T(8,128)(2,1)S(1)} async-done(((bf16[4,64,2048]{2,1,0:T(8,128)(2,1)}), bf16[4,64,2048]{2,1,0:T(8,128)(2,1)S(1)}, u32[]{:S(2)}, u32[]{:S(2)}) %all-to-all-start.5) | async-done | bytes 1048608 | tf_op jit(solution)/shard_map/all_to_all | solution.py:86
  419.5 12.8 %feed.6 = (bf16[256,1408]{1,0:T(8,128)(2,1)}, bf16[256,1408]{1,0:T(8,128)(2,1)}, bf16[256,1408]{1,0:T(8,128)(2,1)}, bf16[256,2048]{1,0:T(8,128)(2,1)}) custom-call(s32[3]{0:T(128)} %pad_add_fusion.place, bf16[256,2048]{1,0:T(8,128)(2,1)} %all-gather.31.cloned.1.call-done.refs_0_, bf16[768,1408]{1,0:T(8,128)(2,1)} %stacked.7.refs_24_.refs_1_.refs_3_, ...), custom_call_target="tpu_custom_call" | custom-call | flops 2600000000 | bytes 39000000 | tf_op jit(solution)/shard_map/feed/pallas_call | solution.py:120
  436.6 21.5 %all-gather.33.cloned.1.call-done.refs_0_.refs_1_ = bf16[256,2048]{1,0:T(8,128)(2,1)} async-done(((bf16[64,2048]{1,0:T(8,128)(2,1)}), bf16[256,2048]{1,0:T(8,128)(2,1)}) %all-gather.33.cloned.1.call-update) | async-done | bytes 1048592 | tf_op jit(solution)/shard_map/all_gather | solution.py:82
  458.1 12.8 %feed.7 = (bf16[256,1408]{1,0:T(8,128)(2,1)}, bf16[256,1408]{1,0:T(8,128)(2,1)}, bf16[256,1408]{1,0:T(8,128)(2,1)}, bf16[256,2048]{1,0:T(8,128)(2,1)}) custom-call(s32[3]{0:T(128)} %pad_add_fusion.place, bf16[256,2048]{1,0:T(8,128)(2,1)} %all-gather.33.cloned.1.call-done.refs_0_.refs_1_, bf16[768,1408]{1,0:T(8,128)(2,1)} %stacked.7.refs_24_.refs_1_.refs_3_, ...), custom_call_target="tpu_custom_call" | custom-call | flops 2600000000 | bytes 39000000 | tf_op jit(solution)/shard_map/feed/pallas_call | solution.py:120
  470.9 15.1 %feed_back.4 = (bf16[256,1408]{1,0:T(8,128)(2,1)}, bf16[256,1408]{1,0:T(8,128)(2,1)}, bf16[256,2048]{1,0:T(8,128)(2,1)}) custom-call(s32[3]{0:T(128)} %pad_add_fusion.place, bf16[256,2048]{1,0:T(8,128)(2,1)} %all-gather.23.cloned.1.call-done.refs_4_.refs_0_, bf16[256,1408]{1,0:T(8,128)(2,1)} %get-tuple-element.267.refs_11_.refs_1_, ...), custom_call_target="tpu_custom_call" | custom-call | flops 3000000000 | bytes 45000000 | tf_op jit(solution)/shard_map/feed_back/pallas_call | solution.py:120
  492.5 15.1 %feed_back.5 = (bf16[256,1408]{1,0:T(8,128)(2,1)}, bf16[256,1408]{1,0:T(8,128)(2,1)}, bf16[256,2048]{1,0:T(8,128)(2,1)}) custom-call(s32[3]{0:T(128)} %pad_add_fusion.place, bf16[256,2048]{1,0:T(8,128)(2,1)} %all-gather.35.cloned.1.call-done.refs_0_.refs_1_, bf16[256,1408]{1,0:T(8,128)(2,1)} %get-tuple-element.270.refs_13_.refs_1_, ...), custom_call_target="tpu_custom_call" | custom-call | flops 3000000000 | bytes 45000000 | tf_op jit(solution)/shard_map/feed_back/pallas_call | solution.py:120
  507.6 7.6 all-to-all-done.9
  523.8 35.1 %all-to-all-done.8 = bf16[4,64,2048]{2,1,0:T(8,128)(2,1)} async-done(((bf16[4,64,2048]{2,1,0:T(8,128)(2,1)}), bf16[4,64,2048]{2,1,0:T(8,128)(2,1)}, u32[]{:S(2)}, u32[]{:S(2)}) %all-to-all-start.8) | async-done | bytes 1048608 | tf_op jit(solution)/shard_map/all_to_all | solution.py:86
  568.4 8.8 weights.8
  580.3 8.7 weights.9
  590.1 13.1 %attend_back.4 = (bf16[256,512]{1,0:T(8,128)(2,1)}, bf16[256,128]{1,0:T(8,128)(2,1)}, bf16[256,128]{1,0:T(8,128)(2,1)}, bf16[256,128]{1,0:T(8,128)(2,1)}, bf16[256,128]{1,0:T(8,128)(2,1)}) custom-call(s32[3]{0:T(128)} %pad_add_fusion.place, bf16[256,2048]{1,0:T(8,128)(2,1)} %all-gather.39.cloned.1.call-done.refs_0_.refs_4_, ...), custom_call_target="tpu_custom_call" | custom-call | flops 2600000000 | bytes 39000000 | tf_op jit(solution)/shard_map/attend_back/pallas_call | solution.py:120
  609.4 13.3 %attend_back.5 = (bf16[256,512]{1,0:T(8,128)(2,1)}, bf16[256,128]{1,0:T(8,128)(2,1)}, bf16[256,128]{1,0:T(8,128)(2,1)}, bf16[256,128]{1,0:T(8,128)(2,1)}, bf16[256,128]{1,0:T(8,128)(2,1)}) custom-call(s32[3]{0:T(128)} %pad_add_fusion.place, bf16[256,2048]{1,0:T(8,128)(2,1)} %all-gather.37.cloned.1.call-done.refs_0_.refs_5_, ...), custom_call_target="tpu_custom_call" | custom-call | flops 2600000000 | bytes 39000000 | tf_op jit(solution)/shard_map/attend_back/pallas_call | solution.py:120
  668.4 8.7 weights.10
  695.4 24.6 %all-to-all-done.11 = bf16[4,64,2048]{2,1,0:T(8,128)(2,1)S(1)} async-done(((bf16[4,64,2048]{2,1,0:T(8,128)(2,1)}), bf16[4,64,2048]{2,1,0:T(8,128)(2,1)S(1)}, u32[]{:S(2)}, u32[]{:S(2)}) %all-to-all-start.11) | async-done | bytes 1048608 | tf_op jit(solution)/shard_map/all_to_all | solution.py:86
  725.1 8.3 weights.11
  733.4 15.1 %feed_back.6 = (bf16[256,1408]{1,0:T(8,128)(2,1)}, bf16[256,1408]{1,0:T(8,128)(2,1)}, bf16[256,2048]{1,0:T(8,128)(2,1)}) custom-call(s32[3]{0:T(128)} %pad_add_fusion.place, bf16[256,2048]{1,0:T(8,128)(2,1)} %all-gather.41.cloned.1.call-done.refs_0_, bf16[256,1408]{1,0:T(8,128)(2,1)} %get-tuple-element.244.refs_11_.refs_1_, ...), custom_call_target="tpu_custom_call" | custom-call | flops 3000000000 | bytes 45000000 | tf_op jit(solution)/shard_map/feed_back/pallas_call | solution.py:120
  757.2 15.1 %feed_back.7 = (bf16[256,1408]{1,0:T(8,128)(2,1)}, bf16[256,1408]{1,0:T(8,128)(2,1)}, bf16[256,2048]{1,0:T(8,128)(2,1)}) custom-call(s32[3]{0:T(128)} %pad_add_fusion.place, bf16[256,2048]{1,0:T(8,128)(2,1)} %all-gather.43.cloned.1.call-done.refs_0_.refs_1_, bf16[256,1408]{1,0:T(8,128)(2,1)} %get-tuple-element.247.refs_3_.refs_1_, ...), custom_call_target="tpu_custom_call" | custom-call | flops 3000000000 | bytes 45000000 | tf_op jit(solution)/shard_map/feed_back/pallas_call | solution.py:120
  795.7 7.4 collective-permute-done.108.refs_5_
  813.3 9.9 all-to-all-done.13
  828.6 5.9 finish_ffn.2
  838.9 8.7 weights.12
  852.1 8.7 weights.13
  860.8 13.3 %attend_back.6 = (bf16[256,512]{1,0:T(8,128)(2,1)}, bf16[256,128]{1,0:T(8,128)(2,1)}, bf16[256,128]{1,0:T(8,128)(2,1)}, bf16[256,128]{1,0:T(8,128)(2,1)}, bf16[256,128]{1,0:T(8,128)(2,1)}) custom-call(s32[3]{0:T(128)} %pad_add_fusion.place, bf16[256,2048]{1,0:T(8,128)(2,1)} %all-gather.45.cloned.1.call-done.refs_0_.refs_4_, ...), custom_call_target="tpu_custom_call" | custom-call | flops 2600000000 | bytes 39000000 | tf_op jit(solution)/shard_map/attend_back/pallas_call | solution.py:120
  877.6 13.3 %attend_back.7 = (bf16[256,512]{1,0:T(8,128)(2,1)}, bf16[256,128]{1,0:T(8,128)(2,1)}, bf16[256,128]{1,0:T(8,128)(2,1)}, bf16[256,128]{1,0:T(8,128)(2,1)}, bf16[256,128]{1,0:T(8,128)(2,1)}) custom-call(s32[3]{0:T(128)} %pad_add_fusion.place, bf16[256,2048]{1,0:T(8,128)(2,1)} %all-gather.47.cloned.1.call-done.refs_0_.refs_5_, ...), custom_call_target="tpu_custom_call" | custom-call | flops 2600000000 | bytes 39000000 | tf_op jit(solution)/shard_map/attend_back/pallas_call | solution.py:120
  895.2 5.4 project_back.6
  908.3 16.8 %collective-permute-done.124.refs_1_ = bf16[256,1408]{1,0:T(8,128)(2,1)} collective-permute-done((bf16[256,1408]{1,0:T(8,128)(2,1)}, bf16[256,1408]{1,0:T(8,128)(2,1)}, u32[]{:S(2)}, u32[]{:S(2)}) %collective-permute-start.124) | collective-permute-done | bytes 720928 | tf_op jit(solution)/shard_map/ppermute | solution.py:38
  949.9 8.7 weights.14
  968.6 8.3 weights.15
  988.4 5.7 collective-permute-done.134.refs_1_
  1002.6 5.9 finish_ffn.3
  1040.7 8.7 all-to-all-done.16
  (736 shorter events, 457.6 us)
Async XLA Ops:
  7.2 57.8 %all-gather.17.cloned.1.call-start = ((), (), s32[]{:S(2)}) async-start(), calls=%async_computation.17 | async-start | bytes 1310720 | tf_op jit(solution)/shard_map/all_gather | solution.py:82
  13.2 59.8 %all-gather.19.cloned.1.call-start = ((), (), s32[]{:S(2)}) async-start(), calls=%async_computation.18 | async-start | bytes 1310720 | tf_op jit(solution)/shard_map/all_gather | solution.py:82
  95.2 46.9 %collective-permute-start.27 = (bf16[768,1408]{1,0:T(8,128)(2,1)}, bf16[768,1408]{1,0:T(8,128)(2,1)S(1)}, u32[]{:S(2)}, u32[]{:S(2)}) collective-permute-start(bf16[768,1408]{1,0:T(8,128)(2,1)} %stacked.5.refs_1_.refs_3_), channel_id=1, source_target_pairs={{0,4},{4,0},{8,12},{12,8},{1,5},{5,1},{9,13},{13,9},{2,6},{6,2},{1... | collective-permute-start | bytes 6488072 | tf_op jit(solution)/shard_map/ppermute | solution.py:38
  95.8 46.6 %collective-permute-start.28 = (bf16[768,1408]{1,0:T(8,128)(2,1)}, bf16[768,1408]{1,0:T(8,128)(2,1)}, u32[]{:S(2)}, u32[]{:S(2)}) collective-permute-start(bf16[768,1408]{1,0:T(8,128)(2,1)} %stacked.5.refs_1_.refs_3_), channel_id=1, source_target_pairs={{0,8},{4,12},{8,0},{12,4},{1,9},{5,13},{9,1},{13,5},{2,10},{6,14},... | collective-permute-start | bytes 6488072 | tf_op jit(solution)/shard_map/ppermute | solution.py:38
  108.5 43.2 %all-to-all-start = ((bf16[4,64,2048]{2,1,0:T(8,128)(2,1)}), bf16[4,64,2048]{2,1,0:T(8,128)(2,1)}, u32[]{:S(2)}, u32[]{:S(2)}) async-start(bf16[4,64,2048]{2,1,0:T(8,128)(2,1)} %bitcast.111), calls=%async_computation | async-start | bytes 2097152 | tf_op jit(solution)/shard_map/all_to_all | solution.py:86
  112.7 72.0 %all-gather.23.cloned.1.call-start = ((), (), s32[]{:S(2)}) async-start(), calls=%async_computation.20 | async-start | bytes 1310720 | tf_op jit(solution)/shard_map/all_gather | solution.py:82
  149.2 52.0 %collective-permute-start.31 = (bf16[768,1408]{1,0:T(8,128)(2,1)}, bf16[768,1408]{1,0:T(8,128)(2,1)S(1)}, u32[]{:S(2)}, u32[]{:S(2)}) collective-permute-start(bf16[768,1408]{1,0:T(8,128)(2,1)} %stacked.5.refs_1_.refs_3_), channel_id=1, source_target_pairs={{0,16},{16,0},{1,17},{17,1},{2,18},{18,2},{3,19},{19,3},{4,20},{20... | collective-permute-start | bytes 6488072 | tf_op jit(solution)/shard_map/ppermute | solution.py:38
  149.2 53.8 %collective-permute-start.32 = (bf16[768,1408]{1,0:T(8,128)(2,1)}, bf16[768,1408]{1,0:T(8,128)(2,1)}, u32[]{:S(2)}, u32[]{:S(2)}) collective-permute-start(bf16[768,1408]{1,0:T(8,128)(2,1)} %copy-done.1), channel_id=1, source_target_pairs={{0,16},{16,0},{1,17},{17,1},{2,18},{18,2},{3,19},{19,3},{4,20},{20... | collective-permute-start | bytes 6488072 | tf_op jit(solution)/shard_map/ppermute | solution.py:38
  149.7 53.3 %collective-permute-start.33 = (bf16[768,1408]{1,0:T(8,128)(2,1)}, bf16[768,1408]{1,0:T(8,128)(2,1)}, u32[]{:S(2)}, u32[]{:S(2)}) collective-permute-start(bf16[768,1408]{1,0:T(8,128)(2,1)} %collective-permute-done.28.refs_0_.refs_3_.refs_5_), channel_id=1, source_target_pairs={{0,16},{16,0},{1,17},{17,1},{2,18},{18,2},{3,19},{19,3},{4,20},{20... | collective-permute-start | bytes 6488072 | tf_op jit(solution)/shard_map/ppermute | solution.py:38
  151.7 43.9 %all-to-all-start.1 = ((bf16[4,64,2048]{2,1,0:T(8,128)(2,1)}), bf16[4,64,2048]{2,1,0:T(8,128)(2,1)}, u32[]{:S(2)}, u32[]{:S(2)}) async-start(bf16[4,64,2048]{2,1,0:T(8,128)(2,1)} %bitcast.106), calls=%async_computation.1 | async-start | bytes 2097152 | tf_op jit(solution)/shard_map/all_to_all | solution.py:86
  156.2 46.7 %all-gather.21.cloned.1.call-start = ((), (), s32[]{:S(2)}) async-start(), calls=%async_computation.19 | async-start | bytes 1310720 | tf_op jit(solution)/shard_map/all_gather | solution.py:82
  159.3 76.2 %all-gather.25.cloned.1.call-start = ((), (), s32[]{:S(2)}) async-start(), calls=%async_computation.21 | async-start | bytes 1310720 | tf_op jit(solution)/shard_map/all_gather | solution.py:82
  225.0 44.0 %collective-permute-start.45 = (bf16[768,1408]{1,0:T(8,128)(2,1)}, bf16[768,1408]{1,0:T(8,128)(2,1)S(1)}, u32[]{:S(2)}, u32[]{:S(2)}) collective-permute-start(bf16[768,1408]{1,0:T(8,128)(2,1)} %stacked.7.refs_24_.refs_1_.refs_3_), channel_id=1, source_target_pairs={{0,4},{4,0},{8,12},{12,8},{1,5},{5,1},{9,13},{13,9},{2,6},{6,2},{1... | collective-permute-start | bytes 6488072 | tf_op jit(solution)/shard_map/ppermute | solution.py:38
  225.6 44.2 %collective-permute-start.46 = (bf16[768,1408]{1,0:T(8,128)(2,1)}, bf16[768,1408]{1,0:T(8,128)(2,1)}, u32[]{:S(2)}, u32[]{:S(2)}) collective-permute-start(bf16[768,1408]{1,0:T(8,128)(2,1)} %stacked.7.refs_24_.refs_1_.refs_3_), channel_id=1, source_target_pairs={{0,8},{4,12},{8,0},{12,4},{1,9},{5,13},{9,1},{13,5},{2,10},{6,14},... | collective-permute-start | bytes 6488072 | tf_op jit(solution)/shard_map/ppermute | solution.py:38
  249.0 44.1 %all-to-all-start.3 = ((bf16[4,64,2048]{2,1,0:T(8,128)(2,1)}), bf16[4,64,2048]{2,1,0:T(8,128)(2,1)}, u32[]{:S(2)}, u32[]{:S(2)}) async-start(bf16[4,64,2048]{2,1,0:T(8,128)(2,1)} %bitcast.109), calls=%async_computation.3 | async-start | bytes 2097152 | tf_op jit(solution)/shard_map/all_to_all | solution.py:86
  253.3 43.5 %all-gather.27.cloned.1.call-start = ((), (), s32[]{:S(2)}) async-start(), calls=%async_computation.22 | async-start | bytes 1310720 | tf_op jit(solution)/shard_map/all_gather | solution.py:82
  256.5 68.9 %all-gather.29.cloned.1.call-start = ((), (), s32[]{:S(2)}) async-start(), calls=%async_computation.23 | async-start | bytes 1310720 | tf_op jit(solution)/shard_map/all_gather | solution.py:82
  256.8 40.0 %collective-permute-start.49 = (bf16[768,1408]{1,0:T(8,128)(2,1)}, bf16[768,1408]{1,0:T(8,128)(2,1)}, u32[]{:S(2)}, u32[]{:S(2)}) collective-permute-start(bf16[768,1408]{1,0:T(8,128)(2,1)} %stacked.7.refs_24_.refs_1_.refs_3_), channel_id=1, source_target_pairs={{0,16},{16,0},{1,17},{17,1},{2,18},{18,2},{3,19},{19,3},{4,20},{20... | collective-permute-start | bytes 6488072 | tf_op jit(solution)/shard_map/ppermute | solution.py:38
  372.2 43.2 %all-to-all-start.5 = ((bf16[4,64,2048]{2,1,0:T(8,128)(2,1)}), bf16[4,64,2048]{2,1,0:T(8,128)(2,1)S(1)}, u32[]{:S(2)}, u32[]{:S(2)}) async-start(bf16[4,64,2048]{2,1,0:T(8,128)(2,1)} %bitcast.116), calls=%async_computation.5 | async-start | bytes 2097152 | tf_op jit(solution)/shard_map/all_to_all | solution.py:86
  375.7 43.8 %all-gather.31.cloned.1.call-start = ((), (), s32[]{:S(2)}) async-start(), calls=%async_computation.24 | async-start | bytes 1310720 | tf_op jit(solution)/shard_map/all_gather | solution.py:82
  378.9 79.2 %all-gather.33.cloned.1.call-start = ((), (), s32[]{:S(2)}) async-start(), calls=%async_computation.25 | async-start | bytes 1310720 | tf_op jit(solution)/shard_map/all_gather | solution.py:82
  432.4 53.6 %all-to-all-start.6 = ((bf16[4,64,2048]{2,1,0:T(8,128)(2,1)}), bf16[4,64,2048]{2,1,0:T(8,128)(2,1)S(1)}, u32[]{:S(2)}, u32[]{:S(2)}) async-start(bf16[4,64,2048]{2,1,0:T(8,128)(2,1)} %bitcast.115), calls=%async_computation.6 | async-start | bytes 2097152 | tf_op jit(solution)/shard_map/all_to_all | solution.py:86
  436.0 56.5 %all-gather.35.cloned.1.call-start = ((), (), s32[]{:S(2)}) async-start(), calls=%async_computation.26 | async-start | bytes 1310720 | tf_op jit(solution)/shard_map/all_gather | solution.py:82
  515.1 43.7 %all-to-all-start.8 = ((bf16[4,64,2048]{2,1,0:T(8,128)(2,1)}), bf16[4,64,2048]{2,1,0:T(8,128)(2,1)}, u32[]{:S(2)}, u32[]{:S(2)}) async-start(bf16[4,64,2048]{2,1,0:T(8,128)(2,1)} %bitcast.110), calls=%async_computation.8 | async-start | bytes 2097152 | tf_op jit(solution)/shard_map/all_to_all | solution.py:86
  519.4 70.7 %all-gather.39.cloned.1.call-start = ((), (), s32[]{:S(2)}) async-start(), calls=%async_computation.28 | async-start | bytes 1310720 | tf_op jit(solution)/shard_map/all_gather | solution.py:82
  523.1 86.4 %all-gather.37.cloned.1.call-start = ((), (), s32[]{:S(2)}) async-start(), calls=%async_computation.27 | async-start | bytes 1310720 | tf_op jit(solution)/shard_map/all_gather | solution.py:82
  523.1 39.8 %collective-permute-start.64 = (bf16[256,1408]{1,0:T(8,128)(2,1)}, bf16[256,1408]{1,0:T(8,128)(2,1)}, u32[]{:S(2)}, u32[]{:S(2)}) collective-permute-start(bf16[256,1408]{1,0:T(8,128)(2,1)} %get-tuple-element.271.refs_2_.refs_4_), channel_id=1, source_target_pairs={{0,16},{16,0},{1,17},{17,1},{2,18},{18,2},{3,19},{19,3},{4,20},{20... | collective-permute-start | bytes 2162696 | tf_op jit(solution)/shard_map/ppermute | solution.py:38
  523.2 44.2 %collective-permute-start.61 = (bf16[256,2048]{1,0:T(8,128)(2,1)S(1)}, bf16[256,2048]{1,0:T(8,128)(2,1)S(1)}, u32[]{:S(2)}, u32[]{:S(2)}) collective-permute-start(bf16[256,2048]{1,0:T(8,128)(2,1)S(1)} %copy-done.21), channel_id=1, source_target_pairs={{0,16},{16,0},{1,17},{17,1},{2,18},{18,2},{3,19},{19,3},{4,20},{20... | collective-permute-start | bytes 3145736 | tf_op jit(solution)/shard_map/ppermute | solution.py:38
  523.7 43.8 %collective-permute-start.60 = (bf16[256,2048]{1,0:T(8,128)(2,1)S(1)}, bf16[256,2048]{1,0:T(8,128)(2,1)}, u32[]{:S(2)}, u32[]{:S(2)}) collective-permute-start(bf16[256,2048]{1,0:T(8,128)(2,1)S(1)} %copy-done.23), channel_id=1, source_target_pairs={{0,16},{16,0},{1,17},{17,1},{2,18},{18,2},{3,19},{19,3},{4,20},{20... | collective-permute-start | bytes 3145736 | tf_op jit(solution)/shard_map/ppermute | solution.py:38
  563.0 71.2 %all-to-all-start.7 = ((bf16[4,64,2048]{2,1,0:T(8,128)(2,1)}), bf16[4,64,2048]{2,1,0:T(8,128)(2,1)}, u32[]{:S(2)}, u32[]{:S(2)}) async-start(bf16[4,64,2048]{2,1,0:T(8,128)(2,1)} %bitcast.102), calls=%async_computation.7 | async-start | bytes 2097152 | tf_op jit(solution)/shard_map/all_to_all | solution.py:86
  577.2 45.4 %collective-permute-start.68 = (bf16[256,1408]{1,0:T(8,128)(2,1)}, bf16[256,1408]{1,0:T(8,128)(2,1)S(1)}, u32[]{:S(2)}, u32[]{:S(2)}) collective-permute-start(bf16[256,1408]{1,0:T(8,128)(2,1)} %get-tuple-element.287), channel_id=1, source_target_pairs={{0,4},{4,0},{8,12},{12,8},{1,5},{5,1},{9,13},{13,9},{2,6},{6,2},{1... | collective-permute-start | bytes 2162696 | tf_op jit(solution)/shard_map/ppermute | solution.py:38
  578.9 45.5 %collective-permute-start.69 = (bf16[256,1408]{1,0:T(8,128)(2,1)}, bf16[256,1408]{1,0:T(8,128)(2,1)S(1)}, u32[]{:S(2)}, u32[]{:S(2)}) collective-permute-start(bf16[256,1408]{1,0:T(8,128)(2,1)} %get-tuple-element.289), channel_id=1, source_target_pairs={{0,8},{4,12},{8,0},{12,4},{1,9},{5,13},{9,1},{13,5},{2,10},{6,14},... | collective-permute-start | bytes 2162696 | tf_op jit(solution)/shard_map/ppermute | solution.py:38
  589.0 40.5 %collective-permute-start.66 = (bf16[256,1408]{1,0:T(8,128)(2,1)}, bf16[256,1408]{1,0:T(8,128)(2,1)S(1)}, u32[]{:S(2)}, u32[]{:S(2)}) collective-permute-start(bf16[256,1408]{1,0:T(8,128)(2,1)} %get-tuple-element.284), channel_id=1, source_target_pairs={{0,4},{4,0},{8,12},{12,8},{1,5},{5,1},{9,13},{13,9},{2,6},{6,2},{1... | collective-permute-start | bytes 2162696 | tf_op jit(solution)/shard_map/ppermute | solution.py:38
  589.6 39.9 %collective-permute-start.67 = (bf16[256,1408]{1,0:T(8,128)(2,1)}, bf16[256,1408]{1,0:T(8,128)(2,1)S(1)}, u32[]{:S(2)}, u32[]{:S(2)}) collective-permute-start(bf16[256,1408]{1,0:T(8,128)(2,1)} %get-tuple-element.286), channel_id=1, source_target_pairs={{0,8},{4,12},{8,0},{12,4},{1,9},{5,13},{9,1},{13,5},{2,10},{6,14},... | collective-permute-start | bytes 2162696 | tf_op jit(solution)/shard_map/ppermute | solution.py:38
  677.2 42.8 %all-to-all-start.11 = ((bf16[4,64,2048]{2,1,0:T(8,128)(2,1)}), bf16[4,64,2048]{2,1,0:T(8,128)(2,1)S(1)}, u32[]{:S(2)}, u32[]{:S(2)}) async-start(bf16[4,64,2048]{2,1,0:T(8,128)(2,1)} %bitcast.33), calls=%async_computation.11 | async-start | bytes 2097152 | tf_op jit(solution)/shard_map/all_to_all | solution.py:86
  682.3 51.1 %all-gather.41.cloned.1.call-start = ((), (), s32[]{:S(2)}) async-start(), calls=%async_computation.29 | async-start | bytes 1310720 | tf_op jit(solution)/shard_map/all_gather | solution.py:82
  686.0 71.2 %all-gather.43.cloned.1.call-start = ((), (), s32[]{:S(2)}) async-start(), calls=%async_computation.30 | async-start | bytes 1310720 | tf_op jit(solution)/shard_map/all_gather | solution.py:82
  782.5 40.7 %all-to-all-start.13 = ((bf16[4,64,2048]{2,1,0:T(8,128)(2,1)}), bf16[4,64,2048]{2,1,0:T(8,128)(2,1)}, u32[]{:S(2)}, u32[]{:S(2)}) async-start(bf16[4,64,2048]{2,1,0:T(8,128)(2,1)} %bitcast.37), calls=%async_computation.13 | async-start | bytes 2097152 | tf_op jit(solution)/shard_map/all_to_all | solution.py:86
  787.2 73.6 %all-gather.45.cloned.1.call-start = ((), (), s32[]{:S(2)}) async-start(), calls=%async_computation.31 | async-start | bytes 1310720 | tf_op jit(solution)/shard_map/all_gather | solution.py:82
  790.9 86.7 %all-gather.47.cloned.1.call-start = ((), (), s32[]{:S(2)}) async-start(), calls=%async_computation.32 | async-start | bytes 1310720 | tf_op jit(solution)/shard_map/all_gather | solution.py:82
  795.6 42.1 %collective-permute-start.98 = (bf16[256,2048]{1,0:T(8,128)(2,1)S(1)}, bf16[256,2048]{1,0:T(8,128)(2,1)S(1)}, u32[]{:S(2)}, u32[]{:S(2)}) collective-permute-start(bf16[256,2048]{1,0:T(8,128)(2,1)S(1)} %copy-done.22), channel_id=1, source_target_pairs={{0,16},{16,0},{1,17},{17,1},{2,18},{18,2},{3,19},{19,3},{4,20},{20... | collective-permute-start | bytes 3145736 | tf_op jit(solution)/shard_map/ppermute | solution.py:38
  851.6 55.7 %collective-permute-start.71 = (bf16[256,2048]{1,0:T(8,128)(2,1)}, bf16[256,2048]{1,0:T(8,128)(2,1)}, u32[]{:S(2)}, u32[]{:S(2)}) collective-permute-start(bf16[256,2048]{1,0:T(8,128)(2,1)} %get-tuple-element.297.refs_1_), channel_id=1, source_target_pairs={{0,16},{16,0},{1,17},{17,1},{2,18},{18,2},{3,19},{19,3},{4,20},{20... | collective-permute-start | bytes 3145736 | tf_op jit(solution)/shard_map/ppermute | solution.py:38
  851.6 55.7 %collective-permute-start.70 = (bf16[256,2048]{1,0:T(8,128)(2,1)}, bf16[256,2048]{1,0:T(8,128)(2,1)}, u32[]{:S(2)}, u32[]{:S(2)}) collective-permute-start(bf16[256,2048]{1,0:T(8,128)(2,1)} %get-tuple-element.296.refs_0_), channel_id=1, source_target_pairs={{0,16},{16,0},{1,17},{17,1},{2,18},{18,2},{3,19},{19,3},{4,20},{20... | collective-permute-start | bytes 3145736 | tf_op jit(solution)/shard_map/ppermute | solution.py:38
  900.6 43.2 %all-to-all-start.14 = ((bf16[4,64,2048]{2,1,0:T(8,128)(2,1)}), bf16[4,64,2048]{2,1,0:T(8,128)(2,1)S(1)}, u32[]{:S(2)}, u32[]{:S(2)}) async-start(bf16[4,64,2048]{2,1,0:T(8,128)(2,1)} %bitcast.104), calls=%async_computation.14 | async-start | bytes 2097152 | tf_op jit(solution)/shard_map/all_to_all | solution.py:86
  907.3 42.0 %collective-permute-start.128 = (bf16[256,2048]{1,0:T(8,128)(2,1)S(1)}, bf16[256,2048]{1,0:T(8,128)(2,1)}, u32[]{:S(2)}, u32[]{:S(2)}) collective-permute-start(bf16[256,2048]{1,0:T(8,128)(2,1)S(1)} %copy-done.36), channel_id=1, source_target_pairs={{0,16},{16,0},{1,17},{17,1},{2,18},{18,2},{3,19},{19,3},{4,20},{20... | collective-permute-start | bytes 3145736 | tf_op jit(solution)/shard_map/ppermute | solution.py:38
  907.3 42.3 %collective-permute-start.129 = (bf16[256,2048]{1,0:T(8,128)(2,1)S(1)}, bf16[256,2048]{1,0:T(8,128)(2,1)}, u32[]{:S(2)}, u32[]{:S(2)}) collective-permute-start(bf16[256,2048]{1,0:T(8,128)(2,1)S(1)} %copy-done.37), channel_id=1, source_target_pairs={{0,16},{16,0},{1,17},{17,1},{2,18},{18,2},{3,19},{19,3},{4,20},{20... | collective-permute-start | bytes 3145736 | tf_op jit(solution)/shard_map/ppermute | solution.py:38
  908.2 40.8 %collective-permute-start.130 = (bf16[256,1408]{1,0:T(8,128)(2,1)}, bf16[256,1408]{1,0:T(8,128)(2,1)}, u32[]{:S(2)}, u32[]{:S(2)}) collective-permute-start(bf16[256,1408]{1,0:T(8,128)(2,1)} %get-tuple-element.379.refs_4_), channel_id=1, source_target_pairs={{0,16},{16,0},{1,17},{17,1},{2,18},{18,2},{3,19},{19,3},{4,20},{20... | collective-permute-start | bytes 2162696 | tf_op jit(solution)/shard_map/ppermute | solution.py:38
  943.8 51.1 %all-to-all-start.15 = ((bf16[4,64,2048]{2,1,0:T(8,128)(2,1)}), bf16[4,64,2048]{2,1,0:T(8,128)(2,1)}, u32[]{:S(2)}, u32[]{:S(2)}) async-start(bf16[4,64,2048]{2,1,0:T(8,128)(2,1)} %bitcast.103), calls=%async_computation.15 | async-start | bytes 2097152 | tf_op jit(solution)/shard_map/all_to_all | solution.py:86
  (277 other events, 2689.2 us)
Sparse Core Ops, SparseCore 0:
  13.3 30.6 all-gather.16
  45.5 27.4 all-gather.18
  115.1 38.5 all-gather.22
  159.4 38.3 all-gather.20
  199.8 35.6 all-gather.24
  256.6 39.3 all-gather.26
  298.1 27.1 all-gather.28
  379.0 39.0 all-gather.30
  420.3 37.7 all-gather.32
  459.5 27.8 all-gather.34
  523.2 38.5 all-gather.38
  563.2 46.1 all-gather.36
  686.2 36.6 all-gather.40
  724.6 29.6 all-gather.42
  791.1 33.2 all-gather.44
  827.0 29.1 all-gather.46
